TPU v7x, 32 devices: a whole 2x2x4 slice. The times are simulated.
32 devices in a mesh: dp: 8 (over z, x), tensor: 4 (over y, core).
Axes of the slice: x: 2, y: 2, z: 4, core: 2. Of those that a mesh axis runs over, the one named last changes fastest.
Arguments:
- tokens: bfloat16 [16384, 768], P(('dp', 'tensor')), may hold values from -6 to 6
- cotangent: bfloat16 [16384, 768], P(('dp', 'tensor')), may hold values from -6 to 6
- w_query: float32 [768, 768], P('dp', 'tensor'), may hold values from -0.0546875 to 0.0546875
- w_key: float32 [768, 768], P('dp', 'tensor'), may hold values from -0.21875 to 0.21875
- w_value: float32 [768, 768], P('dp', 'tensor'), may hold values from -0.21875 to 0.21875
- w_proj: float32 [768, 768], P('tensor', 'dp'), may hold values from -1.25 to 1.25
- w_inner: float32 [768, 3072], P('dp', 'tensor'), may hold values from -0.21875 to 0.21875
- w_outer: float32 [3072, 768], P('tensor', 'dp'), may hold values from -0.15625 to 0.15625
- gain_attn: float32 [768], replicated, may hold values from 0.5 to 1.5
- gain_ffn: float32 [768], replicated, may hold values from 0.5 to 1.5
- rel_table: float32 [32, 12], replicated, may hold values from -4 to 4
- lengths: int32 [8, 2], P('dp'), may hold values from 512 to 1536, as said below
- deal: int32 [16384], P(('dp', 'tensor')), may hold values from 0 to 511, as said below
- buckets: int32 [257], replicated, may hold values from 0 to 31
Outputs:
- output: bfloat16 [16384, 768], P(('dp', 'tensor'))
- grad_tokens: bfloat16 [16384, 768], P(('dp', 'tensor'))
- grad_query: float32 [768, 768], P('dp', 'tensor')
- grad_key: float32 [768, 768], P('dp', 'tensor')
- grad_value: float32 [768, 768], P('dp', 'tensor')
- grad_proj: float32 [768, 768], P('tensor', 'dp')
- grad_inner: float32 [768, 3072], P('dp', 'tensor')
- grad_outer: float32 [3072, 768], P('tensor', 'dp')
- grad_gain_attn: float32 [768], replicated
- grad_gain_ffn: float32 [768], replicated
- grad_table: float32 [32, 12], replicated
Inputs may be any that keep to these rules, and one draw needn't show every extreme that they name: `deal`: each device's 512 consecutive entries are an ordering of 0 to 511. The two lengths of a group sum to 2048; some group holds one of 1536.
All inputs are finite; a program needn't handle non-finite values.
Results may differ from a plain program's by a relative error of at most 0.018.
Values may be sent and summed in bfloat16 or wider, within the bound.
No kernel may reach another device: no remote copies, remote signals or barrier semaphores. Data moves between devices by JAX's collectives and lax.ppermute only.
A program may use at most 256 MiB of HBM per device.

v0:
```python
import functools

import jax
import jax.numpy as jnp
from jax import lax
from jax.experimental import pallas as pl
from jax.experimental.pallas import tpu as pltpu
from jax.sharding import PartitionSpec as P

HEAD_DIM = 64
MAXDIST = 128
TILE = 256
KINDS = 5
EPS = 1e-06
NEG = -1000000000.0
BF16 = jnp.bfloat16
F32 = jnp.float32
VMEM = pl.BlockSpec(memory_space=pltpu.VMEM)
SMEM = pl.BlockSpec(memory_space=pltpu.SMEM)


SHORT = pl.CostEstimate(flops=1 << 20, bytes_accessed=1 << 16, transcendentals=0)


LONG = pl.CostEstimate(flops=3 << 33, bytes_accessed=1 << 26, transcendentals=1 << 23)


def mm(left, right):
    return jnp.dot(left, right, preferred_element_type=F32)


def contract(left, left_dim, right, right_dim):
    return lax.dot_general(
        left, right, (((left_dim,), (right_dim,)), ((), ())), preferred_element_type=F32
    )


def after(*values):
    return lax.optimization_barrier(values)


def ring_order(size):
    return [*range(0, size, 2), *range(size - 1, 0, -2)]


def tile_start(tile, rows_dev, me):
    per_slot = rows_dev // TILE
    return pl.multiple_of((((tile // per_slot) ^ me) * per_slot + tile % per_slot) * TILE, TILE)


def build_bias(base_ref, bias_ref, heads):
    for i in range(heads * KINDS):
        row = base_ref[i : i + 1, :]
        if i % KINDS in (0, KINDS - 1):
            bias_ref[i] = jnp.broadcast_to(row[:, :1], (TILE, TILE))
        else:
            full = jnp.broadcast_to(row, (TILE, 2 * TILE))
            bias_ref[i] = pltpu.roll(full, 0, 1, stride=1, stride_axis=0)[:, TILE:]


def pack_kernel(inner_ref, query_ref, key_ref, value_ref, proj_ref, outer_ref, first_ref, rest_ref):
    hidden = inner_ref.shape[1]
    first = [query_ref[...], key_ref[...], value_ref[...], outer_ref[...], proj_ref[...]]
    first_ref[...] = jnp.concatenate(first, axis=1).astype(BF16)
    rest_ref[...] = inner_ref[...].astype(BF16)


def pack_weights(inner, query, key, value, proj, outer):
    rows, hidden = inner.shape
    cols = query.shape[1]
    return pl.pallas_call(
        pack_kernel,
        out_shape=(
            jax.ShapeDtypeStruct((rows, 4 * cols + hidden), BF16),
            jax.ShapeDtypeStruct((rows, hidden), BF16),
        ),
        in_specs=[VMEM] * 6,
        out_specs=(VMEM, VMEM),
        cost_estimate=SHORT,
        name="pack_weights",
    )(inner, query, key, value, proj, outer)


def unring_kernel(ring, spans, found_ref, *out_refs):
    size = found_ref.shape[0] // len(ring)
    for (begin, end, turned), out_ref in zip(spans, out_refs):
        if turned:
            blocks = [
                found_ref[ring.index(d) * size : (ring.index(d) + 1) * size, begin:end]
                for d in range(len(ring))
            ]
            out_ref[...] = jnp.concatenate(blocks, axis=0).T
        else:
            for p, d in enumerate(ring):
                block = found_ref[p * size : (p + 1) * size, begin:end]
                out_ref[d * size : (d + 1) * size, :] = block


def unring(found, ring, spans):
    rows = found.shape[0]
    size = rows // len(ring)
    if size % 16:
        back = [found[ring.index(d) * size :][:size] for d in range(len(ring))]
        whole = jnp.concatenate(back, axis=0)
        parts = [whole[:, begin:end] for begin, end, _ in spans]
        return [part.T if span[2] else part for part, span in zip(parts, spans)]
    shapes = [(end - begin, rows) if turned else (rows, end - begin) for begin, end, turned in spans]
    return pl.pallas_call(
        functools.partial(unring_kernel, ring, spans),
        out_shape=tuple(jax.ShapeDtypeStruct(shape, found.dtype) for shape in shapes),
        in_specs=[VMEM],
        out_specs=(VMEM,) * len(spans),
        cost_estimate=SHORT,
        name="unring",
    )(found)


def store_ringed(out_ref, ring, begin, end, values):
    size = values.shape[0] // len(ring)
    if size % 16:
        out_ref[:, begin:end] = values
    else:
        for p, d in enumerate(ring):
            out_ref[p * size : (p + 1) * size, begin:end] = values[d * size : (d + 1) * size, :]


def ringed(values, ring):
    size = values.shape[0] // len(ring)
    if size % 16 == 0:
        return values
    return jnp.concatenate([values[d * size :][:size] for d in ring], axis=0)


def segment_rows(width, first_len, start, same, other):
    shape = (HEAD_DIM, width)
    low = start + lax.broadcasted_iota(jnp.int32, shape, 1) < first_len
    row = lax.broadcasted_iota(jnp.int32, shape, 0)
    first = jnp.where(low, same, other)
    second = jnp.where(low, other, same)
    return jnp.where(row == 0, first, jnp.where(row == 1, second, 0.0)).astype(BF16)


def segment_all(rows, rows_dev, first_len, me, same, other):
    slots = rows // rows_dev
    return jnp.concatenate(
        [
            segment_rows(rows_dev, first_len, (s ^ me) * rows_dev, same, other)
            for s in range(slots)
        ],
        axis=1,
    )


def tile_range(tile, first_len, tiles):
    start = tile * TILE
    low = jnp.where(start >= first_len, first_len // TILE, 0)
    high = jnp.where(start + TILE <= first_len, (first_len + TILE - 1) // TILE, tiles)
    return low, high


def over_tiles(low, high, body, carry, sizes=(4, 2, 1)):
    at = low
    for size in sizes:
        count = (high - at) // size

        def step(i, c, at=at, size=size):
            return body(tuple(at + size * i + j for j in range(size)), c)

        carry = lax.fori_loop(0, count, step, carry)
        at = at + size * count
    return carry


def attend_rows(
    heads, rows_dev, first_slot, info_ref, qkv_ref, key_ref, out_ref, wide_ref, lse_ref, score_ref, bias_ref
):
    rows = qkv_ref.shape[1]
    cols = heads * HEAD_DIM
    first_len, me = info_ref[0, 0], info_ref[0, 2]
    tiles = rows // TILE
    per_slot = rows_dev // TILE

    def query_tile(i, carry):
        qb = ((first_slot + i // per_slot) ^ me) * per_slot + i % per_slot
        qs = pl.ds(pl.multiple_of(first_slot * rows_dev + i * TILE, TILE), TILE)
        at = pl.ds(pl.multiple_of(i * TILE, TILE), TILE)
        query_seg = segment_rows(TILE, first_len, qb * TILE, 0.0, NEG)
        queries = [
            jnp.concatenate([qkv_ref[h * HEAD_DIM : (h + 1) * HEAD_DIM, qs], query_seg], axis=0)
            for h in range(heads)
        ]
        low, high = tile_range(qb, first_len, tiles)

        def score_tiles(kbs, tops):
            kss = [pl.ds(tile_start(kb, rows_dev, me), TILE) for kb in kbs]
            kinds = [jnp.clip(kb - qb, -2, 2) + 2 for kb in kbs]
            ss = [[mm(key_ref[h, ks, :], queries[h]) for h in range(heads)] for ks in kss]
            tops = list(tops)
            for i, ks in enumerate(kss):
                for h in range(heads):
                    s = ss[i][h] + bias_ref[h * KINDS + kinds[i]]
                    score_ref[h, ks, :] = s
                    tops[h] = jnp.maximum(tops[h], jnp.max(s.reshape(TILE // 8, 8, TILE), axis=0))
            return tuple(tops)

        tops = over_tiles(low, high, score_tiles, (jnp.full((8, TILE), -3e38, F32),) * heads)
        tops = [jnp.max(t, axis=0, keepdims=True) for t in tops]

        def value_tiles(kbs, sums):
            kss = [pl.ds(tile_start(kb, rows_dev, me), TILE) for kb in kbs]
            sums = list(sums)
            ps = []
            for ks in kss:
                for h in range(heads):
                    p = jnp.exp(score_ref[h, ks, :] - tops[h])
                    total, acc = sums[h]
                    sums[h] = (total + jnp.sum(p.reshape(TILE // 8, 8, TILE), axis=0), acc)
                    ps.append(p.astype(BF16))
            for i, ks in enumerate(kss):
                for h in range(heads):
                    values = qkv_ref[2 * cols + h * HEAD_DIM : 2 * cols + (h + 1) * HEAD_DIM, ks]
                    total, acc = sums[h]
                    sums[h] = (total, acc + mm(values, ps[i * heads + h]))
            return tuple(sums)

        zero = (jnp.zeros((8, TILE), F32), jnp.zeros((HEAD_DIM, TILE), F32))
        sums = over_tiles(low, high, value_tiles, (zero,) * heads)
        for h in range(heads):
            total, acc = sums[h]
            total = jnp.sum(total, axis=0, keepdims=True)
            mixed = acc * (1.0 / total)
            hs = slice(h * HEAD_DIM, (h + 1) * HEAD_DIM)
            wide_ref[hs, at] = mixed
            out_ref[hs, at] = mixed.astype(BF16)
            lse_ref[h : h + 1, at] = tops[h] + jnp.log(total)
        return carry

    lax.fori_loop(0, tiles // 2, query_tile, 0)


def attend_far_kernel(
    heads,
    rows_dev,
    info_ref,
    base_ref,
    w_ref,
    slot0_ref,
    slot1_ref,
    slot2_ref,
    slot3_ref,
    out_ref,
    wide_ref,
    lse_ref,
    qkv_ref,
    key_ref,
    score_ref,
    bias_ref,
):
    rows = qkv_ref.shape[1]
    cols = heads * HEAD_DIM
    w_rows = w_ref[:, : 3 * cols].T
    for i, slot_ref in enumerate((slot0_ref, slot1_ref, slot2_ref, slot3_ref)):
        for begin in range(0, rows_dev, TILE):
            part = contract(w_rows, 1, slot_ref[begin : begin + TILE, :], 1)
            at = i * rows_dev + begin
            qkv_ref[:, at : at + TILE] = part.astype(BF16)
    build_bias(base_ref, bias_ref, heads)
    key_seg = segment_all(rows, rows_dev, info_ref[0, 0], info_ref[0, 2], 1.0, 0.0)
    for h in range(heads):
        key_ref[h] = jnp.concatenate(
            [qkv_ref[cols + h * HEAD_DIM : cols + (h + 1) * HEAD_DIM, :], key_seg], axis=0
        ).T
    far = rows // rows_dev // 2
    attend_rows(
        heads, rows_dev, far, info_ref, qkv_ref, key_ref, out_ref, wide_ref, lse_ref, score_ref, bias_ref
    )


def attend_near_kernel(
    heads, rows_dev, info_ref, base_ref, qkv_ref, key_ref, out_ref, wide_ref, lse_ref, score_ref, bias_ref
):
    build_bias(base_ref, bias_ref, heads)
    attend_rows(
        heads, rows_dev, 0, info_ref, qkv_ref, key_ref, out_ref, wide_ref, lse_ref, score_ref, bias_ref
    )


def attend_shapes(heads, rows):
    cols = heads * HEAD_DIM
    return (
        jax.ShapeDtypeStruct((cols, rows // 2), BF16),
        jax.ShapeDtypeStruct((cols, rows // 2), F32),
        jax.ShapeDtypeStruct((heads, rows // 2), F32),
    )


def attend_scratch(heads, rows):
    return [
        pltpu.VMEM((heads, rows, TILE), F32),
        pltpu.VMEM((heads * KINDS, TILE, TILE), F32),
    ]


def attend_far(info, base, weights, slots):
    rows_dev = slots[0].shape[0]
    rows = rows_dev * len(slots)
    cols = weights.shape[1] // 3
    heads = cols // HEAD_DIM
    return pl.pallas_call(
        functools.partial(attend_far_kernel, heads, rows_dev),
        out_shape=attend_shapes(heads, rows)
        + (
            jax.ShapeDtypeStruct((3 * cols, rows), BF16),
            jax.ShapeDtypeStruct((heads, rows, 2 * HEAD_DIM), BF16),
        ),
        in_specs=[SMEM] + [VMEM] * 6,
        out_specs=(VMEM,) * 5,
        scratch_shapes=attend_scratch(heads, rows),
        compiler_params=pltpu.CompilerParams(vmem_limit_bytes=58 << 20),
        cost_estimate=SHORT,
        name="attend_far",
    )(info, base, weights, *slots)


def attend_near(info, base, qkv, keys, rows_dev):
    heads, rows = keys.shape[:2]
    return pl.pallas_call(
        functools.partial(attend_near_kernel, heads, rows_dev),
        out_shape=attend_shapes(heads, rows),
        in_specs=[SMEM] + [VMEM] * 3,
        out_specs=(VMEM,) * 3,
        scratch_shapes=attend_scratch(heads, rows),
        compiler_params=pltpu.CompilerParams(vmem_limit_bytes=58 << 20),
        cost_estimate=SHORT,
        name="attend_near",
    )(info, base, qkv, keys)


def diagonal_sums(values):
    values = jnp.concatenate([jnp.zeros_like(values), values], axis=1)
    count = TILE
    while count > 1:
        count //= 2
        values = values[:count] + pltpu.roll(values[count:], 2 * TILE - count, 1)
    return values


def grad_rows_to(own_ref, send_ref, rows_dev, grad_ref, w_ref):
    slots = grad_ref.shape[1] // rows_dev
    for i in range(slots // 2):
        slot = (slots - 2 * (i + 1)) % slots
        for at, out_ref in ((slot + 1, send_ref), (slot, own_ref)):
            for begin in range(0, rows_dev, TILE):
                cols = slice(at * rows_dev + begin, at * rows_dev + begin + TILE)
                part = contract(grad_ref[:, cols], 0, w_ref[...], 1)
                to = slice(i * rows_dev + begin, i * rows_dev + begin + TILE)
                out_ref[to, :] = part.astype(out_ref.dtype)


def attend_back_kernel(
    heads,
    rows_dev,
    info_ref,
    base_ref,
    qkv_ref,
    key_ref,
    wide0_ref,
    wide1_ref,
    lse0_ref,
    lse1_ref,
    grad0_ref,
    grad1_ref,
    w_ref,
    out_ref,
    diag_ref,
    own_ref,
    send_ref,
    lse_ref,
    inner_ref,
    grad_ref,
    query_ref,
    value_rows,
    query_rows,
    grad_rows,
    key_acc,
    value_acc,
    bias_ref,
    table_ref,
):
    rows = qkv_ref.shape[1]
    cols = heads * HEAD_DIM
    first_len, me = info_ref[0, 0], info_ref[0, 2]
    tiles = rows // TILE
    build_bias(base_ref, bias_ref, heads)
    query_seg = segment_all(rows, rows_dev, first_len, me, 0.0, NEG)
    q_of = [slice(h * HEAD_DIM, (h + 1) * HEAD_DIM) for h in range(heads)]
    k_of = [slice(cols + h * HEAD_DIM, cols + (h + 1) * HEAD_DIM) for h in range(heads)]
    v_of = [slice(2 * cols + h * HEAD_DIM, 2 * cols + (h + 1) * HEAD_DIM) for h in range(heads)]
    lse_ref[:, : rows // 2] = lse0_ref[...]
    lse_ref[:, rows // 2 :] = lse1_ref[...]
    grad_ref[:, : rows // 2] = grad0_ref[...]
    grad_ref[:, rows // 2 :] = grad1_ref[...]
    for h in range(heads):
        queries = qkv_ref[q_of[h], :]
        query_ref[h] = jnp.concatenate([queries, query_seg], axis=0)
        query_rows[h] = queries.T
        value_rows[h] = qkv_ref[v_of[h], :].T
        grad_rows[h] = grad_ref[q_of[h], :].T
        for half, wide_ref in ((0, wide0_ref), (1, wide1_ref)):
            at = slice(half * rows // 2, (half + 1) * rows // 2)
            terms = grad_ref[q_of[h], at].astype(F32) * wide_ref[q_of[h], :]
            inner_ref[h : h + 1, at] = jnp.sum(terms, axis=0, keepdims=True)
    key_acc[...] = jnp.zeros_like(key_acc)
    value_acc[...] = jnp.zeros_like(value_acc)
    table_ref[...] = jnp.zeros_like(table_ref)

    def query_tile(qb, carry):
        qs = pl.ds(tile_start(qb, rows_dev, me), TILE)
        low, high = tile_range(qb, first_len, tiles)
        grads = [grad_ref[q_of[h], qs] for h in range(heads)]
        inner = [inner_ref[h : h + 1, qs] for h in range(heads)]
        lse = [lse_ref[h : h + 1, qs] for h in range(heads)]

        def tiles_at(kbs, sums):
            kss = [pl.ds(tile_start(kb, rows_dev, me), TILE) for kb in kbs]
            kinds = [jnp.clip(kb - qb, -2, 2) + 2 for kb in kbs]
            ss = [[mm(key_ref[h, ks, :], query_ref[h, :, qs]) for h in range(heads)] for ks in kss]
            dps = [[mm(value_rows[h, ks, :], grads[h]) for h in range(heads)] for ks in kss]
            lows = []
            for i in range(len(kbs)):
                for h in range(heads):
                    p = jnp.exp(ss[i][h] + bias_ref[h * KINDS + kinds[i]] - lse[h])
                    ds = p * (dps[i][h] - inner[h])
                    table_ref[h * KINDS + kinds[i]] += ds
                    lows.append((p.astype(BF16), ds.astype(BF16)))
            sums = list(sums)
            for i, ks in enumerate(kss):
                for h in range(heads):
                    low_p, low_ds = lows[i * heads + h]
                    value_acc[h, ks, :] += mm(low_p, grad_rows[h, qs, :])
                    key_acc[h, ks, :] += mm(low_ds, query_rows[h, qs, :])
                    sums[h] = sums[h] + mm(qkv_ref[k_of[h], ks], low_ds)
            return tuple(sums)

        sums = tuple(jnp.zeros((HEAD_DIM, TILE), F32) for _ in range(heads))
        sums = over_tiles(low, high, tiles_at, sums, (2, 1))
        for h in range(heads):
            out_ref[q_of[h], qs] = sums[h].astype(BF16)
        return carry

    lax.fori_loop(0, tiles, query_tile, 0)
    for h in range(heads):
        out_ref[k_of[h], :] = key_acc[h].astype(BF16).T
        out_ref[v_of[h], :] = value_acc[h].astype(BF16).T
    grad_rows_to(own_ref, send_ref, rows_dev, out_ref, w_ref)
    for i in range(heads * KINDS):
        if i % KINDS in (0, KINDS - 1):
            total = jnp.sum(table_ref[i], axis=0, keepdims=True)
            diag_ref[i : i + 1, :] = jnp.concatenate([total, jnp.zeros_like(total)], axis=1)
        else:
            diag_ref[i : i + 1, :] = diagonal_sums(table_ref[i])


def attend_back(info, base, qkv, keys, wide, lse, grad, weights, rows_dev):
    rows = qkv.shape[1]
    width = weights.shape[0]
    heads = qkv.shape[0] // (3 * HEAD_DIM)
    cols = heads * HEAD_DIM
    return pl.pallas_call(
        functools.partial(attend_back_kernel, heads, rows_dev),
        out_shape=(
            jax.ShapeDtypeStruct((3 * cols, rows), BF16),
            jax.ShapeDtypeStruct((heads * KINDS, 2 * TILE), F32),
            jax.ShapeDtypeStruct((rows // 2, width), F32),
            jax.ShapeDtypeStruct((rows // 2, width), BF16),
        ),
        in_specs=[SMEM] + [VMEM] * 10,
        out_specs=(VMEM,) * 4,
        scratch_shapes=[
            pltpu.VMEM((heads, rows), F32),
            pltpu.VMEM((heads, rows), F32),
            pltpu.VMEM((cols, rows), BF16),
            pltpu.VMEM((heads, 2 * HEAD_DIM, rows), BF16),
            pltpu.VMEM((heads, rows, HEAD_DIM), BF16),
            pltpu.VMEM((heads, rows, HEAD_DIM), BF16),
            pltpu.VMEM((heads, rows, HEAD_DIM), BF16),
            pltpu.VMEM((heads, rows, HEAD_DIM), F32),
            pltpu.VMEM((heads, rows, HEAD_DIM), F32),
            pltpu.VMEM((heads * KINDS, TILE, TILE), F32),
            pltpu.VMEM((heads * KINDS, TILE, TILE), F32),
        ],
        compiler_params=pltpu.CompilerParams(vmem_limit_bytes=58 << 20),
        cost_estimate=LONG,
        name="attend_back",
    )(info, base, qkv, keys, *wide, *lse, *grad, weights)


def scaled_rows(values):
    return values * lax.rsqrt(jnp.mean(values * values, axis=-1, keepdims=True) + EPS)


def join_kernel(rows_ref, near_ref, far_ref, gain_ref, middle_ref, low_ref):
    middle = rows_ref[...].astype(F32) + near_ref[...] + far_ref[...].astype(F32)
    middle_ref[...] = middle
    low_ref[...] = (scaled_rows(middle) * gain_ref[...]).astype(BF16)


def norm_back_rows(values, upstream, gain):
    scale = lax.rsqrt(jnp.mean(values * values, axis=-1, keepdims=True) + EPS)
    normed = values * scale
    scaled = upstream * gain
    inner = jnp.mean(scaled * normed, axis=-1, keepdims=True)
    return scale * (scaled - normed * inner)


def middle_back_kernel(middle_ref, near_ref, far_ref, grads_ref, gain_ref, wide_ref, low_ref):
    upstream = near_ref[...] + far_ref[...].astype(F32)
    back = norm_back_rows(middle_ref[...], upstream, gain_ref[...])
    wide = grads_ref[...].astype(F32) + back
    wide_ref[...] = wide
    low_ref[...] = wide.astype(BF16)


def rows_back_kernel(rows_ref, near_ref, core_ref, far_ref, wide_ref, gain_ref, low_ref):
    upstream = near_ref[...] + core_ref[...].astype(F32) + far_ref[...].astype(F32)
    back = norm_back_rows(rows_ref[...].astype(F32), upstream, gain_ref[...])
    low_ref[...] = (wide_ref[...] + back).astype(BF16)


def by_rows(kernel, name, gain, *operands, out, cost=SHORT):
    rows, width = operands[0].shape
    spec = pl.BlockSpec((TILE, width), lambda i: (i, 0))
    once = pl.BlockSpec((1, width), lambda i: (0, 0))
    return pl.pallas_call(
        kernel,
        grid=(rows // TILE,),
        out_shape=tuple(jax.ShapeDtypeStruct((rows, width), kind) for kind in out),
        in_specs=[spec] * len(operands) + [once],
        out_specs=(spec,) * len(out),
        compiler_params=pltpu.CompilerParams(vmem_limit_bytes=58 << 20),
        cost_estimate=cost,
        name=name,
    )(*operands, gain[None])


def out_proj_kernel(own_ref, other_ref, w_own_ref, w_other_ref, near_ref, send_ref):
    half = near_ref.shape[0]
    for begin in range(0, 2 * half, TILE):
        part = contract(own_ref[:, begin : begin + TILE], 0, w_own_ref[...], 0)
        part = part + contract(other_ref[:, begin : begin + TILE], 0, w_other_ref[...], 0)
        if begin < half:
            near_ref[begin : begin + TILE, :] = part
        else:
            send_ref[begin - half : begin - half + TILE, :] = part.astype(BF16)


def out_proj(own, other, w_own, w_other):
    half, width = own.shape[1] // 2, w_own.shape[1]
    return pl.pallas_call(
        out_proj_kernel,
        out_shape=(
            jax.ShapeDtypeStruct((half, width), F32),
            jax.ShapeDtypeStruct((half, width), BF16),
        ),
        in_specs=[VMEM] * 4,
        out_specs=(VMEM, VMEM),
        cost_estimate=SHORT,
        name="out_proj",
    )(own, other, w_own, w_other)


def mixed_grads_kernel(middle0, middle1, w_own_ref, w_other_ref, own_ref, send_ref):
    half = middle0.shape[0]
    for w_ref, out_ref in ((w_other_ref, send_ref), (w_own_ref, own_ref)):
        for i, middle_ref in enumerate((middle0, middle1)):
            part = contract(w_ref[...], 1, middle_ref[...], 1)
            out_ref[:, i * half : (i + 1) * half] = part.astype(BF16)


def mixed_grads(middle, w_own, w_other):
    shape = jax.ShapeDtypeStruct((w_own.shape[0], 2 * middle[0].shape[0]), BF16)
    return pl.pallas_call(
        mixed_grads_kernel,
        out_shape=(shape, shape),
        in_specs=[VMEM] * 4,
        out_specs=(VMEM, VMEM),
        cost_estimate=SHORT,
        name="mixed_grads",
    )(*middle, w_own, w_other)


def ffn_kernel(
    ring,
    normed0,
    normed1,
    grad0,
    grad1,
    inner0,
    inner1,
    outer0,
    outer1,
    own_ref,
    send_ref,
    out_own_ref,
    out_send_ref,
    grads_ref,
    gain_ref,
    hid_ref,
    pre_ref,
    acc_ref,
    out_acc_ref,
    left_ref,
    gain_acc,
):
    half, width = own_ref.shape
    part = inner0.shape[1]
    block = grads_ref.shape[1]
    per_part = part // TILE
    steps = 2 * per_part
    sweeps = 2 * part // block
    step = pl.program_id(0)
    root, cubic = 0.7978845608028654, 0.044715
    places = [
        (normed_ref, grad_ref, begin, i * half + begin)
        for i, (normed_ref, grad_ref) in enumerate(((normed0, grad0), (normed1, grad1)))
        for begin in range(0, half, TILE)
    ]
    weights = ((inner0, outer0), (inner1, outer1))

    def tile(inner_ref, outer_ref, index, offset):
        js = slice(index * TILE, (index + 1) * TILE)
        to = slice(offset + index * TILE, offset + (index + 1) * TILE)
        firsts = []
        for normed_ref, grad_ref, begin, _ in places:
            rs = slice(begin, begin + TILE)
            a = mm(normed_ref[rs, :], inner_ref[:, js])
            firsts.append((a, mm(grad_ref[rs, :], outer_ref[:, js])))
        for (a, dh), (_, _, _, at) in zip(firsts, places):
            rs = slice(at, at + TILE)
            square = a * a
            t = jnp.tanh(root * a * (1.0 + cubic * square))
            cdf = 0.5 * (1.0 + t)
            slope = cdf + 0.5 * a * (1.0 - t * t) * (root * (1.0 + 3.0 * cubic * square))
            hid_ref[rs, to] = (a * cdf).astype(BF16)
            pre_ref[rs, to] = (dh * slope).astype(BF16)

    def rows_out(kept_ref, w_ref, offset, sum_ref, near_ref, far_ref):
        for _, _, _, at in places:
            rs = slice(at, at + TILE)
            back = contract(kept_ref[rs, offset : offset + part], 1, w_ref[...], 1)
            if offset == 0:
                sum_ref[rs, :] = back
            elif at < half:
                near_ref[rs, :] = sum_ref[rs, :] + back
            else:
                far_ref[at - half : at - half + TILE, :] = (sum_ref[rs, :] + back).astype(BF16)

    for i, (inner_ref, outer_ref) in enumerate(weights):
        for index in range(per_part):

            @pl.when(step == i * per_part + index)
            def _(inner_ref=inner_ref, outer_ref=outer_ref, index=index, offset=i * part):
                tile(inner_ref, outer_ref, index, offset)
                if index == per_part - 1:
                    rows_out(pre_ref, inner_ref, offset, acc_ref, own_ref, send_ref)
                    rows_out(hid_ref, outer_ref, offset, out_acc_ref, out_own_ref, out_send_ref)

    def load(first_ref, second_ref):
        left_ref[:, :half] = first_ref[...].T
        left_ref[:, half:] = second_ref[...].T

    for i in range(sweeps):

        @pl.when(step == steps + i)
        def _(i=i):
            if i == 0:
                load(normed0, normed1)
            values = mm(left_ref[...], pre_ref[:, i * block : (i + 1) * block])
            store_ringed(grads_ref, ring, 0, block, values.astype(BF16))
            lanes = gain_acc.shape[1]
            total = jnp.zeros(gain_acc.shape, F32) if i == 0 else gain_acc[...]
            for b in range(0, block, lanes):
                at = i * block + b
                w_ref = inner0 if at < part else inner1
                w = w_ref[:, at % part : at % part + lanes].astype(F32)
                total = total + values[:, b : b + lanes] * w
            gain_acc[...] = total
            if i == sweeps - 1:
                gain_ref[...] = jnp.sum(total.T, axis=0, keepdims=True)

        @pl.when(step == steps + sweeps + i)
        def _(i=i):
            if i == 0:
                load(grad0, grad1)
            values = mm(left_ref[...], hid_ref[:, i * block : (i + 1) * block])
            store_ringed(grads_ref, ring, 0, block, values.astype(BF16))


def ffn(ring, normed, grads, inners, outers):
    half, width = normed[0].shape
    part = inners[0].shape[1]
    rows, hidden = 2 * half, 2 * part
    block = 2 * TILE
    steps = hidden // TILE
    whole = pl.BlockSpec((half, width), lambda j: (0, 0), pipeline_mode=pl.Buffered(1))
    weight = pl.BlockSpec((width, part), lambda j: (0, 0), pipeline_mode=pl.Buffered(1))
    once = pl.BlockSpec((half, width), lambda j: (0, 0))
    return pl.pallas_call(
        functools.partial(ffn_kernel, ring),
        grid=(steps + 2 * (hidden // block),),
        out_shape=(
            jax.ShapeDtypeStruct((half, width), F32),
            jax.ShapeDtypeStruct((half, width), BF16),
            jax.ShapeDtypeStruct((half, width), F32),
            jax.ShapeDtypeStruct((half, width), BF16),
            jax.ShapeDtypeStruct((width, 2 * hidden), BF16),
            jax.ShapeDtypeStruct((1, width), F32),
        ),
        in_specs=[whole] * 4 + [weight] * 4,
        out_specs=(
            once,
            once,
            once,
            once,
            pl.BlockSpec((width, block), lambda j: (0, jnp.maximum(j - steps, 0))),
            pl.BlockSpec((1, width), lambda j: (0, 0)),
        ),
        scratch_shapes=[
            pltpu.VMEM((rows, hidden), BF16),
            pltpu.VMEM((rows, hidden), BF16),
            pltpu.VMEM((rows, width), F32),
            pltpu.VMEM((rows, width), F32),
            pltpu.VMEM((width, rows), BF16),
            pltpu.VMEM((width, 128), F32),
        ],
        compiler_params=pltpu.CompilerParams(vmem_limit_bytes=52 << 20),
        cost_estimate=SHORT,
        name="ffn",
    )(*normed, *grads, *inners, *outers)


def proj_grads_kernel(middle0, middle1, mixed0, mixed1, out_ref):
    half = middle0.shape[0]
    total = 0.0
    for i, middle_ref in enumerate((middle0, middle1)):
        at = slice(i * half, (i + 1) * half)
        mixed = jnp.concatenate([mixed0[:, at], mixed1[:, at]], axis=0)
        total = total + contract(middle_ref[...].T, 1, mixed, 1)
    out_ref[...] = total.astype(BF16)


def proj_grads(middle, mixed):
    shape = (middle[0].shape[1], 2 * mixed[0].shape[0])
    return pl.pallas_call(
        proj_grads_kernel,
        out_shape=jax.ShapeDtypeStruct(shape, BF16),
        in_specs=[VMEM] * 4,
        out_specs=VMEM,
        compiler_params=pltpu.CompilerParams(vmem_limit_bytes=24 << 20),
        cost_estimate=SHORT,
        name="proj_grads",
    )(*middle, *mixed)


def qkv_grads_kernel(
    ring,
    grad_ref,
    slot0_ref,
    slot1_ref,
    slot2_ref,
    slot3_ref,
    w_ref,
    proj_ref,
    out_ref,
    gain_ref,
):
    rows_dev = slot0_ref.shape[0]
    total = 0.0
    for i, slot_ref in enumerate((slot0_ref, slot1_ref, slot2_ref, slot3_ref)):
        total = total + mm(grad_ref[:, i * rows_dev : (i + 1) * rows_dev], slot_ref[...])
    gain_ref[...] = jnp.sum(total * w_ref[:, : total.shape[0]].T.astype(F32), axis=0, keepdims=True)
    both = jnp.concatenate([total.T.astype(BF16), proj_ref[...]], axis=1)
    store_ringed(out_ref, ring, 0, out_ref.shape[1], both)


def qkv_grads(ring, grad_qkv, slots, weights, proj):
    width = slots[0].shape[1]
    cols = grad_qkv.shape[0] + proj.shape[1]
    return pl.pallas_call(
        functools.partial(qkv_grads_kernel, ring),
        out_shape=(
            jax.ShapeDtypeStruct((width, cols), BF16),
            jax.ShapeDtypeStruct((1, width), F32),
        ),
        in_specs=[VMEM] * 7,
        out_specs=(VMEM, VMEM),
        compiler_params=pltpu.CompilerParams(vmem_limit_bytes=58 << 20),
        cost_estimate=SHORT,
        name="qkv_grads",
    )(grad_qkv, *slots, weights, proj)


def finish_kernel(
    pack_ref, taken_ref, last_ref, far_ref, query_ref, key_ref, value_ref, proj_ref, inner_ref, outer_ref
):
    hidden, cols = inner_ref.shape[1], query_ref.shape[1]
    pack, taken, last = pack_ref[...].astype(F32), taken_ref[...].astype(F32), last_ref[...].astype(F32)
    inner_ref[...] = pack[:, :hidden] + taken[:, :hidden]
    outer_ref[...] = pack[:, 2 * hidden : 3 * hidden] + taken[:, hidden:]
    for i, out_ref in enumerate((query_ref, key_ref, value_ref)):
        out_ref[...] = last[:, i * cols : (i + 1) * cols]
    proj_ref[...] = last[:, 3 * cols : 4 * cols] + far_ref[...].astype(F32)


def finish(pack, taken, last, far, hidden):
    rows, cols = far.shape
    shapes = [(rows, cols)] * 4 + [(rows, hidden)] * 2
    return pl.pallas_call(
        finish_kernel,
        out_shape=tuple(jax.ShapeDtypeStruct(shape, F32) for shape in shapes),
        in_specs=[VMEM] * 4,
        out_specs=(VMEM,) * 6,
        cost_estimate=SHORT,
        name="finish",
    )(pack, taken, last, far)


def bias_rows(line):
    heads = line.shape[0]
    pad = 3 * TILE
    rev = jnp.flip(line, axis=1)
    left = jnp.broadcast_to(rev[:, :1], (heads, pad))
    right = jnp.broadcast_to(rev[:, -1:], (heads, pad + 2 * TILE))
    ext = jnp.concatenate([left, rev, right], axis=1)
    begin = [pad + MAXDIST - TILE - TILE * d for d in range(-2, 3)]
    rows = [ext[:, b : b + 2 * TILE] for b in begin]
    return jnp.stack(rows, axis=1).reshape(heads * KINDS, 2 * TILE)


def line_index():
    kind = lax.broadcasted_iota(jnp.int32, (KINDS, 2 * TILE), 0) - 2
    lane = lax.broadcasted_iota(jnp.int32, (KINDS, 2 * TILE), 1)
    near = jnp.clip(TILE + TILE * kind - lane, -MAXDIST, MAXDIST)
    far = jnp.where(kind < 0, -MAXDIST, MAXDIST)
    return (jnp.where(jnp.abs(kind) == 2, far, near) + MAXDIST).reshape(KINDS * 2 * TILE)


def on_device(
    tokens,
    cotangent,
    w_query,
    w_key,
    w_value,
    w_proj,
    w_inner,
    w_outer,
    gain_attn,
    gain_ffn,
    rel_table,
    lengths,
    deal,
    buckets,
):
    rows_dev = tokens.shape[0]
    tensor_size = lax.axis_size("tensor")
    dp_size = lax.axis_size("dp")
    me = lax.axis_index("tensor")
    heads = w_query.shape[1] // HEAD_DIM
    cols = heads * HEAD_DIM
    hidden = w_inner.shape[1]
    width = tokens.shape[1]
    pair = 2 * rows_dev

    def swap(values, bit):
        return lax.ppermute(values, "tensor", [(i, i ^ bit) for i in range(tensor_size)])

    def deal_out(values):
        return lax.all_to_all(values, "dp", split_axis=0, concat_axis=0, tiled=True)

    def pick(values, order):
        return values.at[order].get(mode="promise_in_bounds", unique_indices=True)

    def total_sum(values, passing):
        values = values + swap(values, 1)
        step = 1
        while step < dp_size:
            if 2 * step >= dp_size:
                values, passing = after(values, passing)
                values = values + swap(values, 2)
            values = values + lax.ppermute(values, "dp", [(i, i ^ step) for i in range(dp_size)])
            step *= 2
        return values, passing

    ring = ring_order(dp_size)
    both = ("dp", "tensor")
    ring_groups = [[d * tensor_size + t for d in ring] for t in range(tensor_size)]

    def gather(values, spans):
        found = lax.all_gather(values, both, axis=0, tiled=True, axis_index_groups=ring_groups)
        return unring(found, ring, spans)

    def scatter_sum(values):
        return lax.psum_scatter(
            ringed(values, ring), both, scatter_dimension=0, tiled=True, axis_index_groups=ring_groups
        )

    own_front, own_inner = pack_weights(
        w_inner, w_query, w_key, w_value, w_proj.T, w_outer.T
    )
    own_front, tokens = after(own_front, tokens)
    ends = (3 * cols, 3 * cols + hidden, 4 * cols + hidden)
    front, outer_own, proj_own = gather(
        own_front, ((0, ends[0], False), (ends[0], ends[1], False), (ends[1], ends[2], True))
    )
    low_rows = deal_out(pick(tokens, deal))
    onehot_buckets = (
        buckets[:, None] == jnp.arange(rel_table.shape[0], dtype=jnp.int32)[None, :]
    ).astype(F32)
    head_table = lax.dynamic_slice_in_dim(rel_table, me * heads, heads, 1)
    offset_bias = jnp.dot(onehot_buckets, head_table, precision=lax.Precision.HIGHEST).T
    base = bias_rows(offset_bias)
    info = jnp.concatenate([lengths, jnp.full((1, 1), me, jnp.int32)], axis=1)

    inverse_order = (
        jnp.zeros((rows_dev,), jnp.int32).at[deal].set(jnp.arange(rows_dev, dtype=jnp.int32))
    )
    slot0 = (scaled_rows(low_rows.astype(F32)) * gain_attn).astype(BF16)
    own_inner, slot0 = after(own_inner, slot0)
    inner_own, inner_other = gather(
        jnp.concatenate([own_inner, swap(own_inner, 2)], axis=1),
        ((0, hidden, False), (hidden, 2 * hidden, False)),
    )
    slot2 = swap(slot0, 2)
    slot1 = swap(slot0, 1)
    slot2, front, base, info = after(slot2, front, base, info)
    slot3 = swap(slot2, 1)
    slots = (slot0, slot1, slot2, slot3)
    proj_other, outer_other = swap(proj_own, 2), swap(outer_own, 2)

    low_grads = deal_out(pick(cotangent, deal))

    mixed_far, wide_far, lse_far, qkv, keys = attend_far(info, base, front, slots)
    mixed_other = swap(mixed_far, 2)
    late_qkv, outer_other, low_grads = after(qkv, outer_other, low_grads)
    mixed_own, wide_own, lse_own = attend_near(info, base, late_qkv, keys, rows_dev)
    near, to_core = out_proj(mixed_own, mixed_other, proj_own, proj_other)
    near, inner_own, inner_other = after(near, inner_own, inner_other)
    middle, low_two = by_rows(
        join_kernel, "join", gain_ffn, low_rows, near, swap(to_core, 1), out=(F32, BF16)
    )

    pair_two = (low_two, swap(low_two, 1))
    pair_grads = (low_grads, swap(low_grads, 1))
    back_own, back_send, out_own, out_far, grad_pack, gain_two = ffn(
        ring, pair_two, pair_grads, (inner_own, inner_other), (outer_own, outer_other)
    )
    shard_pack = scatter_sum(grad_pack)
    grad_middle, low_middle = by_rows(
        middle_back_kernel,
        "middle_back",
        gain_ffn,
        middle,
        back_own,
        swap(back_send, 1),
        low_grads,
        out=(F32, BF16),
    )
    pair_middle = (low_middle, swap(low_middle, 1))
    grad_own, to_other = mixed_grads(pair_middle, proj_own, proj_other)

    proj_pack = proj_grads(pair_middle, (mixed_own, mixed_other))

    out_own, to_other = after(out_own, to_other)
    result_rows = (middle + out_own + swap(out_far, 1).astype(F32)).astype(BF16)
    result_rows, proj_pack = after(result_rows, proj_pack)
    back_rows = deal_out(result_rows)

    grad_far, proj_pack = after(swap(to_other, 2), proj_pack)
    grad_qkv, diagonals, rows_own, rows_send = attend_back(
        info,
        base,
        qkv,
        keys,
        (wide_own, wide_far),
        (lse_own, lse_far),
        (grad_own, grad_far),
        front,
        rows_dev,
    )
    rows_send, back_rows = after(rows_send, back_rows)
    rows_core = swap(rows_send, 1)
    grad_later = (rows_own[:rows_dev] + rows_core[:rows_dev].astype(F32)).astype(BF16)
    later_qkv, grad_later = after(grad_qkv, grad_later)
    low_qkv_w, gain_one = qkv_grads(ring, later_qkv, slots, front, proj_pack)
    low_qkv_w, shard_pack = after(low_qkv_w, shard_pack)
    shard_qkv = scatter_sum(low_qkv_w)
    out_rows = pick(back_rows, inverse_order)
    rows_near, out_rows = after(rows_core[rows_dev:], out_rows)
    (low_grad_rows,) = by_rows(
        rows_back_kernel,
        "rows_back",
        gain_attn,
        low_rows,
        rows_own[rows_dev:],
        rows_near,
        swap(grad_later, 2),
        grad_middle,
        out=(BF16,),
        cost=LONG,
    )
    taken = swap(
        jnp.concatenate([shard_pack[:, hidden : 2 * hidden], shard_pack[:, 3 * hidden :]], axis=1),
        2,
    )

    offset_count = 2 * MAXDIST + 1
    onehot_line = (
        line_index()[:, None] == jnp.arange(offset_count, dtype=jnp.int32)[None, :]
    ).astype(F32)
    offset_total = jnp.dot(
        diagonals.reshape(heads, KINDS * 2 * TILE), onehot_line, precision=lax.Precision.HIGHEST
    )
    table_heads = jnp.dot(onehot_buckets.T, offset_total.T, precision=lax.Precision.HIGHEST)
    table_full = lax.dynamic_update_slice_in_dim(
        jnp.zeros(rel_table.shape, F32), table_heads, me * heads, 1
    )
    terms = [gain_one[0] / gain_attn, gain_two[0] / gain_ffn, table_full.reshape(-1)]
    small, taken = total_sum(jnp.concatenate(terms).reshape(-1, 128), taken)
    small = small.reshape(-1)
    back_grads = deal_out(low_grad_rows)
    weight_shards = finish(shard_pack, taken, shard_qkv, swap(shard_qkv[:, 4 * cols :], 2), hidden)
    return (
        out_rows,
        pick(back_grads, inverse_order),
        *weight_shards[:3],
        weight_shards[3].T,
        weight_shards[4],
        weight_shards[5].T,
        small[:width],
        small[width : 2 * width],
        small[2 * width :].reshape(rel_table.shape),
    )


def solution(mesh):
    rows = P(("dp", "tensor"), None)
    inward, outward = P("dp", "tensor"), P("tensor", "dp")
    weights = (inward, inward, inward, outward, inward, outward)
    return jax.shard_map(
        on_device,
        mesh=mesh,
        in_specs=(rows, rows, *weights, P(), P(), P(), P("dp", None), P(("dp", "tensor")), P()),
        out_specs=(rows, rows, *weights, P(), P(), P()),
        check_vma=False,
    )
```

profile of v0, /device:TPU:12, one launch (start us, length us, event | category | flops | bytes accessed | tf_op | source)
XLA Modules:
  0.0 307.5 jit_solution(6730791558641145330)
XLA Ops:
  13.8 33.1 %all_to_all.47 = bf16[8,64,768]{2,1,0:T(8,128)(2,1)S(1)} all-to-all(bf16[8,64,768]{2,1,0:T(8,128)(2,1)S(1)} %bitcast.36), channel_id=1, replica_groups=mesh['dp'=8,'tensor'=4] {'dp'}, dimensions={0} | all-to-all | bytes 1572864 | tf_op jit(solution)/shard_map/all_to_all | solution.py:878
  48.5 4.7 %collective-permute-done.6 = bf16[96,768]{1,0:T(8,128)(2,1)S(1)} collective-permute-done((bf16[96,768]{1,0:T(8,128)(2,1)S(1)}, bf16[96,768]{1,0:T(8,128)(2,1)S(1)}, u32[]{:S(2)}, u32[]{:S(2)}) %collective-permute-start.6) | collective-permute-done | bytes 147488 | tf_op jit(solution)/shard_map/ppermute | solution.py:875
  54.5 2.7 gather_fusion.1
  57.2 6.2 %all-to-all-start.1 = ((bf16[8,64,768]{2,1,0:T(8,128)(2,1)}), bf16[8,64,768]{2,1,0:T(8,128)(2,1)S(1)}, u32[]{:S(2)}, u32[]{:S(2)}) async-start(bf16[8,64,768]{2,1,0:T(8,128)(2,1)} %bitcast.6), calls=%async_computation.1 | async-start | bytes 1572864 | tf_op jit(solution)/shard_map/all_to_all | solution.py:878
  66.8 3.6 %unring.2 = (bf16[768,576]{1,0:T(8,128)(2,1)}, bf16[768,768]{1,0:T(8,128)(2,1)}, bf16[192,768]{1,0:T(8,128)(2,1)}) custom-call(bf16[768,1536]{1,0:T(8,128)(2,1)} %all-gather.3.cloned.1.call-done.found_ref), custom_call_target="tpu_custom_call" | custom-call | flops 1048576 | bytes 65536 | tf_op jit(solution)/shard_map/unring/pallas_call | solution.py:108
  75.2 14.2 %attend_far.1 = (bf16[192,1024]{1,0:T(8,128)(2,1)}, f32[192,1024]{1,0:T(8,128)}, f32[3,1024]{1,0:T(4,128)}, bf16[576,2048]{1,0:T(8,128)(2,1)}, bf16[3,2048,128]{2,1,0:T(8,128)(2,1)}) custom-call(s32[1,3]{1,0:T(1,128)} %pad_add_fusion.info_ref, f32[15,512]{1,0:T(8,128)} %reshape.111.base_ref, bf16[768,576]{1,0:T(8,128)(2,1)} %get-tuple-element.90.w_ref, ...), custom_call_target="tpu_custom_call" | custom-call | flops 1048576 | bytes 65536 | tf_op jit(solution)/shard_map/attend_far/pallas_call | solution.py:309
  91.4 8.0 %collective-permute-done.3.outer1 = bf16[768,768]{1,0:T(8,128)(2,1)} collective-permute-done((bf16[768,768]{1,0:T(8,128)(2,1)}, bf16[768,768]{1,0:T(8,128)(2,1)}, u32[]{:S(2)}, u32[]{:S(2)}) %collective-permute-start.3) | collective-permute-done | bytes 1179680 | tf_op jit(solution)/shard_map/ppermute | solution.py:875
  99.5 10.5 %attend_near.1 = (bf16[192,1024]{1,0:T(8,128)(2,1)}, f32[192,1024]{1,0:T(8,128)}, f32[3,1024]{1,0:T(4,128)}) custom-call(s32[1,3]{1,0:T(1,128)} %pad_add_fusion.info_ref, f32[15,512]{1,0:T(8,128)} %reshape.111.base_ref, bf16[576,2048]{1,0:T(8,128)(2,1)} %get-tuple-element.95.qkv_ref, bf16[3,2048,128]{2,1,0:T(8,128)(2,1)} %get-tuple-element.93.key_ref), custom_call_target="tpu_custom_call" | custom-call | flops 1048576 | bytes 65536 | tf_op jit(solution)/shard_map/attend_near/pallas_call | solution.py:327
  110.0 3.8 %collective-permute-done.5.w_other_ref = bf16[192,768]{1,0:T(8,128)(2,1)S(1)} collective-permute-done((bf16[192,768]{1,0:T(8,128)(2,1)S(1)}, bf16[192,768]{1,0:T(8,128)(2,1)S(1)}, u32[]{:S(2)}, u32[]{:S(2)}) %collective-permute-start.5) | collective-permute-done | bytes 294944 | tf_op jit(solution)/shard_map/ppermute | solution.py:875
  114.7 3.3 %out_proj.1 = (f32[512,768]{1,0:T(8,128)}, bf16[512,768]{1,0:T(8,128)(2,1)}) custom-call(bf16[192,1024]{1,0:T(8,128)(2,1)} %get-tuple-element.100.own_ref.mixed0, bf16[192,1024]{1,0:T(8,128)(2,1)} %copy-done.6, bf16[192,768]{1,0:T(8,128)(2,1)} %get-tuple-element.102.w_own_ref, bf16[192,768]{1,0:T(8,128)(2,1)} %copy-done.19), custom_call_target="tpu_custom_call" | custom-call | flops 1048576 | bytes 65536 | tf_op jit(solution)/shard_map/out_proj/pallas_call | solution.py:559
  119.1 3.2 %unring.3 = (bf16[768,768]{1,0:T(8,128)(2,1)}, bf16[768,768]{1,0:T(8,128)(2,1)}) custom-call(bf16[768,1536]{1,0:T(8,128)(2,1)} %all-gather.5.cloned.1.call-done.found_ref), custom_call_target="tpu_custom_call" | custom-call | flops 1048576 | bytes 65536 | tf_op jit(solution)/shard_map/unring/pallas_call | solution.py:108
  123.2 3.0 join.1
  126.2 2.5 collective-permute-done.8.normed1
  129.7 25.2 %ffn.1 = (f32[512,768]{1,0:T(8,128)}, bf16[512,768]{1,0:T(8,128)(2,1)S(1)}, f32[512,768]{1,0:T(8,128)}, bf16[512,768]{1,0:T(8,128)(2,1)S(1)}, bf16[768,3072]{1,0:T(8,128)(2,1)}, /*index=5*/f32[1,768]{1,0:T(1,128)S(1)}) custom-call(bf16[512,768]{1,0:T(8,128)(2,1)} %get-tuple-element.110.normed0, bf16[512,768]{1,0:T(8,128)(2,1)} %copy-done.23, ...), custom_call_target="tpu_custom_call" | custom-call | flops 1048576 | bytes 65536 | tf_op jit(solution)/shard_map/ffn/pallas_call | solution.py:708
  158.1 3.7 %middle_back.1 = (f32[512,768]{1,0:T(8,128)}, bf16[512,768]{1,0:T(8,128)(2,1)}) custom-call(f32[512,768]{1,0:T(8,128)} %get-tuple-element.109.middle_ref, f32[512,768]{1,0:T(8,128)} %get-tuple-element.115.near_ref, bf16[512,768]{1,0:T(8,128)(2,1)} %copy-done.20, bf16[512,768]{1,0:T(8,128)(2,1)} %bitcast.35, f32[1,768]{1,0:T(1,128)} %broadcast_in_dim.59.gain_ref), custom_call_target="tpu_custom_call" | custom-call | flops 1048576 | bytes 65536 | tf_op jit(solution)/shard_map/middle_back/pallas_call | solution.py:534
  165.3 3.5 %mixed_grads.1 = (bf16[192,1024]{1,0:T(8,128)(2,1)}, bf16[192,1024]{1,0:T(8,128)(2,1)}) custom-call(bf16[512,768]{1,0:T(8,128)(2,1)} %get-tuple-element.117.middle0, bf16[512,768]{1,0:T(8,128)(2,1)} %copy-done.3, bf16[192,768]{1,0:T(8,128)(2,1)} %get-tuple-element.102.w_own_ref, bf16[192,768]{1,0:T(8,128)(2,1)} %copy-done.19), custom_call_target="tpu_custom_call" | custom-call | flops 1048576 | bytes 65536 | tf_op jit(solution)/shard_map/mixed_grads/pallas_call | solution.py:582
  172.8 2.8 add_convert_fusion.1
  175.6 6.0 %all-to-all-start.2 = ((bf16[8,64,768]{2,1,0:T(8,128)(2,1)}), bf16[8,64,768]{2,1,0:T(8,128)(2,1)S(1)}, u32[]{:S(2)}, u32[]{:S(2)}) async-start(bf16[8,64,768]{2,1,0:T(8,128)(2,1)} %bitcast.8), calls=%async_computation.2 | async-start | bytes 1572864 | tf_op jit(solution)/shard_map/all_to_all | solution.py:878
  182.4 38.9 %attend_back.1 = (bf16[576,2048]{1,0:T(8,128)(2,1)}, f32[15,512]{1,0:T(8,128)}, f32[1024,768]{1,0:T(8,128)}, bf16[1024,768]{1,0:T(8,128)(2,1)}) custom-call(s32[1,3]{1,0:T(1,128)} %pad_add_fusion.info_ref, f32[15,512]{1,0:T(8,128)} %reshape.111.base_ref, bf16[576,2048]{1,0:T(8,128)(2,1)} %get-tuple-element.95.qkv_ref, ...), custom_call_target="tpu_custom_call" | custom-call | flops 25769803776 | bytes 67108864 | tf_op jit(solution)/shard_map/attend_back/pallas_call | solution.py:469
  221.4 3.6 %collective-permute-done.14 = bf16[1024,768]{1,0:T(8,128)(2,1)S(1)} collective-permute-done((bf16[1024,768]{1,0:T(8,128)(2,1)}, bf16[1024,768]{1,0:T(8,128)(2,1)S(1)}, u32[]{:S(2)}, u32[]{:S(2)}) %collective-permute-start.14) | collective-permute-done | bytes 1572896 | tf_op jit(solution)/shard_map/ppermute | solution.py:875
  225.0 3.6 %add_convert_fusion = (bf16[512,768]{1,0:T(8,128)(2,1)}, f32[512,768]{1,0:T(8,128)}) fusion(f32[1024,768]{1,0:T(8,128)} %get-tuple-element.131, bf16[1024,768]{1,0:T(8,128)(2,1)S(1)} %collective-permute-done.14), kind=kLoop, calls=%fused_computation.7 | loop fusion | flops 1179648 | bytes 6291456 | tf_op jit(solution)/shard_map/convert_element_type | solution.py:992
  229.9 2.4 scatter_custom_fusion
  232.6 2.7 gather_fusion.2
  236.2 6.3 %qkv_grads.1 = (bf16[768,960]{1,0:T(8,128)(2,1)}, f32[1,768]{1,0:T(1,128)}) custom-call(bf16[576,2048]{1,0:T(8,128)(2,1)} %get-tuple-element.136.grad_ref, bf16[512,768]{1,0:T(8,128)(2,1)} %copy-done.11, bf16[512,768]{1,0:T(8,128)(2,1)} %copy-done.15, bf16[512,768]{1,0:T(8,128)(2,1)} %copy-done.14, bf16[512,768]{1,0:T(8,128)(2,1)} %copy-done.16, ...), custom_call_target="tpu_custom_call" | custom-call | flops 1048576 | bytes 65536 | tf_op jit(solution)/shard_map/qkv_grads/pallas_call | solution.py:789
  242.5 6.0 %collective-permute-done.15.far_ref = bf16[512,768]{1,0:T(8,128)(2,1)} collective-permute-done((bf16[512,768]{1,0:T(8,128)(2,1)}, bf16[512,768]{1,0:T(8,128)(2,1)}, u32[]{:S(2)}, u32[]{:S(2)}) %collective-permute-start.15) | collective-permute-done | bytes 786464 | tf_op jit(solution)/shard_map/ppermute | solution.py:875
  248.5 3.7 %rows_back.1 = bf16[512,768]{1,0:T(8,128)(2,1)} custom-call(bf16[512,768]{1,0:T(8,128)(2,1)} %bitcast.32, f32[512,768]{1,0:T(8,128)} %get-tuple-element.189.near_ref, bf16[512,768]{1,0:T(8,128)(2,1)} %slice.86.core_ref, bf16[512,768]{1,0:T(8,128)(2,1)} %collective-permute-done.15.far_ref, f32[512,768]{1,0:T(8,128)} %get-tuple-element.135.wide_ref, ...), custom_call_target="tpu_custom_call" | custom-call | flops 25769803776 | bytes 67108864 | tf_op jit(solution)/shard_map/rows_back/pallas_call | solution.py:534
  252.3 9.0 %all-to-all-start.3 = ((bf16[8,64,768]{2,1,0:T(8,128)(2,1)}), bf16[8,64,768]{2,1,0:T(8,128)(2,1)S(1)}, u32[]{:S(2)}, u32[]{:S(2)}) async-start(bf16[8,64,768]{2,1,0:T(8,128)(2,1)} %bitcast.37), calls=%async_computation.3 | async-start | bytes 1572864 | tf_op jit(solution)/shard_map/all_to_all | solution.py:878
  266.2 2.2 collective-permute-done.17
  270.6 12.5 %collective-permute-done.18 = f32[15,128]{1,0:T(8,128)S(1)} collective-permute-done((f32[15,128]{1,0:T(8,128)S(1)}, f32[15,128]{1,0:T(8,128)S(1)}, u32[]{:S(2)}, u32[]{:S(2)}) %collective-permute-start.18) | collective-permute-done | bytes 7712 | tf_op jit(solution)/shard_map/ppermute | solution.py:890
  283.7 3.1 %collective-permute-done.21 = f32[15,128]{1,0:T(8,128)S(1)} collective-permute-done((f32[15,128]{1,0:T(8,128)S(1)}, f32[15,128]{1,0:T(8,128)S(1)}, u32[]{:S(2)}, u32[]{:S(2)}) %collective-permute-start.21) | collective-permute-done | bytes 7712 | tf_op jit(solution)/shard_map/ppermute | solution.py:875
  287.1 2.7 gather_fusion.3
  296.8 2.2 finish.1
  (182 shorter events, 54.0 us)
Async XLA Ops:
  7.2 59.6 %all-gather.3.cloned.1.call-start = ((), (), s32[]{:S(2)}) async-start(), calls=%async_computation.6 | async-start | bytes 2654208 | tf_op jit(solution)/shard_map/all_gather | solution.py:899
  11.0 108.1 %all-gather.5.cloned.1.call-start = ((), (), s32[]{:S(2)}) async-start(), calls=%async_computation.7 | async-start | bytes 2654208 | tf_op jit(solution)/shard_map/all_gather | solution.py:899
  13.8 33.5 %copy-start.27 = (f32[768]{0:T(1024)S(1)}, f32[768]{0:T(1024)}, u32[]{:S(2)}) copy-start(f32[768]{0:T(1024)} %param.22) | copy-start | bytes 9220
  48.0 5.1 %collective-permute-start.6 = (bf16[96,768]{1,0:T(8,128)(2,1)S(1)}, bf16[96,768]{1,0:T(8,128)(2,1)S(1)}, u32[]{:S(2)}, u32[]{:S(2)}) collective-permute-start(bf16[96,768]{1,0:T(8,128)(2,1)S(1)} %copy-done.25), channel_id=1, source_target_pairs={{0,2},{1,3},{2,0},{3,1},{4,6},{5,7},{6,4},{7,5},{8,10},{9,11},{10,... | collective-permute-start | bytes 442376 | tf_op jit(solution)/shard_map/ppermute | solution.py:875
  53.9 18.0 %collective-permute-start = (bf16[512,768]{1,0:T(8,128)(2,1)S(1)}, bf16[512,768]{1,0:T(8,128)(2,1)S(1)}, u32[]{:S(2)}, u32[]{:S(2)}) collective-permute-start(bf16[512,768]{1,0:T(8,128)(2,1)S(1)} %multiply_convert_fusion.slot0_ref), channel_id=1, source_target_pairs={{0,2},{1,3},{2,0},{3,1},{4,6},{5,7},{6,4},{7,5},{8,10},{9,11},{10,... | collective-permute-start | bytes 2359304 | tf_op jit(solution)/shard_map/ppermute | solution.py:875
  57.2 34.3 %all-to-all-start.1 = ((bf16[8,64,768]{2,1,0:T(8,128)(2,1)}), bf16[8,64,768]{2,1,0:T(8,128)(2,1)S(1)}, u32[]{:S(2)}, u32[]{:S(2)}) async-start(bf16[8,64,768]{2,1,0:T(8,128)(2,1)} %bitcast.6), calls=%async_computation.1 | async-start | bytes 1572864 | tf_op jit(solution)/shard_map/all_to_all | solution.py:878
  63.3 179.2 %reduce-scatter.3.cloned.1.call-start = ((), (), s32[]{:S(2)}) async-start(), calls=%async_computation.8 | async-start | bytes 5308416 | tf_op jit(solution)/shard_map/reduce_scatter | solution.py:903
  66.8 5.3 %collective-permute-start.1 = (bf16[512,768]{1,0:T(8,128)(2,1)S(1)}, bf16[512,768]{1,0:T(8,128)(2,1)S(1)}, u32[]{:S(2)}, u32[]{:S(2)}) collective-permute-start(bf16[512,768]{1,0:T(8,128)(2,1)S(1)} %multiply_convert_fusion.slot0_ref), channel_id=1, source_target_pairs={{0,1},{1,0},{2,3},{3,2},{4,5},{5,4},{6,7},{7,6},{8,9},{9,8},{10,11... | collective-permute-start | bytes 2359304 | tf_op jit(solution)/shard_map/ppermute | solution.py:875
  70.4 29.1 %collective-permute-start.3 = (bf16[768,768]{1,0:T(8,128)(2,1)}, bf16[768,768]{1,0:T(8,128)(2,1)}, u32[]{:S(2)}, u32[]{:S(2)}) collective-permute-start(bf16[768,768]{1,0:T(8,128)(2,1)} %get-tuple-element.94.outer0), channel_id=1, source_target_pairs={{0,2},{1,3},{2,0},{3,1},{4,6},{5,7},{6,4},{7,5},{8,10},{9,11},{10,... | collective-permute-start | bytes 3538952 | tf_op jit(solution)/shard_map/ppermute | solution.py:875
  72.0 2.3 collective-permute-start.2
  89.4 24.4 %collective-permute-start.4 = (bf16[192,1024]{1,0:T(8,128)(2,1)}, bf16[192,1024]{1,0:T(8,128)(2,1)S(1)}, u32[]{:S(2)}, u32[]{:S(2)}) collective-permute-start(bf16[192,1024]{1,0:T(8,128)(2,1)} %get-tuple-element.101), channel_id=1, source_target_pairs={{0,2},{1,3},{2,0},{3,1},{4,6},{5,7},{6,4},{7,5},{8,10},{9,11},{10,... | collective-permute-start | bytes 1179656 | tf_op jit(solution)/shard_map/ppermute | solution.py:875
  89.4 24.4 %collective-permute-start.5 = (bf16[192,768]{1,0:T(8,128)(2,1)S(1)}, bf16[192,768]{1,0:T(8,128)(2,1)S(1)}, u32[]{:S(2)}, u32[]{:S(2)}) collective-permute-start(bf16[192,768]{1,0:T(8,128)(2,1)S(1)} %copy-done.18), channel_id=1, source_target_pairs={{0,2},{1,3},{2,0},{3,1},{4,6},{5,7},{6,4},{7,5},{8,10},{9,11},{10,... | collective-permute-start | bytes 884744 | tf_op jit(solution)/shard_map/ppermute | solution.py:875
  91.4 27.2 %copy-start.12 = (bf16[8,64,768]{2,1,0:T(8,128)(2,1)}, bf16[8,64,768]{2,1,0:T(8,128)(2,1)S(1)}, u32[]{:S(2)}) copy-start(bf16[8,64,768]{2,1,0:T(8,128)(2,1)S(1)} %all-to-all-done.1) | copy-start | bytes 2359300
  118.0 4.3 %collective-permute-start.7 = (bf16[512,768]{1,0:T(8,128)(2,1)}, bf16[512,768]{1,0:T(8,128)(2,1)S(1)}, u32[]{:S(2)}, u32[]{:S(2)}) collective-permute-start(bf16[512,768]{1,0:T(8,128)(2,1)} %get-tuple-element.108), channel_id=1, source_target_pairs={{0,1},{1,0},{2,3},{3,2},{4,5},{5,4},{6,7},{7,6},{8,9},{9,8},{10,11... | collective-permute-start | bytes 2359304 | tf_op jit(solution)/shard_map/ppermute | solution.py:875
  118.6 7.6 %collective-permute-start.9 = (bf16[512,768]{1,0:T(8,128)(2,1)S(1)}, bf16[512,768]{1,0:T(8,128)(2,1)S(1)}, u32[]{:S(2)}, u32[]{:S(2)}) collective-permute-start(bf16[512,768]{1,0:T(8,128)(2,1)S(1)} %bitcast.33), channel_id=1, source_target_pairs={{0,1},{1,0},{2,3},{3,2},{4,5},{5,4},{6,7},{7,6},{8,9},{9,8},{10,11... | collective-permute-start | bytes 2359304 | tf_op jit(solution)/shard_map/ppermute | solution.py:875
  126.2 2.5 collective-permute-start.8
  154.9 2.4 collective-permute-start.10
  161.9 2.6 collective-permute-start.11
  162.1 10.3 %collective-permute-start.13 = (bf16[512,768]{1,0:T(8,128)(2,1)S(1)}, bf16[512,768]{1,0:T(8,128)(2,1)}, u32[]{:S(2)}, u32[]{:S(2)}) collective-permute-start(bf16[512,768]{1,0:T(8,128)(2,1)S(1)} %get-tuple-element.123), channel_id=1, source_target_pairs={{0,1},{1,0},{2,3},{3,2},{4,5},{5,4},{6,7},{7,6},{8,9},{9,8},{10,11... | collective-permute-start | bytes 2359304 | tf_op jit(solution)/shard_map/ppermute | solution.py:875
  168.8 12.8 %collective-permute-start.12 = (bf16[192,1024]{1,0:T(8,128)(2,1)}, bf16[192,1024]{1,0:T(8,128)(2,1)S(1)}, u32[]{:S(2)}, u32[]{:S(2)}) collective-permute-start(bf16[192,1024]{1,0:T(8,128)(2,1)} %get-tuple-element.121), channel_id=1, source_target_pairs={{0,2},{1,3},{2,0},{3,1},{4,6},{5,7},{6,4},{7,5},{8,10},{9,11},{10,... | collective-permute-start | bytes 1179656 | tf_op jit(solution)/shard_map/ppermute | solution.py:875
  175.6 45.7 %all-to-all-start.2 = ((bf16[8,64,768]{2,1,0:T(8,128)(2,1)}), bf16[8,64,768]{2,1,0:T(8,128)(2,1)S(1)}, u32[]{:S(2)}, u32[]{:S(2)}) async-start(bf16[8,64,768]{2,1,0:T(8,128)(2,1)} %bitcast.8), calls=%async_computation.2 | async-start | bytes 1572864 | tf_op jit(solution)/shard_map/all_to_all | solution.py:878
  181.6 109.7 %reduce-scatter.5.cloned.1.call-start = ((), (), s32[]{:S(2)}) async-start(), calls=%async_computation.9 | async-start | bytes 1769472 | tf_op jit(solution)/shard_map/reduce_scatter | solution.py:903
  221.3 3.7 %collective-permute-start.14 = (bf16[1024,768]{1,0:T(8,128)(2,1)}, bf16[1024,768]{1,0:T(8,128)(2,1)S(1)}, u32[]{:S(2)}, u32[]{:S(2)}) collective-permute-start(bf16[1024,768]{1,0:T(8,128)(2,1)} %get-tuple-element.128), channel_id=1, source_target_pairs={{0,1},{1,0},{2,3},{3,2},{4,5},{5,4},{6,7},{7,6},{8,9},{9,8},{10,11... | collective-permute-start | bytes 4718600 | tf_op jit(solution)/shard_map/ppermute | solution.py:875
  228.6 19.9 %collective-permute-start.15 = (bf16[512,768]{1,0:T(8,128)(2,1)}, bf16[512,768]{1,0:T(8,128)(2,1)}, u32[]{:S(2)}, u32[]{:S(2)}) collective-permute-start(bf16[512,768]{1,0:T(8,128)(2,1)} %get-tuple-element.134), channel_id=1, source_target_pairs={{0,2},{1,3},{2,0},{3,1},{4,6},{5,7},{6,4},{7,5},{8,10},{9,11},{10,... | collective-permute-start | bytes 2359304 | tf_op jit(solution)/shard_map/ppermute | solution.py:875
  252.3 34.8 %all-to-all-start.3 = ((bf16[8,64,768]{2,1,0:T(8,128)(2,1)}), bf16[8,64,768]{2,1,0:T(8,128)(2,1)S(1)}, u32[]{:S(2)}, u32[]{:S(2)}) async-start(bf16[8,64,768]{2,1,0:T(8,128)(2,1)} %bitcast.37), calls=%async_computation.3 | async-start | bytes 1572864 | tf_op jit(solution)/shard_map/all_to_all | solution.py:878
  263.4 1.2 collective-permute-start.16
  263.6 19.4 %collective-permute-start.19 = (bf16[96,1536]{1,0:T(8,128)(2,1)S(1)}, bf16[96,1536]{1,0:T(8,128)(2,1)S(1)}, u32[]{:S(2)}, u32[]{:S(2)}) collective-permute-start(bf16[96,1536]{1,0:T(8,128)(2,1)S(1)} %pad_maximum_fusion.1), channel_id=1, source_target_pairs={{0,2},{1,3},{2,0},{3,1},{4,6},{5,7},{6,4},{7,5},{8,10},{9,11},{10,... | collective-permute-start | bytes 884744 | tf_op jit(solution)/shard_map/ppermute | solution.py:875
  264.7 3.7 %collective-permute-start.17 = (f32[15,128]{1,0:T(8,128)S(1)}, f32[15,128]{1,0:T(8,128)S(1)}, u32[]{:S(2)}, u32[]{:S(2)}) collective-permute-start(f32[15,128]{1,0:T(8,128)S(1)} %fusion.16), channel_id=1, source_target_pairs={{0,4},{4,0},{8,12},{12,8},{16,20},{20,16},{24,28},{28,24},{1,5},{5... | collective-permute-start | bytes 23048 | tf_op jit(solution)/shard_map/ppermute | solution.py:890
  268.4 14.7 %collective-permute-start.18 = (f32[15,128]{1,0:T(8,128)S(1)}, f32[15,128]{1,0:T(8,128)S(1)}, u32[]{:S(2)}, u32[]{:S(2)}) collective-permute-start(f32[15,128]{1,0:T(8,128)S(1)} %fusion.17), channel_id=1, source_target_pairs={{0,8},{4,12},{8,0},{12,4},{16,24},{20,28},{24,16},{28,20},{1,9},{5... | collective-permute-start | bytes 23048 | tf_op jit(solution)/shard_map/ppermute | solution.py:890
  283.0 3.7 %collective-permute-start.21 = (f32[15,128]{1,0:T(8,128)S(1)}, f32[15,128]{1,0:T(8,128)S(1)}, u32[]{:S(2)}, u32[]{:S(2)}) collective-permute-start(f32[15,128]{1,0:T(8,128)S(1)} %add.83), channel_id=1, source_target_pairs={{0,2},{1,3},{2,0},{3,1},{4,6},{5,7},{6,4},{7,5},{8,10},{9,11},{10,... | collective-permute-start | bytes 23048 | tf_op jit(solution)/shard_map/ppermute | solution.py:875
  286.8 4.5 %collective-permute-start.22 = (f32[15,128]{1,0:T(8,128)S(1)}, f32[15,128]{1,0:T(8,128)S(1)}, u32[]{:S(2)}, u32[]{:S(2)}) collective-permute-start(f32[15,128]{1,0:T(8,128)S(1)} %add.84), channel_id=1, source_target_pairs={{0,16},{4,20},{8,24},{12,28},{16,0},{20,4},{24,8},{28,12},{1,17},{... | collective-permute-start | bytes 23048 | tf_op jit(solution)/shard_map/ppermute | solution.py:890
  292.1 4.1 %collective-permute-start.20 = (bf16[96,192]{1,0:T(8,128)(2,1)S(1)}, bf16[96,192]{1,0:T(8,128)(2,1)S(1)}, u32[]{:S(2)}, u32[]{:S(2)}) collective-permute-start(bf16[96,192]{1,0:T(8,128)(2,1)S(1)} %slice.88), channel_id=1, source_target_pairs={{0,2},{1,3},{2,0},{3,1},{4,6},{5,7},{6,4},{7,5},{8,10},{9,11},{10,... | collective-permute-start | bytes 110600 | tf_op jit(solution)/shard_map/ppermute | solution.py:875
  (32 other events, 186.6 us)
Sparse Core Ops, SparseCore 0:
  11.2 50.2 all-gather.2
  63.0 41.0 all-gather.4
  155.0 71.0 reduce-scatter.2
  242.7 46.5 reduce-scatter.4
where the time goes:
time: 313 us; the launch traced here: 307 us
  Pallas kernels  124 us (40%)
  waiting for transfers between devices  56.8 us (18%)
  starting transfers between devices  35.6 us (11%)
  blocking collectives  33.1 us (11%)
  local copies, waits for them, and re-layouts  31.3 us (10%)
  between operations  14.4 us (5%)
  other arithmetic  9.23 us (3%)
    ppermute x20, waiting for transfers between devices, swap(): lax.ppermute(values, 'tensor', [(i, i ^ bit) for i in range(tensor_size)])  40.6 us
    pallas_call x1, Pallas kernels, attend_back(): pl.pallas_call(functools.partial(attend_back_kernel, heads, rows_dev), ou...  38.9 us
    all_to_all x1, blocking collectives, deal_out(): return lax.all_to_all(values, 'dp', split_axis=0, concat_axis=0, tiled=True)  33.1 us
    pallas_call x1, Pallas kernels, ffn(): pl.pallas_call(functools.partial(ffn_kernel, ring), grid=(steps + 2 * (hi...  25.2 us
    all_to_all x3, starting transfers between devices, deal_out(): return lax.all_to_all(values, 'dp', split_axis=0, concat_axis=0, tiled=True)  21.1 us
    ppermute x3, waiting for transfers between devices, total_sum(): lax.ppermute(values, 'dp', [(i, i ^ step) for i in range(dp_size)])  16.2 us
    pallas_call x1, Pallas kernels, attend_far(): pl.pallas_call(functools.partial(attend_far_kernel, heads, rows_dev), out...  14.2 us
    unnamed x73, local copies, waits for them, and re-layouts  13.3 us
  transfers between devices with their start and end apart: 30, of which 15 were waited for; matrix products, arithmetic and copies ran while one was open for 10% of the time, Pallas kernels for 31%

commit v1 on v0

--- a/solution.py
+++ b/solution.py
@@ -62,7 +62,8 @@
     hidden = inner_ref.shape[1]
     first = [query_ref[...], key_ref[...], value_ref[...], outer_ref[...], proj_ref[...]]
     first_ref[...] = jnp.concatenate(first, axis=1).astype(BF16)
-    rest_ref[...] = inner_ref[...].astype(BF16)
+    rest_ref[:, :hidden] = inner_ref[...].astype(BF16)
+    rest_ref[:, hidden:] = proj_ref[...].astype(BF16)
 
 
 def pack_weights(inner, query, key, value, proj, outer):
@@ -72,7 +73,7 @@
         pack_kernel,
         out_shape=(
             jax.ShapeDtypeStruct((rows, 4 * cols + hidden), BF16),
-            jax.ShapeDtypeStruct((rows, hidden), BF16),
+            jax.ShapeDtypeStruct((rows, hidden + cols), BF16),
         ),
         in_specs=[VMEM] * 6,
         out_specs=(VMEM, VMEM),
@@ -345,16 +346,13 @@
     return values
 
 
-def grad_rows_to(own_ref, send_ref, rows_dev, grad_ref, w_ref):
-    slots = grad_ref.shape[1] // rows_dev
-    for i in range(slots // 2):
-        slot = (slots - 2 * (i + 1)) % slots
-        for at, out_ref in ((slot + 1, send_ref), (slot, own_ref)):
-            for begin in range(0, rows_dev, TILE):
-                cols = slice(at * rows_dev + begin, at * rows_dev + begin + TILE)
-                part = contract(grad_ref[:, cols], 0, w_ref[...], 1)
-                to = slice(i * rows_dev + begin, i * rows_dev + begin + TILE)
-                out_ref[to, :] = part.astype(out_ref.dtype)
+def grad_rows_to(own_ref, send_ref, first_slot, grad_ref, w_ref):
+    rows_dev = own_ref.shape[0]
+    for slot, out_ref in ((first_slot + 1, send_ref), (first_slot, own_ref)):
+        for begin in range(0, rows_dev, TILE):
+            at = slot * rows_dev + begin
+            part = contract(grad_ref[:, at : at + TILE], 0, w_ref[...], 1)
+            out_ref[begin : begin + TILE, :] = part.astype(out_ref.dtype)
 
 
 def attend_back_kernel(
@@ -373,8 +371,10 @@
     w_ref,
     out_ref,
     diag_ref,
-    own_ref,
-    send_ref,
+    far_own_ref,
+    far_send_ref,
+    near_own_ref,
+    near_send_ref,
     lse_ref,
     inner_ref,
     grad_ref,
@@ -452,7 +452,8 @@
     for h in range(heads):
         out_ref[k_of[h], :] = key_acc[h].astype(BF16).T
         out_ref[v_of[h], :] = value_acc[h].astype(BF16).T
-    grad_rows_to(own_ref, send_ref, rows_dev, out_ref, w_ref)
+    grad_rows_to(far_own_ref, far_send_ref, rows // rows_dev // 2, out_ref, w_ref)
+    grad_rows_to(near_own_ref, near_send_ref, 0, out_ref, w_ref)
     for i in range(heads * KINDS):
         if i % KINDS in (0, KINDS - 1):
             total = jnp.sum(table_ref[i], axis=0, keepdims=True)
@@ -471,11 +472,13 @@
         out_shape=(
             jax.ShapeDtypeStruct((3 * cols, rows), BF16),
             jax.ShapeDtypeStruct((heads * KINDS, 2 * TILE), F32),
-            jax.ShapeDtypeStruct((rows // 2, width), F32),
-            jax.ShapeDtypeStruct((rows // 2, width), BF16),
+            jax.ShapeDtypeStruct((rows_dev, width), F32),
+            jax.ShapeDtypeStruct((rows_dev, width), BF16),
+            jax.ShapeDtypeStruct((rows_dev, width), F32),
+            jax.ShapeDtypeStruct((rows_dev, width), BF16),
         ),
         in_specs=[SMEM] + [VMEM] * 10,
-        out_specs=(VMEM,) * 4,
+        out_specs=(VMEM,) * 6,
         scratch_shapes=[
             pltpu.VMEM((heads, rows), F32),
             pltpu.VMEM((heads, rows), F32),
@@ -500,9 +503,14 @@
 
 
 def join_kernel(rows_ref, near_ref, far_ref, gain_ref, middle_ref, low_ref):
-    middle = rows_ref[...].astype(F32) + near_ref[...] + far_ref[...].astype(F32)
-    middle_ref[...] = middle
-    low_ref[...] = (scaled_rows(middle) * gain_ref[...]).astype(BF16)
+    for rs in row_blocks(rows_ref.shape[0]):
+        middle = rows_ref[rs, :].astype(F32) + near_ref[rs, :] + far_ref[rs, :].astype(F32)
+        middle_ref[rs, :] = middle
+        low_ref[rs, :] = (scaled_rows(middle) * gain_ref[...]).astype(BF16)
+
+
+def row_blocks(rows):
+    return [slice(begin, begin + TILE // 4) for begin in range(0, rows, TILE // 4)]
 
 
 def norm_back_rows(values, upstream, gain):
@@ -514,30 +522,29 @@
 
 
 def middle_back_kernel(middle_ref, near_ref, far_ref, grads_ref, gain_ref, wide_ref, low_ref):
-    upstream = near_ref[...] + far_ref[...].astype(F32)
-    back = norm_back_rows(middle_ref[...], upstream, gain_ref[...])
-    wide = grads_ref[...].astype(F32) + back
-    wide_ref[...] = wide
-    low_ref[...] = wide.astype(BF16)
+    for rs in row_blocks(middle_ref.shape[0]):
+        upstream = near_ref[rs, :] + far_ref[rs, :].astype(F32)
+        back = norm_back_rows(middle_ref[rs, :], upstream, gain_ref[...])
+        wide = grads_ref[rs, :].astype(F32) + back
+        wide_ref[rs, :] = wide
+        low_ref[rs, :] = wide.astype(BF16)
 
 
 def rows_back_kernel(rows_ref, near_ref, core_ref, far_ref, wide_ref, gain_ref, low_ref):
-    upstream = near_ref[...] + core_ref[...].astype(F32) + far_ref[...].astype(F32)
-    back = norm_back_rows(rows_ref[...].astype(F32), upstream, gain_ref[...])
-    low_ref[...] = (wide_ref[...] + back).astype(BF16)
+    for rs in row_blocks(rows_ref.shape[0]):
+        upstream = near_ref[rs, :] + core_ref[rs, :].astype(F32) + far_ref[rs, :].astype(F32)
+        back = norm_back_rows(rows_ref[rs, :].astype(F32), upstream, gain_ref[...])
+        low_ref[rs, :] = (wide_ref[rs, :] + back).astype(BF16)
 
 
 def by_rows(kernel, name, gain, *operands, out, cost=SHORT):
-    rows, width = operands[0].shape
-    spec = pl.BlockSpec((TILE, width), lambda i: (i, 0))
-    once = pl.BlockSpec((1, width), lambda i: (0, 0))
+    shape = operands[0].shape
     return pl.pallas_call(
         kernel,
-        grid=(rows // TILE,),
-        out_shape=tuple(jax.ShapeDtypeStruct((rows, width), kind) for kind in out),
-        in_specs=[spec] * len(operands) + [once],
-        out_specs=(spec,) * len(out),
-        compiler_params=pltpu.CompilerParams(vmem_limit_bytes=58 << 20),
+        out_shape=tuple(jax.ShapeDtypeStruct(shape, kind) for kind in out),
+        in_specs=[VMEM] * (len(operands) + 1),
+        out_specs=(VMEM,) * len(out),
+        compiler_params=pltpu.CompilerParams(vmem_limit_bytes=16 << 20),
         cost_estimate=cost,
         name=name,
     )(*operands, gain[None])
@@ -564,6 +571,7 @@
         ),
         in_specs=[VMEM] * 4,
         out_specs=(VMEM, VMEM),
+        compiler_params=pltpu.CompilerParams(vmem_limit_bytes=16 << 20),
         cost_estimate=SHORT,
         name="out_proj",
     )(own, other, w_own, w_other)
@@ -584,6 +592,7 @@
         out_shape=(shape, shape),
         in_specs=[VMEM] * 4,
         out_specs=(VMEM, VMEM),
+        compiler_params=pltpu.CompilerParams(vmem_limit_bytes=16 << 20),
         cost_estimate=SHORT,
         name="mixed_grads",
     )(*middle, w_own, w_other)
@@ -702,9 +711,6 @@
     rows, hidden = 2 * half, 2 * part
     block = 2 * TILE
     steps = hidden // TILE
-    whole = pl.BlockSpec((half, width), lambda j: (0, 0), pipeline_mode=pl.Buffered(1))
-    weight = pl.BlockSpec((width, part), lambda j: (0, 0), pipeline_mode=pl.Buffered(1))
-    once = pl.BlockSpec((half, width), lambda j: (0, 0))
     return pl.pallas_call(
         functools.partial(ffn_kernel, ring),
         grid=(steps + 2 * (hidden // block),),
@@ -716,12 +722,12 @@
             jax.ShapeDtypeStruct((width, 2 * hidden), BF16),
             jax.ShapeDtypeStruct((1, width), F32),
         ),
-        in_specs=[whole] * 4 + [weight] * 4,
+        in_specs=[VMEM] * 8,
         out_specs=(
-            once,
-            once,
-            once,
-            once,
+            VMEM,
+            VMEM,
+            VMEM,
+            VMEM,
             pl.BlockSpec((width, block), lambda j: (0, jnp.maximum(j - steps, 0))),
             pl.BlockSpec((1, width), lambda j: (0, 0)),
         ),
@@ -733,7 +739,7 @@
             pltpu.VMEM((width, rows), BF16),
             pltpu.VMEM((width, 128), F32),
         ],
-        compiler_params=pltpu.CompilerParams(vmem_limit_bytes=52 << 20),
+        compiler_params=pltpu.CompilerParams(vmem_limit_bytes=44 << 20),
         cost_estimate=SHORT,
         name="ffn",
     )(*normed, *grads, *inners, *outers)
@@ -794,7 +800,7 @@
         ),
         in_specs=[VMEM] * 7,
         out_specs=(VMEM, VMEM),
-        compiler_params=pltpu.CompilerParams(vmem_limit_bytes=58 << 20),
+        compiler_params=pltpu.CompilerParams(vmem_limit_bytes=24 << 20),
         cost_estimate=SHORT,
         name="qkv_grads",
     )(grad_qkv, *slots, weights, proj)
@@ -880,16 +886,12 @@
     def pick(values, order):
         return values.at[order].get(mode="promise_in_bounds", unique_indices=True)
 
-    def total_sum(values, passing):
-        values = values + swap(values, 1)
+    def sum_groups(values):
         step = 1
         while step < dp_size:
-            if 2 * step >= dp_size:
-                values, passing = after(values, passing)
-                values = values + swap(values, 2)
             values = values + lax.ppermute(values, "dp", [(i, i ^ step) for i in range(dp_size)])
             step *= 2
-        return values, passing
+        return values
 
     ring = ring_order(dp_size)
     both = ("dp", "tensor")
@@ -904,7 +906,7 @@
             ringed(values, ring), both, scatter_dimension=0, tiled=True, axis_index_groups=ring_groups
         )
 
-    own_front, own_inner = pack_weights(
+    own_front, own_rest = pack_weights(
         w_inner, w_query, w_key, w_value, w_proj.T, w_outer.T
     )
     own_front, tokens = after(own_front, tokens)
@@ -913,6 +915,15 @@
         own_front, ((0, ends[0], False), (ends[0], ends[1], False), (ends[1], ends[2], True))
     )
     low_rows = deal_out(pick(tokens, deal))
+    other_rest, low_rows = after(swap(own_rest, 2), low_rows)
+    inner_own, inner_other, proj_other = gather(
+        jnp.concatenate([own_rest[:, :hidden], other_rest], axis=1),
+        (
+            (0, hidden, False),
+            (hidden, 2 * hidden, False),
+            (2 * hidden, 2 * hidden + cols, True),
+        ),
+    )
     onehot_buckets = (
         buckets[:, None] == jnp.arange(rel_table.shape[0], dtype=jnp.int32)[None, :]
     ).astype(F32)
@@ -925,26 +936,21 @@
         jnp.zeros((rows_dev,), jnp.int32).at[deal].set(jnp.arange(rows_dev, dtype=jnp.int32))
     )
     slot0 = (scaled_rows(low_rows.astype(F32)) * gain_attn).astype(BF16)
-    own_inner, slot0 = after(own_inner, slot0)
-    inner_own, inner_other = gather(
-        jnp.concatenate([own_inner, swap(own_inner, 2)], axis=1),
-        ((0, hidden, False), (hidden, 2 * hidden, False)),
-    )
     slot2 = swap(slot0, 2)
     slot1 = swap(slot0, 1)
-    slot2, front, base, info = after(slot2, front, base, info)
+    slot2, front, base, info, inverse_order = after(slot2, front, base, info, inverse_order)
     slot3 = swap(slot2, 1)
     slots = (slot0, slot1, slot2, slot3)
-    proj_other, outer_other = swap(proj_own, 2), swap(outer_own, 2)
+    outer_other = swap(outer_own, 2)
 
     low_grads = deal_out(pick(cotangent, deal))
 
     mixed_far, wide_far, lse_far, qkv, keys = attend_far(info, base, front, slots)
     mixed_other = swap(mixed_far, 2)
-    late_qkv, outer_other, low_grads = after(qkv, outer_other, low_grads)
+    late_qkv, low_grads = after(qkv, low_grads)
     mixed_own, wide_own, lse_own = attend_near(info, base, late_qkv, keys, rows_dev)
+    mixed_own, outer_other, inner_own = after(mixed_own, outer_other, inner_own)
     near, to_core = out_proj(mixed_own, mixed_other, proj_own, proj_other)
-    near, inner_own, inner_other = after(near, inner_own, inner_other)
     middle, low_two = by_rows(
         join_kernel, "join", gain_ffn, low_rows, near, swap(to_core, 1), out=(F32, BF16)
     )
@@ -976,7 +982,7 @@
     back_rows = deal_out(result_rows)
 
     grad_far, proj_pack = after(swap(to_other, 2), proj_pack)
-    grad_qkv, diagonals, rows_own, rows_send = attend_back(
+    grad_qkv, diagonals, far_own, far_send, near_own, near_send = attend_back(
         info,
         base,
         qkv,
@@ -987,32 +993,18 @@
         front,
         rows_dev,
     )
-    rows_send, back_rows = after(rows_send, back_rows)
-    rows_core = swap(rows_send, 1)
-    grad_later = (rows_own[:rows_dev] + rows_core[:rows_dev].astype(F32)).astype(BF16)
+    far_send, back_rows = after(far_send, back_rows)
+    grad_later = (far_own + swap(far_send, 1).astype(F32)).astype(BF16)
+    grad_later, near_send = after(grad_later, near_send)
     later_qkv, grad_later = after(grad_qkv, grad_later)
     low_qkv_w, gain_one = qkv_grads(ring, later_qkv, slots, front, proj_pack)
     low_qkv_w, shard_pack = after(low_qkv_w, shard_pack)
+    low_qkv_w, diagonals = after(low_qkv_w, diagonals)
     shard_qkv = scatter_sum(low_qkv_w)
-    out_rows = pick(back_rows, inverse_order)
-    rows_near, out_rows = after(rows_core[rows_dev:], out_rows)
-    (low_grad_rows,) = by_rows(
-        rows_back_kernel,
-        "rows_back",
-        gain_attn,
-        low_rows,
-        rows_own[rows_dev:],
-        rows_near,
-        swap(grad_later, 2),
-        grad_middle,
-        out=(BF16,),
-        cost=LONG,
-    )
     taken = swap(
         jnp.concatenate([shard_pack[:, hidden : 2 * hidden], shard_pack[:, 3 * hidden :]], axis=1),
         2,
     )
-
     offset_count = 2 * MAXDIST + 1
     onehot_line = (
         line_index()[:, None] == jnp.arange(offset_count, dtype=jnp.int32)[None, :]
@@ -1025,10 +1017,32 @@
         jnp.zeros(rel_table.shape, F32), table_heads, me * heads, 1
     )
     terms = [gain_one[0] / gain_attn, gain_two[0] / gain_ffn, table_full.reshape(-1)]
-    small, taken = total_sum(jnp.concatenate(terms).reshape(-1, 128), taken)
+    small = sum_groups(jnp.concatenate(terms).reshape(-1, 128))
+    grad_two_rows, small = after(swap(grad_later, 2), small)
+    small = small + swap(small, 1)
+    small, taken = after(small, taken)
+    small = small + swap(small, 2)
+
+    near_core = swap(near_send, 1)
+    (low_grad_rows,) = by_rows(
+        rows_back_kernel,
+        "rows_back",
+        gain_attn,
+        low_rows,
+        near_own,
+        near_core,
+        grad_two_rows,
+        grad_middle,
+        out=(BF16,),
+        cost=pl.CostEstimate(flops=(3<<33)//2, bytes_accessed=(1<<26)//2, transcendentals=(1<<23)//2),
+    )
+
+    shard_far = swap(shard_qkv[:, 4 * cols :], 2)
+    weight_shards = finish(shard_pack, taken, shard_qkv, shard_far, hidden)
+    out_rows = pick(back_rows, inverse_order)
     small = small.reshape(-1)
     back_grads = deal_out(low_grad_rows)
-    weight_shards = finish(shard_pack, taken, shard_qkv, swap(shard_qkv[:, 4 * cols :], 2), hidden)
+    back_grads, out_rows, *weight_shards = after(back_grads, out_rows, *weight_shards)
     return (
         out_rows,
         pick(back_grads, inverse_order),

time: 313 us -> 278 us (0.89)
  the two profiles are of different devices: /device:TPU:12 before, /device:TPU:0 now
where the time goes in v1:
time: 278 us; the launch traced here: 274 us
  Pallas kernels  113 us (41%)
  waiting for transfers between devices  70.9 us (26%)
  local copies, waits for them, and re-layouts  35.6 us (13%)
  starting transfers between devices  30.7 us (11%)
  between operations  14.5 us (5%)
  other arithmetic  6.74 us (2%)
    pallas_call x1, Pallas kernels, attend_back(): pl.pallas_call(functools.partial(attend_back_kernel, heads, rows_dev), ou...  40.8 us
    ppermute x20, waiting for transfers between devices, swap(): lax.ppermute(values, 'tensor', [(i, i ^ bit) for i in range(tensor_size)])  29.2 us
    all_to_all x4, waiting for transfers between devices, deal_out(): return lax.all_to_all(values, 'dp', split_axis=0, concat_axis=0, tiled=True)  24 us
    pallas_call x1, Pallas kernels, ffn(): pl.pallas_call(functools.partial(ffn_kernel, ring), grid=(steps + 2 * (hi...  23.1 us
    all_to_all x4, starting transfers between devices, deal_out(): return lax.all_to_all(values, 'dp', split_axis=0, concat_axis=0, tiled=True)  19.3 us
    unnamed x87, local copies, waits for them, and re-layouts  18.9 us
    pallas_call x1, Pallas kernels, attend_far(): pl.pallas_call(functools.partial(attend_far_kernel, heads, rows_dev), out...  15.2 us
    ppermute x3, waiting for transfers between devices, sum_groups(): lax.ppermute(values, 'dp', [(i, i ^ step) for i in range(dp_size)])  11.8 us
  transfers between devices with their start and end apart: 31, of which 19 were waited for; matrix products, arithmetic and copies ran while one was open for 9% of the time, Pallas kernels for 32%

profile of v1, /device:TPU:0, one launch (start us, length us, event | category | flops | bytes accessed | tf_op | source)
XLA Modules:
  0.0 273.6 jit_solution(2333644737766243153)
XLA Ops:
  8.9 2.1 pack_weights.1
  11.7 2.7 gather_fusion
  14.5 7.4 %all-to-all-start = ((bf16[8,64,768]{2,1,0:T(8,128)(2,1)}), bf16[8,64,768]{2,1,0:T(8,128)(2,1)S(1)}, u32[]{:S(2)}, u32[]{:S(2)}) async-start(bf16[8,64,768]{2,1,0:T(8,128)(2,1)} %bitcast.2), calls=%async_computation | async-start | bytes 1572864 | tf_op jit(solution)/shard_map/all_to_all | solution.py:884
  23.5 4.8 %collective-permute-done = bf16[96,960]{1,0:T(8,128)(2,1)S(1)} collective-permute-done((bf16[96,960]{1,0:T(8,128)(2,1)S(1)}, bf16[96,960]{1,0:T(8,128)(2,1)S(1)}, u32[]{:S(2)}, u32[]{:S(2)}) %collective-permute-start) | collective-permute-done | bytes 184352 | tf_op jit(solution)/shard_map/ppermute | solution.py:881
  28.3 22.8 %all-to-all-done = bf16[8,64,768]{2,1,0:T(8,128)(2,1)S(1)} async-done(((bf16[8,64,768]{2,1,0:T(8,128)(2,1)}), bf16[8,64,768]{2,1,0:T(8,128)(2,1)S(1)}, u32[]{:S(2)}, u32[]{:S(2)}) %all-to-all-start) | async-done | bytes 786464 | tf_op jit(solution)/shard_map/all_to_all | solution.py:884
  54.1 2.7 gather_fusion.1
  56.8 3.7 %all-to-all-start.1 = ((bf16[8,64,768]{2,1,0:T(8,128)(2,1)}), bf16[8,64,768]{2,1,0:T(8,128)(2,1)S(1)}, u32[]{:S(2)}, u32[]{:S(2)}) async-start(bf16[8,64,768]{2,1,0:T(8,128)(2,1)} %bitcast.37), calls=%async_computation.1 | async-start | bytes 1572864 | tf_op jit(solution)/shard_map/all_to_all | solution.py:884
  63.2 2.6 scatter_custom_fusion
  66.5 3.6 %unring.2 = (bf16[768,576]{1,0:T(8,128)(2,1)}, bf16[768,768]{1,0:T(8,128)(2,1)}, bf16[192,768]{1,0:T(8,128)(2,1)}) custom-call(bf16[768,1536]{1,0:T(8,128)(2,1)} %all-gather.3.cloned.1.call-done.found_ref), custom_call_target="tpu_custom_call" | custom-call | flops 1048576 | bytes 65536 | tf_op jit(solution)/shard_map/unring/pallas_call | solution.py:109
  73.7 15.2 %attend_far.1 = (bf16[192,1024]{1,0:T(8,128)(2,1)}, f32[192,1024]{1,0:T(8,128)}, f32[3,1024]{1,0:T(4,128)}, bf16[576,2048]{1,0:T(8,128)(2,1)}, bf16[3,2048,128]{2,1,0:T(8,128)(2,1)}) custom-call(s32[1,3]{1,0:T(1,128)} %pad_add_fusion.info_ref, f32[15,512]{1,0:T(8,128)} %reshape.102.base_ref, bf16[768,576]{1,0:T(8,128)(2,1)} %get-tuple-element.105.w_ref, ...), custom_call_target="tpu_custom_call" | custom-call | flops 1048576 | bytes 65536 | tf_op jit(solution)/shard_map/attend_far/pallas_call | solution.py:310
  89.5 11.3 %attend_near.1 = (bf16[192,1024]{1,0:T(8,128)(2,1)}, f32[192,1024]{1,0:T(8,128)}, f32[3,1024]{1,0:T(4,128)}) custom-call(s32[1,3]{1,0:T(1,128)} %pad_add_fusion.info_ref, f32[15,512]{1,0:T(8,128)} %reshape.102.base_ref, bf16[576,2048]{1,0:T(8,128)(2,1)} %get-tuple-element.109.qkv_ref, bf16[3,2048,128]{2,1,0:T(8,128)(2,1)} %get-tuple-element.108.key_ref), custom_call_target="tpu_custom_call" | custom-call | flops 1048576 | bytes 65536 | tf_op jit(solution)/shard_map/attend_near/pallas_call | solution.py:328
  100.8 5.2 %all-gather.5.cloned.1.call-done.found_ref = bf16[768,1728]{1,0:T(8,128)(2,1)} async-done(((bf16[96,1728]{1,0:T(8,128)(2,1)}), bf16[768,1728]{1,0:T(8,128)(2,1)}) %all-gather.5.cloned.1.call-update) | async-done | bytes 2654224 | tf_op jit(solution)/shard_map/all_gather | solution.py:901
  106.0 3.4 %unring.3 = (bf16[768,768]{1,0:T(8,128)(2,1)}, bf16[768,768]{1,0:T(8,128)(2,1)}, bf16[192,768]{1,0:T(8,128)(2,1)}) custom-call(bf16[768,1728]{1,0:T(8,128)(2,1)} %all-gather.5.cloned.1.call-done.found_ref), custom_call_target="tpu_custom_call" | custom-call | flops 1048576 | bytes 65536 | tf_op jit(solution)/shard_map/unring/pallas_call | solution.py:109
  115.7 2.1 collective-permute-done.7.normed1
  117.8 23.1 %ffn.1 = (f32[512,768]{1,0:T(8,128)}, bf16[512,768]{1,0:T(8,128)(2,1)S(1)}, f32[512,768]{1,0:T(8,128)}, bf16[512,768]{1,0:T(8,128)(2,1)S(1)}, bf16[768,3072]{1,0:T(8,128)(2,1)}, /*index=5*/f32[1,768]{1,0:T(1,128)S(1)}) custom-call(bf16[512,768]{1,0:T(8,128)(2,1)S(1)} %get-tuple-element.125.normed0, bf16[512,768]{1,0:T(8,128)(2,1)S(1)} %collective-permute-done.7.normed1, ...), custom_call_target="tpu_custom_call" | custom-call | flops 1048576 | bytes 65536 | tf_op jit(solution)/shard_map/ffn/pallas_call | solution.py:714
  142.1 2.4 collective-permute-done.9.far_ref
  156.9 4.0 %all-to-all-start.2 = ((bf16[8,64,768]{2,1,0:T(8,128)(2,1)}), bf16[8,64,768]{2,1,0:T(8,128)(2,1)S(1)}, u32[]{:S(2)}, u32[]{:S(2)}) async-start(bf16[8,64,768]{2,1,0:T(8,128)(2,1)} %bitcast.8), calls=%async_computation.2 | async-start | bytes 1572864 | tf_op jit(solution)/shard_map/all_to_all | solution.py:884
  160.9 4.6 %collective-permute-done.11.grad1_ref = bf16[192,1024]{1,0:T(8,128)(2,1)} collective-permute-done((bf16[192,1024]{1,0:T(8,128)(2,1)}, bf16[192,1024]{1,0:T(8,128)(2,1)}, u32[]{:S(2)}, u32[]{:S(2)}) %collective-permute-start.11) | collective-permute-done | bytes 393248 | tf_op jit(solution)/shard_map/ppermute | solution.py:881
  165.5 40.8 %attend_back.1 = (bf16[576,2048]{1,0:T(8,128)(2,1)}, f32[15,512]{1,0:T(8,128)}, f32[512,768]{1,0:T(8,128)}, bf16[512,768]{1,0:T(8,128)(2,1)}, f32[512,768]{1,0:T(8,128)}, /*index=5*/bf16[512,768]{1,0:T(8,128)(2,1)}) custom-call(s32[1,3]{1,0:T(1,128)} %pad_add_fusion.info_ref, f32[15,512]{1,0:T(8,128)} %reshape.102.base_ref, ...), custom_call_target="tpu_custom_call" | custom-call | flops 25769803776 | bytes 67108864 | tf_op jit(solution)/shard_map/attend_back/pallas_call | solution.py:470
  206.6 2.5 collective-permute-done.13
  209.0 2.8 %add_convert_fusion = bf16[512,768]{1,0:T(8,128)(2,1)} fusion(f32[512,768]{1,0:T(8,128)} %get-tuple-element.142, bf16[512,768]{1,0:T(8,128)(2,1)} %collective-permute-done.13), kind=kLoop, calls=%fused_computation.12 | loop fusion | flops 1179648 | bytes 3145728 | tf_op jit(solution)/shard_map/convert_element_type | solution.py:997
  214.4 3.3 %qkv_grads.1 = (bf16[768,960]{1,0:T(8,128)(2,1)S(1)}, f32[1,768]{1,0:T(1,128)S(1)}) custom-call(bf16[576,2048]{1,0:T(8,128)(2,1)S(1)} %copy-done.12, bf16[512,768]{1,0:T(8,128)(2,1)S(1)} %copy-done.3, bf16[512,768]{1,0:T(8,128)(2,1)} %collective-permute-done.2.slot1_ref, bf16[512,768]{1,0:T(8,128)(2,1)S(1)} %copy-done.9, bf16[512,768]{1,0:T(8,128)(2,1)S(1)} %copy-done.11, ...), custom_call_target="tpu_custom_call" | custom-call | flops 1048576 | bytes 65536 | tf_op jit(solution)/shard_map/qkv_grads/pallas_call | solution.py:795
  221.1 3.6 %collective-permute-done.16 = f32[15,128]{1,0:T(8,128)S(1)} collective-permute-done((f32[15,128]{1,0:T(8,128)S(1)}, f32[15,128]{1,0:T(8,128)S(1)}, u32[]{:S(2)}, u32[]{:S(2)}) %collective-permute-start.16) | collective-permute-done | bytes 7712 | tf_op jit(solution)/shard_map/ppermute | solution.py:892
  224.8 3.6 %collective-permute-done.17 = f32[15,128]{1,0:T(8,128)S(1)} collective-permute-done((f32[15,128]{1,0:T(8,128)S(1)}, f32[15,128]{1,0:T(8,128)S(1)}, u32[]{:S(2)}, u32[]{:S(2)}) %collective-permute-start.17) | collective-permute-done | bytes 7712 | tf_op jit(solution)/shard_map/ppermute | solution.py:892
  228.5 4.5 %collective-permute-done.18 = f32[15,128]{1,0:T(8,128)S(1)} collective-permute-done((f32[15,128]{1,0:T(8,128)S(1)}, f32[15,128]{1,0:T(8,128)S(1)}, u32[]{:S(2)}, u32[]{:S(2)}) %collective-permute-start.18) | collective-permute-done | bytes 7712 | tf_op jit(solution)/shard_map/ppermute | solution.py:892
  235.9 2.9 %rows_back.1 = bf16[512,768]{1,0:T(8,128)(2,1)} custom-call(bf16[512,768]{1,0:T(8,128)(2,1)S(1)} %bitcast.31, f32[512,768]{1,0:T(8,128)S(1)} %copy-done.26, bf16[512,768]{1,0:T(8,128)(2,1)S(1)} %collective-permute-done.14.core_ref, bf16[512,768]{1,0:T(8,128)(2,1)} %collective-permute-done.15.far_ref, f32[512,768]{1,0:T(8,128)S(1)} %copy-done.23, ...), custom_call_target="tpu_custom_call" | custom-call | flops 12884901888 | bytes 33554432 | tf_op jit(solution)/shard_map/rows_back/pallas_call | solution.py:542
  238.7 4.3 %all-to-all-start.3 = ((bf16[8,64,768]{2,1,0:T(8,128)(2,1)}), bf16[8,64,768]{2,1,0:T(8,128)(2,1)S(1)}, u32[]{:S(2)}, u32[]{:S(2)}) async-start(bf16[8,64,768]{2,1,0:T(8,128)(2,1)} %bitcast.11), calls=%async_computation.4 | async-start | bytes 1572864 | tf_op jit(solution)/shard_map/all_to_all | solution.py:884
  245.4 4.8 %collective-permute-done.20.taken_ref = bf16[96,1536]{1,0:T(8,128)(2,1)S(1)} collective-permute-done((bf16[96,1536]{1,0:T(8,128)(2,1)S(1)}, bf16[96,1536]{1,0:T(8,128)(2,1)S(1)}, u32[]{:S(2)}, u32[]{:S(2)}) %collective-permute-start.20) | collective-permute-done | bytes 294944 | tf_op jit(solution)/shard_map/ppermute | solution.py:881
  251.1 2.7 gather_fusion.2
  257.4 2.1 collective-permute-done.21.far_ref
  260.1 2.2 finish.1
  263.4 2.7 gather_fusion.3
  (196 shorter events, 52.5 us)
Async XLA Ops:
  7.2 59.3 %all-gather.3.cloned.1.call-start = ((), (), s32[]{:S(2)}) async-start(), calls=%async_computation.6 | async-start | bytes 2654208 | tf_op jit(solution)/shard_map/all_gather | solution.py:901
  14.5 36.7 %all-to-all-start = ((bf16[8,64,768]{2,1,0:T(8,128)(2,1)}), bf16[8,64,768]{2,1,0:T(8,128)(2,1)S(1)}, u32[]{:S(2)}, u32[]{:S(2)}) async-start(bf16[8,64,768]{2,1,0:T(8,128)(2,1)} %bitcast.2), calls=%async_computation | async-start | bytes 1572864 | tf_op jit(solution)/shard_map/all_to_all | solution.py:884
  21.9 84.2 %all-gather.5.cloned.1.call-start = ((), (), s32[]{:S(2)}) async-start(), calls=%async_computation.7 | async-start | bytes 3096576 | tf_op jit(solution)/shard_map/all_gather | solution.py:901
  21.9 6.4 %collective-permute-start = (bf16[96,960]{1,0:T(8,128)(2,1)S(1)}, bf16[96,960]{1,0:T(8,128)(2,1)S(1)}, u32[]{:S(2)}, u32[]{:S(2)}) collective-permute-start(bf16[96,960]{1,0:T(8,128)(2,1)S(1)} %copy-done.33), channel_id=1, source_target_pairs={{0,2},{1,3},{2,0},{3,1},{4,6},{5,7},{6,4},{7,5},{8,10},{9,11},{10,... | collective-permute-start | bytes 552968 | tf_op jit(solution)/shard_map/ppermute | solution.py:881
  52.5 18.0 %collective-permute-start.1 = (bf16[512,768]{1,0:T(8,128)(2,1)S(1)}, bf16[512,768]{1,0:T(8,128)(2,1)S(1)}, u32[]{:S(2)}, u32[]{:S(2)}) collective-permute-start(bf16[512,768]{1,0:T(8,128)(2,1)S(1)} %fusion.3.slot0_ref), channel_id=1, source_target_pairs={{0,2},{1,3},{2,0},{3,1},{4,6},{5,7},{6,4},{7,5},{8,10},{9,11},{10,... | collective-permute-start | bytes 2359304 | tf_op jit(solution)/shard_map/ppermute | solution.py:881
  56.8 32.7 %all-to-all-start.1 = ((bf16[8,64,768]{2,1,0:T(8,128)(2,1)}), bf16[8,64,768]{2,1,0:T(8,128)(2,1)S(1)}, u32[]{:S(2)}, u32[]{:S(2)}) async-start(bf16[8,64,768]{2,1,0:T(8,128)(2,1)} %bitcast.37), calls=%async_computation.1 | async-start | bytes 1572864 | tf_op jit(solution)/shard_map/all_to_all | solution.py:884
  60.5 158.5 %reduce-scatter.3.cloned.1.call-start = ((), (), s32[]{:S(2)}) async-start(), calls=%async_computation.8 | async-start | bytes 5308416 | tf_op jit(solution)/shard_map/reduce_scatter | solution.py:905
  66.5 5.6 %collective-permute-start.2 = (bf16[512,768]{1,0:T(8,128)(2,1)S(1)}, bf16[512,768]{1,0:T(8,128)(2,1)}, u32[]{:S(2)}, u32[]{:S(2)}) collective-permute-start(bf16[512,768]{1,0:T(8,128)(2,1)S(1)} %fusion.3.slot0_ref), channel_id=1, source_target_pairs={{0,1},{1,0},{2,3},{3,2},{4,5},{5,4},{6,7},{7,6},{8,9},{9,8},{10,11... | collective-permute-start | bytes 2359304 | tf_op jit(solution)/shard_map/ppermute | solution.py:881
  70.5 2.3 collective-permute-start.3
  70.6 38.9 %collective-permute-start.4 = (bf16[768,768]{1,0:T(8,128)(2,1)}, bf16[768,768]{1,0:T(8,128)(2,1)}, u32[]{:S(2)}, u32[]{:S(2)}) collective-permute-start(bf16[768,768]{1,0:T(8,128)(2,1)} %get-tuple-element.115.outer0), channel_id=1, source_target_pairs={{0,2},{1,3},{2,0},{3,1},{4,6},{5,7},{6,4},{7,5},{8,10},{9,11},{10,... | collective-permute-start | bytes 3538952 | tf_op jit(solution)/shard_map/ppermute | solution.py:881
  88.9 20.6 %collective-permute-start.5 = (bf16[192,1024]{1,0:T(8,128)(2,1)}, bf16[192,1024]{1,0:T(8,128)(2,1)S(1)}, u32[]{:S(2)}, u32[]{:S(2)}) collective-permute-start(bf16[192,1024]{1,0:T(8,128)(2,1)} %get-tuple-element.119), channel_id=1, source_target_pairs={{0,2},{1,3},{2,0},{3,1},{4,6},{5,7},{6,4},{7,5},{8,10},{9,11},{10,... | collective-permute-start | bytes 1179656 | tf_op jit(solution)/shard_map/ppermute | solution.py:881
  111.5 2.4 collective-permute-start.6
  111.6 4.1 %collective-permute-start.8 = (bf16[512,768]{1,0:T(8,128)(2,1)S(1)}, bf16[512,768]{1,0:T(8,128)(2,1)S(1)}, u32[]{:S(2)}, u32[]{:S(2)}) collective-permute-start(bf16[512,768]{1,0:T(8,128)(2,1)S(1)} %bitcast.32), channel_id=1, source_target_pairs={{0,1},{1,0},{2,3},{3,2},{4,5},{5,4},{6,7},{7,6},{8,9},{9,8},{10,11... | collective-permute-start | bytes 2359304 | tf_op jit(solution)/shard_map/ppermute | solution.py:881
  115.5 2.3 collective-permute-start.7
  141.9 2.6 collective-permute-start.9
  149.5 2.3 collective-permute-start.10
  149.5 6.2 %collective-permute-start.12 = (bf16[512,768]{1,0:T(8,128)(2,1)S(1)}, bf16[512,768]{1,0:T(8,128)(2,1)S(1)}, u32[]{:S(2)}, u32[]{:S(2)}) collective-permute-start(bf16[512,768]{1,0:T(8,128)(2,1)S(1)} %get-tuple-element.138), channel_id=1, source_target_pairs={{0,1},{1,0},{2,3},{3,2},{4,5},{5,4},{6,7},{7,6},{8,9},{9,8},{10,11... | collective-permute-start | bytes 2359304 | tf_op jit(solution)/shard_map/ppermute | solution.py:881
  154.0 11.5 %collective-permute-start.11 = (bf16[192,1024]{1,0:T(8,128)(2,1)}, bf16[192,1024]{1,0:T(8,128)(2,1)}, u32[]{:S(2)}, u32[]{:S(2)}) collective-permute-start(bf16[192,1024]{1,0:T(8,128)(2,1)} %get-tuple-element.136), channel_id=1, source_target_pairs={{0,2},{1,3},{2,0},{3,1},{4,6},{5,7},{6,4},{7,5},{8,10},{9,11},{10,... | collective-permute-start | bytes 1179656 | tf_op jit(solution)/shard_map/ppermute | solution.py:881
  156.9 49.5 %all-to-all-start.2 = ((bf16[8,64,768]{2,1,0:T(8,128)(2,1)}), bf16[8,64,768]{2,1,0:T(8,128)(2,1)S(1)}, u32[]{:S(2)}, u32[]{:S(2)}) async-start(bf16[8,64,768]{2,1,0:T(8,128)(2,1)} %bitcast.8), calls=%async_computation.2 | async-start | bytes 1572864 | tf_op jit(solution)/shard_map/all_to_all | solution.py:884
  160.8 93.7 %reduce-scatter.5.cloned.1.call-start = ((), (), s32[]{:S(2)}) async-start(), calls=%async_computation.9 | async-start | bytes 1769472 | tf_op jit(solution)/shard_map/reduce_scatter | solution.py:905
  165.5 47.2 %copy-start.11 = (bf16[512,768]{1,0:T(8,128)(2,1)S(1)}, bf16[512,768]{1,0:T(8,128)(2,1)}, u32[]{:S(2)}) copy-start(bf16[512,768]{1,0:T(8,128)(2,1)} %copy-done.10) | copy-start | bytes 2359300
  206.3 2.7 collective-permute-start.13
  211.8 21.2 %collective-permute-start.14 = (bf16[512,768]{1,0:T(8,128)(2,1)}, bf16[512,768]{1,0:T(8,128)(2,1)S(1)}, u32[]{:S(2)}, u32[]{:S(2)}) collective-permute-start(bf16[512,768]{1,0:T(8,128)(2,1)} %get-tuple-element.147), channel_id=1, source_target_pairs={{0,1},{1,0},{2,3},{3,2},{4,5},{5,4},{6,7},{7,6},{8,9},{9,8},{10,11... | collective-permute-start | bytes 2359304 | tf_op jit(solution)/shard_map/ppermute | solution.py:881
  212.0 21.1 %collective-permute-start.15 = (bf16[512,768]{1,0:T(8,128)(2,1)}, bf16[512,768]{1,0:T(8,128)(2,1)}, u32[]{:S(2)}, u32[]{:S(2)}) collective-permute-start(bf16[512,768]{1,0:T(8,128)(2,1)} %add_convert_fusion), channel_id=1, source_target_pairs={{0,2},{1,3},{2,0},{3,1},{4,6},{5,7},{6,4},{7,5},{8,10},{9,11},{10,... | collective-permute-start | bytes 2359304 | tf_op jit(solution)/shard_map/ppermute | solution.py:881
  221.0 3.7 %collective-permute-start.16 = (f32[15,128]{1,0:T(8,128)S(1)}, f32[15,128]{1,0:T(8,128)S(1)}, u32[]{:S(2)}, u32[]{:S(2)}) collective-permute-start(f32[15,128]{1,0:T(8,128)S(1)} %maximum_bitcast_fusion), channel_id=1, source_target_pairs={{0,4},{4,0},{8,12},{12,8},{16,20},{20,16},{24,28},{28,24},{1,5},{5... | collective-permute-start | bytes 23048 | tf_op jit(solution)/shard_map/ppermute | solution.py:892
  224.8 3.7 %collective-permute-start.17 = (f32[15,128]{1,0:T(8,128)S(1)}, f32[15,128]{1,0:T(8,128)S(1)}, u32[]{:S(2)}, u32[]{:S(2)}) collective-permute-start(f32[15,128]{1,0:T(8,128)S(1)} %fusion.19), channel_id=1, source_target_pairs={{0,8},{4,12},{8,0},{12,4},{16,24},{20,28},{24,16},{28,20},{1,9},{5... | collective-permute-start | bytes 23048 | tf_op jit(solution)/shard_map/ppermute | solution.py:892
  228.4 4.6 %collective-permute-start.18 = (f32[15,128]{1,0:T(8,128)S(1)}, f32[15,128]{1,0:T(8,128)S(1)}, u32[]{:S(2)}, u32[]{:S(2)}) collective-permute-start(f32[15,128]{1,0:T(8,128)S(1)} %fusion.20), channel_id=1, source_target_pairs={{0,16},{4,20},{8,24},{12,28},{16,0},{20,4},{24,8},{28,12},{1,17},{... | collective-permute-start | bytes 23048 | tf_op jit(solution)/shard_map/ppermute | solution.py:892
  238.7 24.7 %all-to-all-start.3 = ((bf16[8,64,768]{2,1,0:T(8,128)(2,1)}), bf16[8,64,768]{2,1,0:T(8,128)(2,1)S(1)}, u32[]{:S(2)}, u32[]{:S(2)}) async-start(bf16[8,64,768]{2,1,0:T(8,128)(2,1)} %bitcast.11), calls=%async_computation.4 | async-start | bytes 1572864 | tf_op jit(solution)/shard_map/all_to_all | solution.py:884
  243.1 7.1 %collective-permute-start.20 = (bf16[96,1536]{1,0:T(8,128)(2,1)S(1)}, bf16[96,1536]{1,0:T(8,128)(2,1)S(1)}, u32[]{:S(2)}, u32[]{:S(2)}) collective-permute-start(bf16[96,1536]{1,0:T(8,128)(2,1)S(1)} %pad_maximum_fusion.1), channel_id=1, source_target_pairs={{0,2},{1,3},{2,0},{3,1},{4,6},{5,7},{6,4},{7,5},{8,10},{9,11},{10,... | collective-permute-start | bytes 884744 | tf_op jit(solution)/shard_map/ppermute | solution.py:881
  244.3 1.2 collective-permute-start.19
  250.2 3.7 %collective-permute-start.22 = (f32[15,128]{1,0:T(8,128)S(1)}, f32[15,128]{1,0:T(8,128)S(1)}, u32[]{:S(2)}, u32[]{:S(2)}) collective-permute-start(f32[15,128]{1,0:T(8,128)S(1)} %add.83), channel_id=1, source_target_pairs={{0,2},{1,3},{2,0},{3,1},{4,6},{5,7},{6,4},{7,5},{8,10},{9,11},{10,... | collective-permute-start | bytes 23048 | tf_op jit(solution)/shard_map/ppermute | solution.py:881
  255.4 4.1 %collective-permute-start.21 = (bf16[96,192]{1,0:T(8,128)(2,1)S(1)}, bf16[96,192]{1,0:T(8,128)(2,1)S(1)}, u32[]{:S(2)}, u32[]{:S(2)}) collective-permute-start(bf16[96,192]{1,0:T(8,128)(2,1)S(1)} %slice.74), channel_id=1, source_target_pairs={{0,2},{1,3},{2,0},{3,1},{4,6},{5,7},{6,4},{7,5},{8,10},{9,11},{10,... | collective-permute-start | bytes 110600 | tf_op jit(solution)/shard_map/ppermute | solution.py:881
  (40 other events, 197.9 us)
Sparse Core Ops, SparseCore 0:
  11.2 52.2 all-gather.2
  65.0 40.9 all-gather.4
  142.0 67.0 reduce-scatter.2
  219.1 35.4 reduce-scatter.4

commit v2 on v1

--- a/solution.py
+++ b/solution.py
@@ -58,12 +58,33 @@
             bias_ref[i] = pltpu.roll(full, 0, 1, stride=1, stride_axis=0)[:, TILE:]
 
 
+def deal_kernel(back, order_ref, values_ref, out_ref):
+    rows = values_ref.shape[0]
+    place = lax.broadcasted_iota(jnp.int32, (rows, rows), 0)
+    chosen = jnp.where(place == order_ref[...], 1.0, 0.0).astype(BF16)
+    dealt = mm(chosen, values_ref[...]) if back else contract(chosen, 0, values_ref[...], 0)
+    out_ref[...] = dealt.astype(BF16)
+
+
+def deal_rows(values, order, back):
+    return pl.pallas_call(
+        functools.partial(deal_kernel, back),
+        out_shape=jax.ShapeDtypeStruct(values.shape, BF16),
+        in_specs=[VMEM, VMEM],
+        out_specs=VMEM,
+        compiler_params=pltpu.CompilerParams(vmem_limit_bytes=16 << 20),
+        cost_estimate=SHORT,
+        name="deal_back" if back else "deal_rows",
+    )(order[None], values)
+
+
 def pack_kernel(inner_ref, query_ref, key_ref, value_ref, proj_ref, outer_ref, first_ref, rest_ref):
     hidden = inner_ref.shape[1]
-    first = [query_ref[...], key_ref[...], value_ref[...], outer_ref[...], proj_ref[...]]
-    first_ref[...] = jnp.concatenate(first, axis=1).astype(BF16)
+    proj = proj_ref[...].T.astype(BF16)
+    first = [query_ref[...], key_ref[...], value_ref[...], outer_ref[...]]
+    first_ref[...] = jnp.concatenate([part.astype(BF16) for part in first] + [proj], axis=1)
     rest_ref[:, :hidden] = inner_ref[...].astype(BF16)
-    rest_ref[:, hidden:] = proj_ref[...].astype(BF16)
+    rest_ref[:, hidden:] = proj
 
 
 def pack_weights(inner, query, key, value, proj, outer):
@@ -472,10 +493,7 @@
         out_shape=(
             jax.ShapeDtypeStruct((3 * cols, rows), BF16),
             jax.ShapeDtypeStruct((heads * KINDS, 2 * TILE), F32),
-            jax.ShapeDtypeStruct((rows_dev, width), F32),
-            jax.ShapeDtypeStruct((rows_dev, width), BF16),
-            jax.ShapeDtypeStruct((rows_dev, width), F32),
-            jax.ShapeDtypeStruct((rows_dev, width), BF16),
+            *[jax.ShapeDtypeStruct((rows_dev, width), BF16)] * 4,
         ),
         in_specs=[SMEM] + [VMEM] * 10,
         out_specs=(VMEM,) * 6,
@@ -521,20 +539,19 @@
     return scale * (scaled - normed * inner)
 
 
-def middle_back_kernel(middle_ref, near_ref, far_ref, grads_ref, gain_ref, wide_ref, low_ref):
+def middle_back_kernel(middle_ref, near_ref, far_ref, grads_ref, gain_ref, low_ref):
     for rs in row_blocks(middle_ref.shape[0]):
-        upstream = near_ref[rs, :] + far_ref[rs, :].astype(F32)
+        upstream = near_ref[rs, :].astype(F32) + far_ref[rs, :].astype(F32)
         back = norm_back_rows(middle_ref[rs, :], upstream, gain_ref[...])
-        wide = grads_ref[rs, :].astype(F32) + back
-        wide_ref[rs, :] = wide
-        low_ref[rs, :] = wide.astype(BF16)
-
-
-def rows_back_kernel(rows_ref, near_ref, core_ref, far_ref, wide_ref, gain_ref, low_ref):
+        low_ref[rs, :] = (grads_ref[rs, :].astype(F32) + back).astype(BF16)
+
+
+def rows_back_kernel(rows_ref, near_ref, core_ref, far_ref, after_ref, gain_ref, low_ref):
     for rs in row_blocks(rows_ref.shape[0]):
-        upstream = near_ref[rs, :] + core_ref[rs, :].astype(F32) + far_ref[rs, :].astype(F32)
+        upstream = near_ref[rs, :].astype(F32) + core_ref[rs, :].astype(F32)
+        upstream = upstream + far_ref[rs, :].astype(F32)
         back = norm_back_rows(rows_ref[rs, :].astype(F32), upstream, gain_ref[...])
-        low_ref[rs, :] = (wide_ref[rs, :] + back).astype(BF16)
+        low_ref[rs, :] = (after_ref[rs, :].astype(F32) + back).astype(BF16)
 
 
 def by_rows(kernel, name, gain, *operands, out, cost=SHORT):
@@ -625,7 +642,7 @@
     part = inner0.shape[1]
     block = grads_ref.shape[1]
     per_part = part // TILE
-    steps = 2 * per_part
+    steps = 2
     sweeps = 2 * part // block
     step = pl.program_id(0)
     root, cubic = 0.7978845608028654, 0.044715
@@ -636,20 +653,25 @@
     ]
     weights = ((inner0, outer0), (inner1, outer1))
 
-    def tile(inner_ref, outer_ref, index, offset):
-        js = slice(index * TILE, (index + 1) * TILE)
-        to = slice(offset + index * TILE, offset + (index + 1) * TILE)
-        firsts = []
-        for normed_ref, grad_ref, begin, _ in places:
-            rs = slice(begin, begin + TILE)
-            a = mm(normed_ref[rs, :], inner_ref[:, js])
-            firsts.append((a, mm(grad_ref[rs, :], outer_ref[:, js])))
-        for (a, dh), (_, _, _, at) in zip(firsts, places):
-            rs = slice(at, at + TILE)
+    def products(inner_ref, outer_ref, index, place):
+        normed_ref, grad_ref, begin, _ = place
+        rs, js = slice(begin, begin + TILE), slice(index * TILE, (index + 1) * TILE)
+        return mm(normed_ref[rs, :], inner_ref[:, js]), mm(grad_ref[rs, :], outer_ref[:, js])
+
+    def hidden_part(inner_ref, outer_ref, offset):
+        work = [(index, place) for index in range(per_part) for place in places]
+        ahead = products(inner_ref, outer_ref, *work[0])
+        for n, (index, place) in enumerate(work):
+            a, dh = ahead
+            if n + 1 < len(work):
+                ahead = products(inner_ref, outer_ref, *work[n + 1])
+            rs = slice(place[3], place[3] + TILE)
+            to = slice(offset + index * TILE, offset + (index + 1) * TILE)
             square = a * a
-            t = jnp.tanh(root * a * (1.0 + cubic * square))
-            cdf = 0.5 * (1.0 + t)
-            slope = cdf + 0.5 * a * (1.0 - t * t) * (root * (1.0 + 3.0 * cubic * square))
+            t = jnp.tanh(a * (root + (root * cubic) * square))
+            half_a = 0.5 * a
+            cdf = 0.5 + 0.5 * t
+            slope = cdf + half_a * (1.0 - t * t) * (root + (3.0 * root * cubic) * square)
             hid_ref[rs, to] = (a * cdf).astype(BF16)
             pre_ref[rs, to] = (dh * slope).astype(BF16)
 
@@ -660,19 +682,17 @@
             if offset == 0:
                 sum_ref[rs, :] = back
             elif at < half:
-                near_ref[rs, :] = sum_ref[rs, :] + back
+                near_ref[rs, :] = (sum_ref[rs, :] + back).astype(BF16)
             else:
                 far_ref[at - half : at - half + TILE, :] = (sum_ref[rs, :] + back).astype(BF16)
 
     for i, (inner_ref, outer_ref) in enumerate(weights):
-        for index in range(per_part):
-
-            @pl.when(step == i * per_part + index)
-            def _(inner_ref=inner_ref, outer_ref=outer_ref, index=index, offset=i * part):
-                tile(inner_ref, outer_ref, index, offset)
-                if index == per_part - 1:
-                    rows_out(pre_ref, inner_ref, offset, acc_ref, own_ref, send_ref)
-                    rows_out(hid_ref, outer_ref, offset, out_acc_ref, out_own_ref, out_send_ref)
+
+        @pl.when(step == i)
+        def _(inner_ref=inner_ref, outer_ref=outer_ref, offset=i * part):
+            hidden_part(inner_ref, outer_ref, offset)
+            rows_out(pre_ref, inner_ref, offset, acc_ref, own_ref, send_ref)
+            rows_out(hid_ref, outer_ref, offset, out_acc_ref, out_own_ref, out_send_ref)
 
     def load(first_ref, second_ref):
         left_ref[:, :half] = first_ref[...].T
@@ -710,17 +730,14 @@
     part = inners[0].shape[1]
     rows, hidden = 2 * half, 2 * part
     block = 2 * TILE
-    steps = hidden // TILE
+    steps = 2
     return pl.pallas_call(
         functools.partial(ffn_kernel, ring),
         grid=(steps + 2 * (hidden // block),),
         out_shape=(
-            jax.ShapeDtypeStruct((half, width), F32),
-            jax.ShapeDtypeStruct((half, width), BF16),
-            jax.ShapeDtypeStruct((half, width), F32),
-            jax.ShapeDtypeStruct((half, width), BF16),
-            jax.ShapeDtypeStruct((width, 2 * hidden), BF16),
-            jax.ShapeDtypeStruct((1, width), F32),
+            *[pltpu.HBM((half, width), BF16)] * 4,
+            pltpu.HBM((width, 2 * hidden), BF16),
+            pltpu.HBM((1, width), F32),
         ),
         in_specs=[VMEM] * 8,
         out_specs=(
@@ -800,35 +817,50 @@
         ),
         in_specs=[VMEM] * 7,
         out_specs=(VMEM, VMEM),
-        compiler_params=pltpu.CompilerParams(vmem_limit_bytes=24 << 20),
+        compiler_params=pltpu.CompilerParams(vmem_limit_bytes=58 << 20),
         cost_estimate=SHORT,
         name="qkv_grads",
     )(grad_qkv, *slots, weights, proj)
 
 
-def finish_kernel(
-    pack_ref, taken_ref, last_ref, far_ref, query_ref, key_ref, value_ref, proj_ref, inner_ref, outer_ref
-):
-    hidden, cols = inner_ref.shape[1], query_ref.shape[1]
-    pack, taken, last = pack_ref[...].astype(F32), taken_ref[...].astype(F32), last_ref[...].astype(F32)
+def finish_kernel(pack_ref, taken_ref, inner_ref, outer_ref):
+    hidden = inner_ref.shape[1]
+    pack, taken = pack_ref[...].astype(F32), taken_ref[...].astype(F32)
     inner_ref[...] = pack[:, :hidden] + taken[:, :hidden]
     outer_ref[...] = pack[:, 2 * hidden : 3 * hidden] + taken[:, hidden:]
+
+
+def finish(pack, taken):
+    shape = jax.ShapeDtypeStruct((taken.shape[0], taken.shape[1] // 2), F32)
+    return pl.pallas_call(
+        finish_kernel,
+        out_shape=(shape, shape),
+        in_specs=[VMEM] * 2,
+        out_specs=(VMEM,) * 2,
+        cost_estimate=SHORT,
+        name="finish",
+    )(pack, taken)
+
+
+def finish_last_kernel(last_ref, far_ref, query_ref, key_ref, value_ref, proj_ref):
+    cols = query_ref.shape[1]
+    last = last_ref[...].astype(F32)
     for i, out_ref in enumerate((query_ref, key_ref, value_ref)):
         out_ref[...] = last[:, i * cols : (i + 1) * cols]
-    proj_ref[...] = last[:, 3 * cols : 4 * cols] + far_ref[...].astype(F32)
-
-
-def finish(pack, taken, last, far, hidden):
+    proj_ref[...] = (last[:, 3 * cols : 4 * cols] + far_ref[...].astype(F32)).T
+
+
+def finish_last(last, far):
     rows, cols = far.shape
-    shapes = [(rows, cols)] * 4 + [(rows, hidden)] * 2
-    return pl.pallas_call(
-        finish_kernel,
+    shapes = [(rows, cols)] * 3 + [(cols, rows)]
+    return pl.pallas_call(
+        finish_last_kernel,
         out_shape=tuple(jax.ShapeDtypeStruct(shape, F32) for shape in shapes),
-        in_specs=[VMEM] * 4,
-        out_specs=(VMEM,) * 6,
-        cost_estimate=SHORT,
-        name="finish",
-    )(pack, taken, last, far)
+        in_specs=[VMEM] * 2,
+        out_specs=(VMEM,) * 4,
+        cost_estimate=SHORT,
+        name="finish_last",
+    )(last, far)
 
 
 def bias_rows(line):
@@ -883,9 +915,6 @@
     def deal_out(values):
         return lax.all_to_all(values, "dp", split_axis=0, concat_axis=0, tiled=True)
 
-    def pick(values, order):
-        return values.at[order].get(mode="promise_in_bounds", unique_indices=True)
-
     def sum_groups(values):
         step = 1
         while step < dp_size:
@@ -907,14 +936,14 @@
         )
 
     own_front, own_rest = pack_weights(
-        w_inner, w_query, w_key, w_value, w_proj.T, w_outer.T
+        w_inner, w_query, w_key, w_value, w_proj, w_outer.T
     )
     own_front, tokens = after(own_front, tokens)
     ends = (3 * cols, 3 * cols + hidden, 4 * cols + hidden)
     front, outer_own, proj_own = gather(
         own_front, ((0, ends[0], False), (ends[0], ends[1], False), (ends[1], ends[2], True))
     )
-    low_rows = deal_out(pick(tokens, deal))
+    low_rows = deal_out(tokens.at[deal].get(mode="promise_in_bounds", unique_indices=True))
     other_rest, low_rows = after(swap(own_rest, 2), low_rows)
     inner_own, inner_other, proj_other = gather(
         jnp.concatenate([own_rest[:, :hidden], other_rest], axis=1),
@@ -932,18 +961,15 @@
     base = bias_rows(offset_bias)
     info = jnp.concatenate([lengths, jnp.full((1, 1), me, jnp.int32)], axis=1)
 
-    inverse_order = (
-        jnp.zeros((rows_dev,), jnp.int32).at[deal].set(jnp.arange(rows_dev, dtype=jnp.int32))
-    )
     slot0 = (scaled_rows(low_rows.astype(F32)) * gain_attn).astype(BF16)
     slot2 = swap(slot0, 2)
     slot1 = swap(slot0, 1)
-    slot2, front, base, info, inverse_order = after(slot2, front, base, info, inverse_order)
+    slot2, front, base, info = after(slot2, front, base, info)
     slot3 = swap(slot2, 1)
     slots = (slot0, slot1, slot2, slot3)
     outer_other = swap(outer_own, 2)
 
-    low_grads = deal_out(pick(cotangent, deal))
+    low_grads = deal_out(cotangent.at[deal].get(mode="promise_in_bounds", unique_indices=True))
 
     mixed_far, wide_far, lse_far, qkv, keys = attend_far(info, base, front, slots)
     mixed_other = swap(mixed_far, 2)
@@ -961,7 +987,7 @@
         ring, pair_two, pair_grads, (inner_own, inner_other), (outer_own, outer_other)
     )
     shard_pack = scatter_sum(grad_pack)
-    grad_middle, low_middle = by_rows(
+    (low_middle,) = by_rows(
         middle_back_kernel,
         "middle_back",
         gain_ffn,
@@ -969,7 +995,7 @@
         back_own,
         swap(back_send, 1),
         low_grads,
-        out=(F32, BF16),
+        out=(BF16,),
     )
     pair_middle = (low_middle, swap(low_middle, 1))
     grad_own, to_other = mixed_grads(pair_middle, proj_own, proj_other)
@@ -977,7 +1003,7 @@
     proj_pack = proj_grads(pair_middle, (mixed_own, mixed_other))
 
     out_own, to_other = after(out_own, to_other)
-    result_rows = (middle + out_own + swap(out_far, 1).astype(F32)).astype(BF16)
+    result_rows = (middle + out_own.astype(F32) + swap(out_far, 1).astype(F32)).astype(BF16)
     result_rows, proj_pack = after(result_rows, proj_pack)
     back_rows = deal_out(result_rows)
 
@@ -994,17 +1020,7 @@
         rows_dev,
     )
     far_send, back_rows = after(far_send, back_rows)
-    grad_later = (far_own + swap(far_send, 1).astype(F32)).astype(BF16)
-    grad_later, near_send = after(grad_later, near_send)
-    later_qkv, grad_later = after(grad_qkv, grad_later)
-    low_qkv_w, gain_one = qkv_grads(ring, later_qkv, slots, front, proj_pack)
-    low_qkv_w, shard_pack = after(low_qkv_w, shard_pack)
-    low_qkv_w, diagonals = after(low_qkv_w, diagonals)
-    shard_qkv = scatter_sum(low_qkv_w)
-    taken = swap(
-        jnp.concatenate([shard_pack[:, hidden : 2 * hidden], shard_pack[:, 3 * hidden :]], axis=1),
-        2,
-    )
+    grad_later = (far_own.astype(F32) + swap(far_send, 1).astype(F32)).astype(BF16)
     offset_count = 2 * MAXDIST + 1
     onehot_line = (
         line_index()[:, None] == jnp.arange(offset_count, dtype=jnp.int32)[None, :]
@@ -1015,6 +1031,15 @@
     table_heads = jnp.dot(onehot_buckets.T, offset_total.T, precision=lax.Precision.HIGHEST)
     table_full = lax.dynamic_update_slice_in_dim(
         jnp.zeros(rel_table.shape, F32), table_heads, me * heads, 1
+    )
+    grad_later, near_send, table_full = after(grad_later, near_send, table_full)
+    later_qkv, grad_later = after(grad_qkv, grad_later)
+    low_qkv_w, gain_one = qkv_grads(ring, later_qkv, slots, front, proj_pack)
+    low_qkv_w, shard_pack = after(low_qkv_w, shard_pack)
+    shard_qkv = scatter_sum(low_qkv_w)
+    taken = swap(
+        jnp.concatenate([shard_pack[:, hidden : 2 * hidden], shard_pack[:, 3 * hidden :]], axis=1),
+        2,
     )
     terms = [gain_one[0] / gain_attn, gain_two[0] / gain_ffn, table_full.reshape(-1)]
     small = sum_groups(jnp.concatenate(terms).reshape(-1, 128))
@@ -1032,23 +1057,22 @@
         near_own,
         near_core,
         grad_two_rows,
-        grad_middle,
+        low_middle,
         out=(BF16,),
         cost=pl.CostEstimate(flops=(3<<33)//2, bytes_accessed=(1<<26)//2, transcendentals=(1<<23)//2),
     )
 
     shard_far = swap(shard_qkv[:, 4 * cols :], 2)
-    weight_shards = finish(shard_pack, taken, shard_qkv, shard_far, hidden)
-    out_rows = pick(back_rows, inverse_order)
+    weight_shards = [*finish_last(shard_qkv, shard_far), *finish(shard_pack, taken)]
+    out_rows = deal_rows(back_rows, deal, True)
     small = small.reshape(-1)
     back_grads = deal_out(low_grad_rows)
     back_grads, out_rows, *weight_shards = after(back_grads, out_rows, *weight_shards)
     return (
         out_rows,
-        pick(back_grads, inverse_order),
+        deal_rows(back_grads, deal, True),
         *weight_shards[:3],
-        weight_shards[3].T,
-        weight_shards[4],
+        *weight_shards[3:5],
         weight_shards[5].T,
         small[:width],
         small[width : 2 * width],

time: 278 us -> 273 us (0.982)
  the two profiles are of different devices: /device:TPU:0 before, /device:TPU:12 now
where the time goes in v2:
time: 273 us; the launch traced here: 269 us
  Pallas kernels  118 us (43%)
  waiting for transfers between devices  74 us (27%)
  starting transfers between devices  32.8 us (12%)
  local copies, waits for them, and re-layouts  21.7 us (8%)
  between operations  14.4 us (5%)
  other arithmetic  6.36 us (2%)
    pallas_call x1, Pallas kernels, attend_back(): pl.pallas_call(functools.partial(attend_back_kernel, heads, rows_dev), ou...  40.6 us
    ppermute x20, waiting for transfers between devices, swap(): lax.ppermute(values, 'tensor', [(i, i ^ bit) for i in range(tensor_size)])  28.7 us
    all_to_all x4, starting transfers between devices, deal_out(): return lax.all_to_all(values, 'dp', split_axis=0, concat_axis=0, tiled=True)  22.2 us
    pallas_call x1, Pallas kernels, ffn(): pl.pallas_call(functools.partial(ffn_kernel, ring), grid=(steps + 2 * (hi...  21.3 us
    all_to_all x4, waiting for transfers between devices, deal_out(): return lax.all_to_all(values, 'dp', split_axis=0, concat_axis=0, tiled=True)  20.7 us
    pallas_call x1, Pallas kernels, attend_far(): pl.pallas_call(functools.partial(attend_far_kernel, heads, rows_dev), out...  14.2 us
    pallas_call x1, Pallas kernels, attend_near(): pl.pallas_call(functools.partial(attend_near_kernel, heads, rows_dev), ou...  12.3 us
    unnamed x75, local copies, waits for them, and re-layouts  12.2 us
  transfers between devices with their start and end apart: 31, of which 18 were waited for; matrix products, arithmetic and copies ran while one was open for 7% of the time, Pallas kernels for 34%

profile of v2, /device:TPU:12, one launch (start us, length us, event | category | flops | bytes accessed | tf_op | source)
XLA Modules:
  0.0 269.3 jit_solution(14443086395483703585)
XLA Ops:
  7.2 2.2 pack_weights.1
  10.2 2.7 %gather_fusion = bf16[512,768]{1,0:T(8,128)(2,1)} fusion(bf16[512,768]{1,0:T(8,128)(2,1)S(1)} %copy-done, s32[1024]{0:T(1024)S(1)} %pad_clamp_fusion), kind=kCustom, calls=%fused_computation | custom fusion | bytes 1574912 | tf_op jit(solution)/shard_map/gather | solution.py:946
  12.9 6.4 %all-to-all-start = ((bf16[8,64,768]{2,1,0:T(8,128)(2,1)}), bf16[8,64,768]{2,1,0:T(8,128)(2,1)S(1)}, u32[]{:S(2)}, u32[]{:S(2)}) async-start(bf16[8,64,768]{2,1,0:T(8,128)(2,1)} %bitcast.1), calls=%async_computation | async-start | bytes 1572864 | tf_op jit(solution)/shard_map/all_to_all | solution.py:916
  19.8 5.6 %collective-permute-done = bf16[96,960]{1,0:T(8,128)(2,1)S(1)} collective-permute-done((bf16[96,960]{1,0:T(8,128)(2,1)S(1)}, bf16[96,960]{1,0:T(8,128)(2,1)S(1)}, u32[]{:S(2)}, u32[]{:S(2)}) %collective-permute-start) | collective-permute-done | bytes 184352 | tf_op jit(solution)/shard_map/ppermute | solution.py:913
  25.4 20.7 %all-to-all-done = bf16[8,64,768]{2,1,0:T(8,128)(2,1)S(1)} async-done(((bf16[8,64,768]{2,1,0:T(8,128)(2,1)}), bf16[8,64,768]{2,1,0:T(8,128)(2,1)S(1)}, u32[]{:S(2)}, u32[]{:S(2)}) %all-to-all-start) | async-done | bytes 786464 | tf_op jit(solution)/shard_map/all_to_all | solution.py:916
  48.0 2.7 %gather_fusion.1 = bf16[512,768]{1,0:T(8,128)(2,1)} fusion(bf16[512,768]{1,0:T(8,128)(2,1)S(1)} %copy-done.19, s32[1024]{0:T(1024)S(1)} %pad_clamp_fusion), kind=kCustom, calls=%fused_computation.1 | custom fusion | bytes 1574912 | tf_op jit(solution)/shard_map/gather | solution.py:972
  50.7 6.1 %all-to-all-start.1 = ((bf16[8,64,768]{2,1,0:T(8,128)(2,1)}), bf16[8,64,768]{2,1,0:T(8,128)(2,1)S(1)}, u32[]{:S(2)}, u32[]{:S(2)}) async-start(bf16[8,64,768]{2,1,0:T(8,128)(2,1)} %bitcast.39), calls=%async_computation.1 | async-start | bytes 1572864 | tf_op jit(solution)/shard_map/all_to_all | solution.py:916
  60.3 1.9 all-gather.3.cloned.1.call-done.found_ref
  62.2 3.6 %unring.2 = (bf16[768,576]{1,0:T(8,128)(2,1)}, bf16[768,768]{1,0:T(8,128)(2,1)}, bf16[192,768]{1,0:T(8,128)(2,1)}) custom-call(bf16[768,1536]{1,0:T(8,128)(2,1)} %all-gather.3.cloned.1.call-done.found_ref), custom_call_target="tpu_custom_call" | custom-call | flops 1048576 | bytes 65536 | tf_op jit(solution)/shard_map/unring/pallas_call | solution.py:130
  66.2 2.0 collective-permute-done.3.slot3_ref
  69.1 14.2 %attend_far.1 = (bf16[192,1024]{1,0:T(8,128)(2,1)}, f32[192,1024]{1,0:T(8,128)}, f32[3,1024]{1,0:T(4,128)}, bf16[576,2048]{1,0:T(8,128)(2,1)}, bf16[3,2048,128]{2,1,0:T(8,128)(2,1)}) custom-call(s32[1,3]{1,0:T(1,128)} %pad_add_fusion.info_ref, f32[15,512]{1,0:T(8,128)} %reshape.102.base_ref, bf16[768,576]{1,0:T(8,128)(2,1)} %get-tuple-element.101.w_ref, ...), custom_call_target="tpu_custom_call" | custom-call | flops 1048576 | bytes 65536 | tf_op jit(solution)/shard_map/attend_far/pallas_call | solution.py:331
  84.7 12.3 %attend_near.1 = (bf16[192,1024]{1,0:T(8,128)(2,1)}, f32[192,1024]{1,0:T(8,128)}, f32[3,1024]{1,0:T(4,128)}) custom-call(s32[1,3]{1,0:T(1,128)} %pad_add_fusion.info_ref, f32[15,512]{1,0:T(8,128)} %reshape.102.base_ref, bf16[576,2048]{1,0:T(8,128)(2,1)} %get-tuple-element.105.qkv_ref, bf16[3,2048,128]{2,1,0:T(8,128)(2,1)} %get-tuple-element.104.key_ref), custom_call_target="tpu_custom_call" | custom-call | flops 1048576 | bytes 65536 | tf_op jit(solution)/shard_map/attend_near/pallas_call | solution.py:349
  97.0 6.2 %all-gather.5.cloned.1.call-done.found_ref = bf16[768,1728]{1,0:T(8,128)(2,1)} async-done(((bf16[96,1728]{1,0:T(8,128)(2,1)}), bf16[768,1728]{1,0:T(8,128)(2,1)}) %all-gather.5.cloned.1.call-update) | async-done | bytes 2654224 | tf_op jit(solution)/shard_map/all_gather | solution.py:930
  103.2 3.4 %unring.3 = (bf16[768,768]{1,0:T(8,128)(2,1)}, bf16[768,768]{1,0:T(8,128)(2,1)}, bf16[192,768]{1,0:T(8,128)(2,1)}) custom-call(bf16[768,1728]{1,0:T(8,128)(2,1)} %all-gather.5.cloned.1.call-done.found_ref), custom_call_target="tpu_custom_call" | custom-call | flops 1048576 | bytes 65536 | tf_op jit(solution)/shard_map/unring/pallas_call | solution.py:130
  112.8 2.1 collective-permute-done.7.normed1
  115.0 21.3 %ffn.1 = (bf16[512,768]{1,0:T(8,128)(2,1)}, bf16[512,768]{1,0:T(8,128)(2,1)}, bf16[512,768]{1,0:T(8,128)(2,1)}, bf16[512,768]{1,0:T(8,128)(2,1)}, bf16[768,3072]{1,0:T(8,128)(2,1)}, /*index=5*/f32[1,768]{1,0:T(1,128)}) custom-call(bf16[512,768]{1,0:T(8,128)(2,1)S(1)} %get-tuple-element.121.normed0, bf16[512,768]{1,0:T(8,128)(2,1)S(1)} %collective-permute-done.7.normed1, ...), custom_call_target="tpu_custom_call" | custom-call | flops 1048576 | bytes 65536 | tf_op jit(solution)/shard_map/ffn/pallas_call | solution.py:734
  137.6 2.1 collective-permute-done.9.far_ref
  150.4 4.9 %all-to-all-start.2 = ((bf16[8,64,768]{2,1,0:T(8,128)(2,1)}), bf16[8,64,768]{2,1,0:T(8,128)(2,1)S(1)}, u32[]{:S(2)}, u32[]{:S(2)}) async-start(bf16[8,64,768]{2,1,0:T(8,128)(2,1)} %bitcast.40), calls=%async_computation.2 | async-start | bytes 1572864 | tf_op jit(solution)/shard_map/all_to_all | solution.py:916
  155.4 3.7 %collective-permute-done.11.grad1_ref = bf16[192,1024]{1,0:T(8,128)(2,1)} collective-permute-done((bf16[192,1024]{1,0:T(8,128)(2,1)}, bf16[192,1024]{1,0:T(8,128)(2,1)}, u32[]{:S(2)}, u32[]{:S(2)}) %collective-permute-start.11) | collective-permute-done | bytes 393248 | tf_op jit(solution)/shard_map/ppermute | solution.py:913
  159.1 40.6 %attend_back.1 = (bf16[576,2048]{1,0:T(8,128)(2,1)}, f32[15,512]{1,0:T(8,128)}, bf16[512,768]{1,0:T(8,128)(2,1)}, bf16[512,768]{1,0:T(8,128)(2,1)}, bf16[512,768]{1,0:T(8,128)(2,1)}, /*index=5*/bf16[512,768]{1,0:T(8,128)(2,1)}) custom-call(s32[1,3]{1,0:T(1,128)} %pad_add_fusion.info_ref, f32[15,512]{1,0:T(8,128)} %reshape.102.base_ref, ...), custom_call_target="tpu_custom_call" | custom-call | flops 25769803776 | bytes 67108864 | tf_op jit(solution)/shard_map/attend_back/pallas_call | solution.py:491
  202.7 2.5 add_convert_fusion
  205.9 6.4 %qkv_grads.1 = (bf16[768,960]{1,0:T(8,128)(2,1)}, f32[1,768]{1,0:T(1,128)}) custom-call(bf16[576,2048]{1,0:T(8,128)(2,1)} %get-tuple-element.147.grad_ref, bf16[512,768]{1,0:T(8,128)(2,1)} %copy-done.20, bf16[512,768]{1,0:T(8,128)(2,1)} %collective-permute-done.2.slot1_ref, bf16[512,768]{1,0:T(8,128)(2,1)} %collective-permute-done.1.slot2_ref, ...), custom_call_target="tpu_custom_call" | custom-call | flops 1048576 | bytes 65536 | tf_op jit(solution)/shard_map/qkv_grads/pallas_call | solution.py:812
  214.3 2.6 collective-permute-done.16
  217.9 2.6 collective-permute-done.17
  220.9 4.3 %collective-permute-done.18 = f32[15,128]{1,0:T(8,128)S(1)} collective-permute-done((f32[15,128]{1,0:T(8,128)S(1)}, f32[15,128]{1,0:T(8,128)S(1)}, u32[]{:S(2)}, u32[]{:S(2)}) %collective-permute-start.18) | collective-permute-done | bytes 7712 | tf_op jit(solution)/shard_map/ppermute | solution.py:921
  226.5 2.3 rows_back.1
  229.7 4.8 %all-to-all-start.3 = ((bf16[8,64,768]{2,1,0:T(8,128)(2,1)}), bf16[8,64,768]{2,1,0:T(8,128)(2,1)S(1)}, u32[]{:S(2)}, u32[]{:S(2)}) async-start(bf16[8,64,768]{2,1,0:T(8,128)(2,1)} %bitcast.36), calls=%async_computation.3 | async-start | bytes 1572864 | tf_op jit(solution)/shard_map/all_to_all | solution.py:916
  237.1 5.7 %collective-permute-done.21.taken_ref = bf16[96,1536]{1,0:T(8,128)(2,1)S(1)} collective-permute-done((bf16[96,1536]{1,0:T(8,128)(2,1)S(1)}, bf16[96,1536]{1,0:T(8,128)(2,1)S(1)}, u32[]{:S(2)}, u32[]{:S(2)}) %collective-permute-start.21) | collective-permute-done | bytes 294944 | tf_op jit(solution)/shard_map/ppermute | solution.py:913
  245.0 2.0 finish.1
  247.0 6.8 %reduce-scatter.5.cloned.1.call-done.last_ref = bf16[96,960]{1,0:T(8,128)(2,1)} async-done(((bf16[768,960]{1,0:T(8,128)(2,1)}), bf16[96,960]{1,0:T(8,128)(2,1)}) %reduce-scatter.5.cloned.1.call-update) | async-done | bytes 184336 | tf_op jit(solution)/shard_map/reduce_scatter | solution.py:934
  256.0 2.7 %collective-permute-done.19.far_ref = bf16[96,192]{1,0:T(8,128)(2,1)S(1)} collective-permute-done((bf16[96,192]{1,0:T(8,128)(2,1)S(1)}, bf16[96,192]{1,0:T(8,128)(2,1)S(1)}, u32[]{:S(2)}, u32[]{:S(2)}) %collective-permute-start.19) | collective-permute-done | bytes 36896 | tf_op jit(solution)/shard_map/ppermute | solution.py:913
  259.3 1.8 finish_last.1
  (181 shorter events, 45.7 us)
Async XLA Ops:
  7.2 55.0 %all-gather.3.cloned.1.call-start = ((), (), s32[]{:S(2)}) async-start(), calls=%async_computation.6 | async-start | bytes 2654208 | tf_op jit(solution)/shard_map/all_gather | solution.py:930
  12.9 33.2 %all-to-all-start = ((bf16[8,64,768]{2,1,0:T(8,128)(2,1)}), bf16[8,64,768]{2,1,0:T(8,128)(2,1)S(1)}, u32[]{:S(2)}, u32[]{:S(2)}) async-start(bf16[8,64,768]{2,1,0:T(8,128)(2,1)} %bitcast.1), calls=%async_computation | async-start | bytes 1572864 | tf_op jit(solution)/shard_map/all_to_all | solution.py:916
  19.3 83.9 %all-gather.5.cloned.1.call-start = ((), (), s32[]{:S(2)}) async-start(), calls=%async_computation.7 | async-start | bytes 3096576 | tf_op jit(solution)/shard_map/all_gather | solution.py:930
  19.3 6.1 %collective-permute-start = (bf16[96,960]{1,0:T(8,128)(2,1)S(1)}, bf16[96,960]{1,0:T(8,128)(2,1)S(1)}, u32[]{:S(2)}, u32[]{:S(2)}) collective-permute-start(bf16[96,960]{1,0:T(8,128)(2,1)S(1)} %copy-done.25), channel_id=1, source_target_pairs={{0,2},{1,3},{2,0},{3,1},{4,6},{5,7},{6,4},{7,5},{8,10},{9,11},{10,... | collective-permute-start | bytes 552968 | tf_op jit(solution)/shard_map/ppermute | solution.py:913
  47.4 18.3 %collective-permute-start.1 = (bf16[512,768]{1,0:T(8,128)(2,1)S(1)}, bf16[512,768]{1,0:T(8,128)(2,1)}, u32[]{:S(2)}, u32[]{:S(2)}) collective-permute-start(bf16[512,768]{1,0:T(8,128)(2,1)S(1)} %fusion.3.slot0_ref), channel_id=1, source_target_pairs={{0,2},{1,3},{2,0},{3,1},{4,6},{5,7},{6,4},{7,5},{8,10},{9,11},{10,... | collective-permute-start | bytes 2359304 | tf_op jit(solution)/shard_map/ppermute | solution.py:913
  50.7 34.0 %all-to-all-start.1 = ((bf16[8,64,768]{2,1,0:T(8,128)(2,1)}), bf16[8,64,768]{2,1,0:T(8,128)(2,1)S(1)}, u32[]{:S(2)}, u32[]{:S(2)}) async-start(bf16[8,64,768]{2,1,0:T(8,128)(2,1)} %bitcast.39), calls=%async_computation.1 | async-start | bytes 1572864 | tf_op jit(solution)/shard_map/all_to_all | solution.py:916
  56.8 155.5 %reduce-scatter.3.cloned.1.call-start = ((), (), s32[]{:S(2)}) async-start(), calls=%async_computation.8 | async-start | bytes 5308416 | tf_op jit(solution)/shard_map/reduce_scatter | solution.py:934
  60.3 5.9 %collective-permute-start.2 = (bf16[512,768]{1,0:T(8,128)(2,1)S(1)}, bf16[512,768]{1,0:T(8,128)(2,1)}, u32[]{:S(2)}, u32[]{:S(2)}) collective-permute-start(bf16[512,768]{1,0:T(8,128)(2,1)S(1)} %fusion.3.slot0_ref), channel_id=1, source_target_pairs={{0,1},{1,0},{2,3},{3,2},{4,5},{5,4},{6,7},{7,6},{8,9},{9,8},{10,11... | collective-permute-start | bytes 2359304 | tf_op jit(solution)/shard_map/ppermute | solution.py:913
  65.7 2.5 collective-permute-start.3
  65.7 40.9 %collective-permute-start.4 = (bf16[768,768]{1,0:T(8,128)(2,1)}, bf16[768,768]{1,0:T(8,128)(2,1)}, u32[]{:S(2)}, u32[]{:S(2)}) collective-permute-start(bf16[768,768]{1,0:T(8,128)(2,1)} %get-tuple-element.111.outer0), channel_id=1, source_target_pairs={{0,2},{1,3},{2,0},{3,1},{4,6},{5,7},{6,4},{7,5},{8,10},{9,11},{10,... | collective-permute-start | bytes 3538952 | tf_op jit(solution)/shard_map/ppermute | solution.py:913
  83.3 23.3 %collective-permute-start.5 = (bf16[192,1024]{1,0:T(8,128)(2,1)}, bf16[192,1024]{1,0:T(8,128)(2,1)S(1)}, u32[]{:S(2)}, u32[]{:S(2)}) collective-permute-start(bf16[192,1024]{1,0:T(8,128)(2,1)} %get-tuple-element.115), channel_id=1, source_target_pairs={{0,2},{1,3},{2,0},{3,1},{4,6},{5,7},{6,4},{7,5},{8,10},{9,11},{10,... | collective-permute-start | bytes 1179656 | tf_op jit(solution)/shard_map/ppermute | solution.py:913
  108.6 2.4 collective-permute-start.6
  108.7 4.1 %collective-permute-start.8 = (bf16[512,768]{1,0:T(8,128)(2,1)S(1)}, bf16[512,768]{1,0:T(8,128)(2,1)S(1)}, u32[]{:S(2)}, u32[]{:S(2)}) collective-permute-start(bf16[512,768]{1,0:T(8,128)(2,1)S(1)} %bitcast.31), channel_id=1, source_target_pairs={{0,1},{1,0},{2,3},{3,2},{4,5},{5,4},{6,7},{7,6},{8,9},{9,8},{10,11... | collective-permute-start | bytes 2359304 | tf_op jit(solution)/shard_map/ppermute | solution.py:913
  112.7 2.3 collective-permute-start.7
  137.5 2.3 collective-permute-start.9
  143.1 2.4 collective-permute-start.10
  143.6 5.7 %collective-permute-start.12 = (bf16[512,768]{1,0:T(8,128)(2,1)S(1)}, bf16[512,768]{1,0:T(8,128)(2,1)S(1)}, u32[]{:S(2)}, u32[]{:S(2)}) collective-permute-start(bf16[512,768]{1,0:T(8,128)(2,1)S(1)} %copy-done.31), channel_id=1, source_target_pairs={{0,1},{1,0},{2,3},{3,2},{4,5},{5,4},{6,7},{7,6},{8,9},{9,8},{10,11... | collective-permute-start | bytes 2359304 | tf_op jit(solution)/shard_map/ppermute | solution.py:913
  147.6 11.5 %collective-permute-start.11 = (bf16[192,1024]{1,0:T(8,128)(2,1)}, bf16[192,1024]{1,0:T(8,128)(2,1)}, u32[]{:S(2)}, u32[]{:S(2)}) collective-permute-start(bf16[192,1024]{1,0:T(8,128)(2,1)} %get-tuple-element.131), channel_id=1, source_target_pairs={{0,2},{1,3},{2,0},{3,1},{4,6},{5,7},{6,4},{7,5},{8,10},{9,11},{10,... | collective-permute-start | bytes 1179656 | tf_op jit(solution)/shard_map/ppermute | solution.py:913
  150.4 49.2 %all-to-all-start.2 = ((bf16[8,64,768]{2,1,0:T(8,128)(2,1)}), bf16[8,64,768]{2,1,0:T(8,128)(2,1)S(1)}, u32[]{:S(2)}, u32[]{:S(2)}) async-start(bf16[8,64,768]{2,1,0:T(8,128)(2,1)} %bitcast.40), calls=%async_computation.2 | async-start | bytes 1572864 | tf_op jit(solution)/shard_map/all_to_all | solution.py:916
  155.4 98.5 %reduce-scatter.5.cloned.1.call-start = ((), (), s32[]{:S(2)}) async-start(), calls=%async_computation.9 | async-start | bytes 1769472 | tf_op jit(solution)/shard_map/reduce_scatter | solution.py:934
  159.1 42.9 %copy-start.34 = (s32[257]{0:T(512)S(1)}, s32[257]{0:T(512)}, u32[]{:S(2)}) copy-start(s32[257]{0:T(512)} %param.27) | copy-start | bytes 3088
  199.7 3.0 %collective-permute-start.13 = (bf16[512,768]{1,0:T(8,128)(2,1)}, bf16[512,768]{1,0:T(8,128)(2,1)}, u32[]{:S(2)}, u32[]{:S(2)}) collective-permute-start(bf16[512,768]{1,0:T(8,128)(2,1)} %get-tuple-element.140), channel_id=1, source_target_pairs={{0,1},{1,0},{2,3},{3,2},{4,5},{5,4},{6,7},{7,6},{8,9},{9,8},{10,11... | collective-permute-start | bytes 2359304 | tf_op jit(solution)/shard_map/ppermute | solution.py:913
  205.1 20.2 %collective-permute-start.15 = (bf16[512,768]{1,0:T(8,128)(2,1)}, bf16[512,768]{1,0:T(8,128)(2,1)}, u32[]{:S(2)}, u32[]{:S(2)}) collective-permute-start(bf16[512,768]{1,0:T(8,128)(2,1)} %add_convert_fusion), channel_id=1, source_target_pairs={{0,2},{1,3},{2,0},{3,1},{4,6},{5,7},{6,4},{7,5},{8,10},{9,11},{10,... | collective-permute-start | bytes 2359304 | tf_op jit(solution)/shard_map/ppermute | solution.py:913
  205.6 19.7 %collective-permute-start.14 = (bf16[512,768]{1,0:T(8,128)(2,1)}, bf16[512,768]{1,0:T(8,128)(2,1)}, u32[]{:S(2)}, u32[]{:S(2)}) collective-permute-start(bf16[512,768]{1,0:T(8,128)(2,1)} %get-tuple-element.143), channel_id=1, source_target_pairs={{0,1},{1,0},{2,3},{3,2},{4,5},{5,4},{6,7},{7,6},{8,9},{9,8},{10,11... | collective-permute-start | bytes 2359304 | tf_op jit(solution)/shard_map/ppermute | solution.py:913
  213.2 3.7 %collective-permute-start.16 = (f32[15,128]{1,0:T(8,128)S(1)}, f32[15,128]{1,0:T(8,128)S(1)}, u32[]{:S(2)}, u32[]{:S(2)}) collective-permute-start(f32[15,128]{1,0:T(8,128)S(1)} %maximum_bitcast_fusion), channel_id=1, source_target_pairs={{0,4},{4,0},{8,12},{12,8},{16,20},{20,16},{24,28},{28,24},{1,5},{5... | collective-permute-start | bytes 23048 | tf_op jit(solution)/shard_map/ppermute | solution.py:921
  216.9 3.7 %collective-permute-start.17 = (f32[15,128]{1,0:T(8,128)S(1)}, f32[15,128]{1,0:T(8,128)S(1)}, u32[]{:S(2)}, u32[]{:S(2)}) collective-permute-start(f32[15,128]{1,0:T(8,128)S(1)} %fusion.17), channel_id=1, source_target_pairs={{0,8},{4,12},{8,0},{12,4},{16,24},{20,28},{24,16},{28,20},{1,9},{5... | collective-permute-start | bytes 23048 | tf_op jit(solution)/shard_map/ppermute | solution.py:921
  220.6 4.7 %collective-permute-start.18 = (f32[15,128]{1,0:T(8,128)S(1)}, f32[15,128]{1,0:T(8,128)S(1)}, u32[]{:S(2)}, u32[]{:S(2)}) collective-permute-start(f32[15,128]{1,0:T(8,128)S(1)} %fusion.18), channel_id=1, source_target_pairs={{0,16},{4,20},{8,24},{12,28},{16,0},{20,4},{24,8},{28,12},{1,17},{... | collective-permute-start | bytes 23048 | tf_op jit(solution)/shard_map/ppermute | solution.py:921
  229.7 31.4 %all-to-all-start.3 = ((bf16[8,64,768]{2,1,0:T(8,128)(2,1)}), bf16[8,64,768]{2,1,0:T(8,128)(2,1)S(1)}, u32[]{:S(2)}, u32[]{:S(2)}) async-start(bf16[8,64,768]{2,1,0:T(8,128)(2,1)} %bitcast.36), calls=%async_computation.3 | async-start | bytes 1572864 | tf_op jit(solution)/shard_map/all_to_all | solution.py:916
  234.5 8.2 %collective-permute-start.21 = (bf16[96,1536]{1,0:T(8,128)(2,1)S(1)}, bf16[96,1536]{1,0:T(8,128)(2,1)S(1)}, u32[]{:S(2)}, u32[]{:S(2)}) collective-permute-start(bf16[96,1536]{1,0:T(8,128)(2,1)S(1)} %pad_maximum_fusion.1), channel_id=1, source_target_pairs={{0,2},{1,3},{2,0},{3,1},{4,6},{5,7},{6,4},{7,5},{8,10},{9,11},{10,... | collective-permute-start | bytes 884744 | tf_op jit(solution)/shard_map/ppermute | solution.py:913
  235.9 1.2 collective-permute-start.20
  242.8 4.2 %collective-permute-start.22 = (f32[15,128]{1,0:T(8,128)S(1)}, f32[15,128]{1,0:T(8,128)S(1)}, u32[]{:S(2)}, u32[]{:S(2)}) collective-permute-start(f32[15,128]{1,0:T(8,128)S(1)} %add.77), channel_id=1, source_target_pairs={{0,2},{1,3},{2,0},{3,1},{4,6},{5,7},{6,4},{7,5},{8,10},{9,11},{10,... | collective-permute-start | bytes 23048 | tf_op jit(solution)/shard_map/ppermute | solution.py:913
  254.6 4.1 %collective-permute-start.19 = (bf16[96,192]{1,0:T(8,128)(2,1)S(1)}, bf16[96,192]{1,0:T(8,128)(2,1)S(1)}, u32[]{:S(2)}, u32[]{:S(2)}) collective-permute-start(bf16[96,192]{1,0:T(8,128)(2,1)S(1)} %slice.70), channel_id=1, source_target_pairs={{0,2},{1,3},{2,0},{3,1},{4,6},{5,7},{6,4},{7,5},{8,10},{9,11},{10,... | collective-permute-start | bytes 110600 | tf_op jit(solution)/shard_map/ppermute | solution.py:913
  (35 other events, 170.0 us)
Sparse Core Ops, SparseCore 0:
  10.1 51.9 all-gather.2
  63.7 39.4 all-gather.4
  136.5 70.0 reduce-scatter.2
  212.5 41.3 reduce-scatter.4

commit v3 on v2

--- a/solution.py
+++ b/solution.py
@@ -381,21 +381,32 @@
     rows_dev,
     info_ref,
     base_ref,
-    qkv_ref,
-    key_ref,
-    wide0_ref,
-    wide1_ref,
     lse0_ref,
     lse1_ref,
     grad0_ref,
     grad1_ref,
+    qkv_far,
+    wide0_far,
+    wide1_far,
+    key_far,
+    w_far,
+    diag_ref,
+    out_far,
+    far_send_far,
+    far_own_far,
+    near_send_far,
+    near_own_far,
+    qkv_ref,
+    wide0_ref,
+    wide1_ref,
+    key_ref,
     w_ref,
     out_ref,
-    diag_ref,
+    far_send_ref,
     far_own_ref,
-    far_send_ref,
+    near_send_ref,
     near_own_ref,
-    near_send_ref,
+    sems,
     lse_ref,
     inner_ref,
     grad_ref,
@@ -412,6 +423,28 @@
     cols = heads * HEAD_DIM
     first_len, me = info_ref[0, 0], info_ref[0, 2]
     tiles = rows // TILE
+    moves = [
+        pltpu.make_async_copy(source, target, sems.at[n])
+        for n, (source, target) in enumerate(
+            (
+                (qkv_far, qkv_ref),
+                (wide0_far, wide0_ref),
+                (wide1_far, wide1_ref),
+                (key_far, key_ref),
+                (w_far, w_ref),
+                (out_ref, out_far),
+                (far_send_ref, far_send_far),
+                (far_own_ref, far_own_far),
+                (near_send_ref, near_send_far),
+                (near_own_ref, near_own_far),
+            )
+        )
+    ]
+    for move in moves[:5]:
+        move.start()
+    key_acc[...] = jnp.zeros_like(key_acc)
+    value_acc[...] = jnp.zeros_like(value_acc)
+    table_ref[...] = jnp.zeros_like(table_ref)
     build_bias(base_ref, bias_ref, heads)
     query_seg = segment_all(rows, rows_dev, first_len, me, 0.0, NEG)
     q_of = [slice(h * HEAD_DIM, (h + 1) * HEAD_DIM) for h in range(heads)]
@@ -421,6 +454,8 @@
     lse_ref[:, rows // 2 :] = lse1_ref[...]
     grad_ref[:, : rows // 2] = grad0_ref[...]
     grad_ref[:, rows // 2 :] = grad1_ref[...]
+    for move in moves[:3]:
+        move.wait()
     for h in range(heads):
         queries = qkv_ref[q_of[h], :]
         query_ref[h] = jnp.concatenate([queries, query_seg], axis=0)
@@ -431,9 +466,7 @@
             at = slice(half * rows // 2, (half + 1) * rows // 2)
             terms = grad_ref[q_of[h], at].astype(F32) * wide_ref[q_of[h], :]
             inner_ref[h : h + 1, at] = jnp.sum(terms, axis=0, keepdims=True)
-    key_acc[...] = jnp.zeros_like(key_acc)
-    value_acc[...] = jnp.zeros_like(value_acc)
-    table_ref[...] = jnp.zeros_like(table_ref)
+    moves[3].wait()
 
     def query_tile(qb, carry):
         qs = pl.ds(tile_start(qb, rows_dev, me), TILE)
@@ -464,7 +497,7 @@
             return tuple(sums)
 
         sums = tuple(jnp.zeros((HEAD_DIM, TILE), F32) for _ in range(heads))
-        sums = over_tiles(low, high, tiles_at, sums, (2, 1))
+        sums = over_tiles(low, high, tiles_at, sums, (4, 2, 1))
         for h in range(heads):
             out_ref[q_of[h], qs] = sums[h].astype(BF16)
         return carry
@@ -473,14 +506,22 @@
     for h in range(heads):
         out_ref[k_of[h], :] = key_acc[h].astype(BF16).T
         out_ref[v_of[h], :] = value_acc[h].astype(BF16).T
+    moves[5].start()
+    moves[4].wait()
     grad_rows_to(far_own_ref, far_send_ref, rows // rows_dev // 2, out_ref, w_ref)
+    moves[6].start()
+    moves[7].start()
     grad_rows_to(near_own_ref, near_send_ref, 0, out_ref, w_ref)
+    moves[8].start()
+    moves[9].start()
     for i in range(heads * KINDS):
         if i % KINDS in (0, KINDS - 1):
             total = jnp.sum(table_ref[i], axis=0, keepdims=True)
             diag_ref[i : i + 1, :] = jnp.concatenate([total, jnp.zeros_like(total)], axis=1)
         else:
             diag_ref[i : i + 1, :] = diagonal_sums(table_ref[i])
+    for move in moves[5:]:
+        move.wait()
 
 
 def attend_back(info, base, qkv, keys, wide, lse, grad, weights, rows_dev):
@@ -488,16 +529,26 @@
     width = weights.shape[0]
     heads = qkv.shape[0] // (3 * HEAD_DIM)
     cols = heads * HEAD_DIM
-    return pl.pallas_call(
+    far = pl.BlockSpec(memory_space=pl.ANY)
+    half = [pltpu.VMEM((rows_dev, width), BF16)] * 4
+    out = pl.pallas_call(
         functools.partial(attend_back_kernel, heads, rows_dev),
         out_shape=(
+            jax.ShapeDtypeStruct((heads * KINDS, 2 * TILE), F32),
             jax.ShapeDtypeStruct((3 * cols, rows), BF16),
-            jax.ShapeDtypeStruct((heads * KINDS, 2 * TILE), F32),
             *[jax.ShapeDtypeStruct((rows_dev, width), BF16)] * 4,
         ),
-        in_specs=[SMEM] + [VMEM] * 10,
-        out_specs=(VMEM,) * 6,
+        in_specs=[SMEM] + [VMEM] * 5 + [far] * 5,
+        out_specs=(VMEM,) + (far,) * 5,
         scratch_shapes=[
+            pltpu.VMEM(qkv.shape, BF16),
+            pltpu.VMEM(wide[0].shape, F32),
+            pltpu.VMEM(wide[1].shape, F32),
+            pltpu.VMEM(keys.shape, BF16),
+            pltpu.VMEM(weights.shape, BF16),
+            pltpu.VMEM((3 * cols, rows), BF16),
+            *half,
+            pltpu.SemaphoreType.DMA((10,)),
             pltpu.VMEM((heads, rows), F32),
             pltpu.VMEM((heads, rows), F32),
             pltpu.VMEM((cols, rows), BF16),
@@ -510,10 +561,12 @@
             pltpu.VMEM((heads * KINDS, TILE, TILE), F32),
             pltpu.VMEM((heads * KINDS, TILE, TILE), F32),
         ],
-        compiler_params=pltpu.CompilerParams(vmem_limit_bytes=58 << 20),
+        compiler_params=pltpu.CompilerParams(vmem_limit_bytes=60 << 20),
         cost_estimate=LONG,
         name="attend_back",
-    )(info, base, qkv, keys, *wide, *lse, *grad, weights)
+    )(info, base, *lse, *grad, qkv, *wide, keys, weights)
+    diagonals, grad_qkv, far_send, far_own, near_send, near_own = out
+    return grad_qkv, diagonals, far_own, far_send, near_own, near_send
 
 
 def scaled_rows(values):
@@ -735,7 +788,9 @@
         functools.partial(ffn_kernel, ring),
         grid=(steps + 2 * (hidden // block),),
         out_shape=(
-            *[pltpu.HBM((half, width), BF16)] * 4,
+            pltpu.HBM((half, width), BF16),
+            pltpu.VMEM((half, width), BF16),
+            *[pltpu.HBM((half, width), BF16)] * 2,
             pltpu.HBM((width, 2 * hidden), BF16),
             pltpu.HBM((1, width), F32),
         ),

time: 273 us -> 271 us (level)
  Pallas kernels: 118 us -> 112 us
  starting transfers between devices: 32.8 us -> 37.3 us
    pallas_call x1, Pallas kernels: 40.6 us -> 36.5 us  [attend_back(): pl.pallas_call(functools.partial(attend_back_kernel, heads, rows_dev), ou...]
    ppermute x3, starting transfers between devices: 2.48 us -> 6.5 us  [sum_groups(): lax.ppermute(values, 'dp', [(i, i ^ step) for i in range(dp_size)])]
    ppermute x3, waiting for transfers between devices: 9.6 us -> 6.4 us  [sum_groups(): lax.ppermute(values, 'dp', [(i, i ^ step) for i in range(dp_size)])]
    all_gather x2, waiting for transfers between devices: 8.04 us -> 11.2 us  [gather(): lax.all_gather(values, both, axis=0, tiled=True, axis_index_groups=ring_g...]
    unnamed x75 -> x73, local copies, waits for them, and re-layouts: 12.2 us -> 11.1 us
  transfers between devices with their start and end apart: 31 -> 31, of which waited for: 18 -> 17; matrix products, arithmetic and copies ran while one was open for 7% -> 7% of each run, Pallas kernels for 34% -> 32%
where the time goes in v3:
time: 271 us; the launch traced here: 267 us
  Pallas kernels  112 us (41%)
  waiting for transfers between devices  73.9 us (27%)
  starting transfers between devices  37.3 us (14%)
  local copies, waits for them, and re-layouts  20.8 us (8%)
  between operations  14.4 us (5%)
  other arithmetic  6.36 us (2%)
    pallas_call x1, Pallas kernels, attend_back(): pl.pallas_call(functools.partial(attend_back_kernel, heads, rows_dev), ou...  36.5 us
    ppermute x20, waiting for transfers between devices, swap(): lax.ppermute(values, 'tensor', [(i, i ^ bit) for i in range(tensor_size)])  28.6 us
    all_to_all x4, starting transfers between devices, deal_out(): return lax.all_to_all(values, 'dp', split_axis=0, concat_axis=0, tiled=True)  24.3 us
    pallas_call x1, Pallas kernels, ffn(): pl.pallas_call(functools.partial(ffn_kernel, ring), grid=(steps + 2 * (hi...  21.2 us
    all_to_all x4, waiting for transfers between devices, deal_out(): return lax.all_to_all(values, 'dp', split_axis=0, concat_axis=0, tiled=True)  20.7 us
    pallas_call x1, Pallas kernels, attend_far(): pl.pallas_call(functools.partial(attend_far_kernel, heads, rows_dev), out...  14.2 us
    all_gather x2, waiting for transfers between devices, gather(): lax.all_gather(values, both, axis=0, tiled=True, axis_index_groups=ring_g...  11.2 us
    unnamed x73, local copies, waits for them, and re-layouts  11.1 us
  transfers between devices with their start and end apart: 31, of which 17 were waited for; matrix products, arithmetic and copies ran while one was open for 7% of the time, Pallas kernels for 32%

profile of v3, /device:TPU:12, one launch (start us, length us, event | category | flops | bytes accessed | tf_op | source)
XLA Modules:
  0.0 267.0 jit_solution(2213134914636010125)
XLA Ops:
  7.2 2.2 pack_weights.1
  10.2 2.7 %gather_fusion = bf16[512,768]{1,0:T(8,128)(2,1)} fusion(bf16[512,768]{1,0:T(8,128)(2,1)S(1)} %copy-done, s32[1024]{0:T(1024)S(1)} %pad_clamp_fusion), kind=kCustom, calls=%fused_computation | custom fusion | bytes 1574912 | tf_op jit(solution)/shard_map/gather | solution.py:1001
  12.9 6.4 %all-to-all-start = ((bf16[8,64,768]{2,1,0:T(8,128)(2,1)}), bf16[8,64,768]{2,1,0:T(8,128)(2,1)S(1)}, u32[]{:S(2)}, u32[]{:S(2)}) async-start(bf16[8,64,768]{2,1,0:T(8,128)(2,1)} %bitcast.1), calls=%async_computation | async-start | bytes 1572864 | tf_op jit(solution)/shard_map/all_to_all | solution.py:971
  19.8 5.6 %collective-permute-done = bf16[96,960]{1,0:T(8,128)(2,1)S(1)} collective-permute-done((bf16[96,960]{1,0:T(8,128)(2,1)S(1)}, bf16[96,960]{1,0:T(8,128)(2,1)S(1)}, u32[]{:S(2)}, u32[]{:S(2)}) %collective-permute-start) | collective-permute-done | bytes 184352 | tf_op jit(solution)/shard_map/ppermute | solution.py:968
  25.4 20.7 %all-to-all-done = bf16[8,64,768]{2,1,0:T(8,128)(2,1)S(1)} async-done(((bf16[8,64,768]{2,1,0:T(8,128)(2,1)}), bf16[8,64,768]{2,1,0:T(8,128)(2,1)S(1)}, u32[]{:S(2)}, u32[]{:S(2)}) %all-to-all-start) | async-done | bytes 786464 | tf_op jit(solution)/shard_map/all_to_all | solution.py:971
  48.0 2.7 %gather_fusion.1 = bf16[512,768]{1,0:T(8,128)(2,1)} fusion(bf16[512,768]{1,0:T(8,128)(2,1)S(1)} %copy-done.19, s32[1024]{0:T(1024)S(1)} %pad_clamp_fusion), kind=kCustom, calls=%fused_computation.1 | custom fusion | bytes 1574912 | tf_op jit(solution)/shard_map/gather | solution.py:1027
  50.7 6.1 %all-to-all-start.1 = ((bf16[8,64,768]{2,1,0:T(8,128)(2,1)}), bf16[8,64,768]{2,1,0:T(8,128)(2,1)S(1)}, u32[]{:S(2)}, u32[]{:S(2)}) async-start(bf16[8,64,768]{2,1,0:T(8,128)(2,1)} %bitcast.39), calls=%async_computation.1 | async-start | bytes 1572864 | tf_op jit(solution)/shard_map/all_to_all | solution.py:971
  62.1 3.6 %unring.2 = (bf16[768,576]{1,0:T(8,128)(2,1)}, bf16[768,768]{1,0:T(8,128)(2,1)}, bf16[192,768]{1,0:T(8,128)(2,1)}) custom-call(bf16[768,1536]{1,0:T(8,128)(2,1)} %all-gather.3.cloned.1.call-done.found_ref), custom_call_target="tpu_custom_call" | custom-call | flops 1048576 | bytes 65536 | tf_op jit(solution)/shard_map/unring/pallas_call | solution.py:130
  66.2 2.0 collective-permute-done.3.slot3_ref
  69.1 14.2 %attend_far.1 = (bf16[192,1024]{1,0:T(8,128)(2,1)}, f32[192,1024]{1,0:T(8,128)}, f32[3,1024]{1,0:T(4,128)}, bf16[576,2048]{1,0:T(8,128)(2,1)}, bf16[3,2048,128]{2,1,0:T(8,128)(2,1)}) custom-call(s32[1,3]{1,0:T(1,128)} %pad_add_fusion.info_ref, f32[15,512]{1,0:T(8,128)} %reshape.102.base_ref, bf16[768,576]{1,0:T(8,128)(2,1)} %get-tuple-element.101.w_ref.w_far, ...), custom_call_target="tpu_custom_call" | custom-call | flops 1048576 | bytes 65536 | tf_op jit(solution)/shard_map/attend_far/pallas_call | solution.py:331
  83.3 10.5 %attend_near.1 = (bf16[192,1024]{1,0:T(8,128)(2,1)}, f32[192,1024]{1,0:T(8,128)}, f32[3,1024]{1,0:T(4,128)}) custom-call(s32[1,3]{1,0:T(1,128)} %pad_add_fusion.info_ref, f32[15,512]{1,0:T(8,128)} %reshape.102.base_ref, bf16[576,2048]{1,0:T(8,128)(2,1)} %get-tuple-element.104.qkv_ref.qkv_far, bf16[3,2048,128]{2,1,0:T(8,128)(2,1)} %get-tuple-element.105.key_ref.key_far), custom_call_target="tpu_custom_call" | custom-call | flops 1048576 | bytes 65536 | tf_op jit(solution)/shard_map/attend_near/pallas_call | solution.py:349
  93.9 9.3 %all-gather.5.cloned.1.call-done.found_ref = bf16[768,1728]{1,0:T(8,128)(2,1)} async-done(((bf16[96,1728]{1,0:T(8,128)(2,1)}), bf16[768,1728]{1,0:T(8,128)(2,1)}) %all-gather.5.cloned.1.call-update) | async-done | bytes 2654224 | tf_op jit(solution)/shard_map/all_gather | solution.py:985
  103.2 3.4 %unring.3 = (bf16[768,768]{1,0:T(8,128)(2,1)}, bf16[768,768]{1,0:T(8,128)(2,1)}, bf16[192,768]{1,0:T(8,128)(2,1)}) custom-call(bf16[768,1728]{1,0:T(8,128)(2,1)} %all-gather.5.cloned.1.call-done.found_ref), custom_call_target="tpu_custom_call" | custom-call | flops 1048576 | bytes 65536 | tf_op jit(solution)/shard_map/unring/pallas_call | solution.py:130
  112.9 2.1 collective-permute-done.7.normed1
  115.0 21.2 %ffn.1 = (bf16[512,768]{1,0:T(8,128)(2,1)}, bf16[512,768]{1,0:T(8,128)(2,1)S(1)}, bf16[512,768]{1,0:T(8,128)(2,1)}, bf16[512,768]{1,0:T(8,128)(2,1)}, bf16[768,3072]{1,0:T(8,128)(2,1)}, /*index=5*/f32[1,768]{1,0:T(1,128)}) custom-call(bf16[512,768]{1,0:T(8,128)(2,1)S(1)} %get-tuple-element.119.normed0, bf16[512,768]{1,0:T(8,128)(2,1)S(1)} %collective-permute-done.7.normed1, ...), custom_call_target="tpu_custom_call" | custom-call | flops 1048576 | bytes 65536 | tf_op jit(solution)/shard_map/ffn/pallas_call | solution.py:787
  136.4 2.2 collective-permute-done.9.far_ref
  149.2 5.0 %all-to-all-start.2 = ((bf16[8,64,768]{2,1,0:T(8,128)(2,1)}), bf16[8,64,768]{2,1,0:T(8,128)(2,1)S(1)}, u32[]{:S(2)}, u32[]{:S(2)}) async-start(bf16[8,64,768]{2,1,0:T(8,128)(2,1)} %bitcast.40), calls=%async_computation.2 | async-start | bytes 1572864 | tf_op jit(solution)/shard_map/all_to_all | solution.py:971
  154.2 3.7 %collective-permute-done.11.grad1_ref = bf16[192,1024]{1,0:T(8,128)(2,1)} collective-permute-done((bf16[192,1024]{1,0:T(8,128)(2,1)}, bf16[192,1024]{1,0:T(8,128)(2,1)}, u32[]{:S(2)}, u32[]{:S(2)}) %collective-permute-start.11) | collective-permute-done | bytes 393248 | tf_op jit(solution)/shard_map/ppermute | solution.py:968
  157.9 36.5 %attend_back.1 = (f32[15,512]{1,0:T(8,128)}, bf16[576,2048]{1,0:T(8,128)(2,1)}, bf16[512,768]{1,0:T(8,128)(2,1)}, bf16[512,768]{1,0:T(8,128)(2,1)}, bf16[512,768]{1,0:T(8,128)(2,1)}, /*index=5*/bf16[512,768]{1,0:T(8,128)(2,1)}) custom-call(s32[1,3]{1,0:T(1,128)} %pad_add_fusion.info_ref, f32[15,512]{1,0:T(8,128)} %reshape.102.base_ref, ...), custom_call_target="tpu_custom_call" | custom-call | flops 25769803776 | bytes 67108864 | tf_op jit(solution)/shard_map/attend_back/pallas_call | solution.py:534
  197.7 2.5 add_convert_fusion
  200.8 6.4 %qkv_grads.1 = (bf16[768,960]{1,0:T(8,128)(2,1)}, f32[1,768]{1,0:T(1,128)}) custom-call(bf16[576,2048]{1,0:T(8,128)(2,1)} %get-tuple-element.147.grad_ref, bf16[512,768]{1,0:T(8,128)(2,1)} %copy-done.20, bf16[512,768]{1,0:T(8,128)(2,1)} %collective-permute-done.2.slot1_ref, bf16[512,768]{1,0:T(8,128)(2,1)} %collective-permute-done.1.slot2_ref, ...), custom_call_target="tpu_custom_call" | custom-call | flops 1048576 | bytes 65536 | tf_op jit(solution)/shard_map/qkv_grads/pallas_call | solution.py:867
  209.3 2.5 collective-permute-done.16
  211.8 3.0 %collective-permute-start.17 = (f32[15,128]{1,0:T(8,128)S(1)}, f32[15,128]{1,0:T(8,128)S(1)}, u32[]{:S(2)}, u32[]{:S(2)}) collective-permute-start(f32[15,128]{1,0:T(8,128)S(1)} %fusion.17), channel_id=1, source_target_pairs={{0,8},{4,12},{8,0},{12,4},{16,24},{20,28},{24,16},{28,20},{1,9},{5... | collective-permute-start | bytes 23048 | tf_op jit(solution)/shard_map/ppermute | solution.py:976
  216.4 2.3 collective-permute-start.18
  218.8 2.3 collective-permute-done.18
  222.2 2.3 rows_back.1
  225.4 6.9 %all-to-all-start.3 = ((bf16[8,64,768]{2,1,0:T(8,128)(2,1)}), bf16[8,64,768]{2,1,0:T(8,128)(2,1)S(1)}, u32[]{:S(2)}, u32[]{:S(2)}) async-start(bf16[8,64,768]{2,1,0:T(8,128)(2,1)} %bitcast.36), calls=%async_computation.3 | async-start | bytes 1572864 | tf_op jit(solution)/shard_map/all_to_all | solution.py:971
  234.9 5.6 %collective-permute-done.21.taken_ref = bf16[96,1536]{1,0:T(8,128)(2,1)S(1)} collective-permute-done((bf16[96,1536]{1,0:T(8,128)(2,1)S(1)}, bf16[96,1536]{1,0:T(8,128)(2,1)S(1)}, u32[]{:S(2)}, u32[]{:S(2)}) %collective-permute-start.21) | collective-permute-done | bytes 294944 | tf_op jit(solution)/shard_map/ppermute | solution.py:968
  242.6 2.0 finish.1
  244.6 6.9 %reduce-scatter.5.cloned.1.call-done.last_ref = bf16[96,960]{1,0:T(8,128)(2,1)} async-done(((bf16[768,960]{1,0:T(8,128)(2,1)}), bf16[96,960]{1,0:T(8,128)(2,1)}) %reduce-scatter.5.cloned.1.call-update) | async-done | bytes 184336 | tf_op jit(solution)/shard_map/reduce_scatter | solution.py:989
  253.7 2.7 %collective-permute-done.19.far_ref = bf16[96,192]{1,0:T(8,128)(2,1)S(1)} collective-permute-done((bf16[96,192]{1,0:T(8,128)(2,1)S(1)}, bf16[96,192]{1,0:T(8,128)(2,1)S(1)}, u32[]{:S(2)}, u32[]{:S(2)}) %collective-permute-start.19) | collective-permute-done | bytes 36896 | tf_op jit(solution)/shard_map/ppermute | solution.py:968
  257.0 1.8 finish_last.1
  (179 shorter events, 45.3 us)
Async XLA Ops:
  7.2 55.0 %all-gather.3.cloned.1.call-start = ((), (), s32[]{:S(2)}) async-start(), calls=%async_computation.6 | async-start | bytes 2654208 | tf_op jit(solution)/shard_map/all_gather | solution.py:985
  12.9 33.2 %all-to-all-start = ((bf16[8,64,768]{2,1,0:T(8,128)(2,1)}), bf16[8,64,768]{2,1,0:T(8,128)(2,1)S(1)}, u32[]{:S(2)}, u32[]{:S(2)}) async-start(bf16[8,64,768]{2,1,0:T(8,128)(2,1)} %bitcast.1), calls=%async_computation | async-start | bytes 1572864 | tf_op jit(solution)/shard_map/all_to_all | solution.py:971
  19.3 84.0 %all-gather.5.cloned.1.call-start = ((), (), s32[]{:S(2)}) async-start(), calls=%async_computation.7 | async-start | bytes 3096576 | tf_op jit(solution)/shard_map/all_gather | solution.py:985
  19.3 6.1 %collective-permute-start = (bf16[96,960]{1,0:T(8,128)(2,1)S(1)}, bf16[96,960]{1,0:T(8,128)(2,1)S(1)}, u32[]{:S(2)}, u32[]{:S(2)}) collective-permute-start(bf16[96,960]{1,0:T(8,128)(2,1)S(1)} %copy-done.25), channel_id=1, source_target_pairs={{0,2},{1,3},{2,0},{3,1},{4,6},{5,7},{6,4},{7,5},{8,10},{9,11},{10,... | collective-permute-start | bytes 552968 | tf_op jit(solution)/shard_map/ppermute | solution.py:968
  47.4 18.3 %collective-permute-start.1 = (bf16[512,768]{1,0:T(8,128)(2,1)S(1)}, bf16[512,768]{1,0:T(8,128)(2,1)}, u32[]{:S(2)}, u32[]{:S(2)}) collective-permute-start(bf16[512,768]{1,0:T(8,128)(2,1)S(1)} %fusion.3.slot0_ref), channel_id=1, source_target_pairs={{0,2},{1,3},{2,0},{3,1},{4,6},{5,7},{6,4},{7,5},{8,10},{9,11},{10,... | collective-permute-start | bytes 2359304 | tf_op jit(solution)/shard_map/ppermute | solution.py:968
  50.7 32.6 %all-to-all-start.1 = ((bf16[8,64,768]{2,1,0:T(8,128)(2,1)}), bf16[8,64,768]{2,1,0:T(8,128)(2,1)S(1)}, u32[]{:S(2)}, u32[]{:S(2)}) async-start(bf16[8,64,768]{2,1,0:T(8,128)(2,1)} %bitcast.39), calls=%async_computation.1 | async-start | bytes 1572864 | tf_op jit(solution)/shard_map/all_to_all | solution.py:971
  56.8 150.4 %reduce-scatter.3.cloned.1.call-start = ((), (), s32[]{:S(2)}) async-start(), calls=%async_computation.8 | async-start | bytes 5308416 | tf_op jit(solution)/shard_map/reduce_scatter | solution.py:989
  60.3 5.9 %collective-permute-start.2 = (bf16[512,768]{1,0:T(8,128)(2,1)S(1)}, bf16[512,768]{1,0:T(8,128)(2,1)}, u32[]{:S(2)}, u32[]{:S(2)}) collective-permute-start(bf16[512,768]{1,0:T(8,128)(2,1)S(1)} %fusion.3.slot0_ref), channel_id=1, source_target_pairs={{0,1},{1,0},{2,3},{3,2},{4,5},{5,4},{6,7},{7,6},{8,9},{9,8},{10,11... | collective-permute-start | bytes 2359304 | tf_op jit(solution)/shard_map/ppermute | solution.py:968
  65.7 2.5 collective-permute-start.3
  65.7 40.9 %collective-permute-start.4 = (bf16[768,768]{1,0:T(8,128)(2,1)}, bf16[768,768]{1,0:T(8,128)(2,1)}, u32[]{:S(2)}, u32[]{:S(2)}) collective-permute-start(bf16[768,768]{1,0:T(8,128)(2,1)} %get-tuple-element.109.outer0), channel_id=1, source_target_pairs={{0,2},{1,3},{2,0},{3,1},{4,6},{5,7},{6,4},{7,5},{8,10},{9,11},{10,... | collective-permute-start | bytes 3538952 | tf_op jit(solution)/shard_map/ppermute | solution.py:968
  83.3 23.3 %collective-permute-start.5 = (bf16[192,1024]{1,0:T(8,128)(2,1)}, bf16[192,1024]{1,0:T(8,128)(2,1)S(1)}, u32[]{:S(2)}, u32[]{:S(2)}) collective-permute-start(bf16[192,1024]{1,0:T(8,128)(2,1)} %get-tuple-element.113), channel_id=1, source_target_pairs={{0,2},{1,3},{2,0},{3,1},{4,6},{5,7},{6,4},{7,5},{8,10},{9,11},{10,... | collective-permute-start | bytes 1179656 | tf_op jit(solution)/shard_map/ppermute | solution.py:968
  108.7 2.4 collective-permute-start.6
  108.8 4.1 %collective-permute-start.8 = (bf16[512,768]{1,0:T(8,128)(2,1)S(1)}, bf16[512,768]{1,0:T(8,128)(2,1)S(1)}, u32[]{:S(2)}, u32[]{:S(2)}) collective-permute-start(bf16[512,768]{1,0:T(8,128)(2,1)S(1)} %bitcast.31), channel_id=1, source_target_pairs={{0,1},{1,0},{2,3},{3,2},{4,5},{5,4},{6,7},{7,6},{8,9},{9,8},{10,11... | collective-permute-start | bytes 2359304 | tf_op jit(solution)/shard_map/ppermute | solution.py:968
  112.7 2.3 collective-permute-start.7
  136.2 2.4 collective-permute-start.9
  141.9 2.4 collective-permute-start.10
  142.3 5.6 %collective-permute-start.12 = (bf16[512,768]{1,0:T(8,128)(2,1)S(1)}, bf16[512,768]{1,0:T(8,128)(2,1)S(1)}, u32[]{:S(2)}, u32[]{:S(2)}) collective-permute-start(bf16[512,768]{1,0:T(8,128)(2,1)S(1)} %copy-done.31), channel_id=1, source_target_pairs={{0,1},{1,0},{2,3},{3,2},{4,5},{5,4},{6,7},{7,6},{8,9},{9,8},{10,11... | collective-permute-start | bytes 2359304 | tf_op jit(solution)/shard_map/ppermute | solution.py:968
  146.5 11.5 %collective-permute-start.11 = (bf16[192,1024]{1,0:T(8,128)(2,1)}, bf16[192,1024]{1,0:T(8,128)(2,1)}, u32[]{:S(2)}, u32[]{:S(2)}) collective-permute-start(bf16[192,1024]{1,0:T(8,128)(2,1)} %get-tuple-element.129), channel_id=1, source_target_pairs={{0,2},{1,3},{2,0},{3,1},{4,6},{5,7},{6,4},{7,5},{8,10},{9,11},{10,... | collective-permute-start | bytes 1179656 | tf_op jit(solution)/shard_map/ppermute | solution.py:968
  149.2 45.2 %all-to-all-start.2 = ((bf16[8,64,768]{2,1,0:T(8,128)(2,1)}), bf16[8,64,768]{2,1,0:T(8,128)(2,1)S(1)}, u32[]{:S(2)}, u32[]{:S(2)}) async-start(bf16[8,64,768]{2,1,0:T(8,128)(2,1)} %bitcast.40), calls=%async_computation.2 | async-start | bytes 1572864 | tf_op jit(solution)/shard_map/all_to_all | solution.py:971
  154.2 97.3 %reduce-scatter.5.cloned.1.call-start = ((), (), s32[]{:S(2)}) async-start(), calls=%async_computation.9 | async-start | bytes 1769472 | tf_op jit(solution)/shard_map/reduce_scatter | solution.py:989
  157.9 38.8 %copy-start.33 = (s32[257]{0:T(512)S(1)}, s32[257]{0:T(512)}, u32[]{:S(2)}) copy-start(s32[257]{0:T(512)} %param.27) | copy-start | bytes 3088
  194.5 3.2 %collective-permute-start.13 = (bf16[512,768]{1,0:T(8,128)(2,1)}, bf16[512,768]{1,0:T(8,128)(2,1)}, u32[]{:S(2)}, u32[]{:S(2)}) collective-permute-start(bf16[512,768]{1,0:T(8,128)(2,1)} %get-tuple-element.140), channel_id=1, source_target_pairs={{0,1},{1,0},{2,3},{3,2},{4,5},{5,4},{6,7},{7,6},{8,9},{9,8},{10,11... | collective-permute-start | bytes 2359304 | tf_op jit(solution)/shard_map/ppermute | solution.py:968
  200.1 20.9 %collective-permute-start.15 = (bf16[512,768]{1,0:T(8,128)(2,1)}, bf16[512,768]{1,0:T(8,128)(2,1)}, u32[]{:S(2)}, u32[]{:S(2)}) collective-permute-start(bf16[512,768]{1,0:T(8,128)(2,1)} %add_convert_fusion), channel_id=1, source_target_pairs={{0,2},{1,3},{2,0},{3,1},{4,6},{5,7},{6,4},{7,5},{8,10},{9,11},{10,... | collective-permute-start | bytes 2359304 | tf_op jit(solution)/shard_map/ppermute | solution.py:968
  200.5 20.6 %collective-permute-start.14 = (bf16[512,768]{1,0:T(8,128)(2,1)}, bf16[512,768]{1,0:T(8,128)(2,1)}, u32[]{:S(2)}, u32[]{:S(2)}) collective-permute-start(bf16[512,768]{1,0:T(8,128)(2,1)} %get-tuple-element.143), channel_id=1, source_target_pairs={{0,1},{1,0},{2,3},{3,2},{4,5},{5,4},{6,7},{7,6},{8,9},{9,8},{10,11... | collective-permute-start | bytes 2359304 | tf_op jit(solution)/shard_map/ppermute | solution.py:968
  208.1 3.7 %collective-permute-start.16 = (f32[15,128]{1,0:T(8,128)S(1)}, f32[15,128]{1,0:T(8,128)S(1)}, u32[]{:S(2)}, u32[]{:S(2)}) collective-permute-start(f32[15,128]{1,0:T(8,128)S(1)} %maximum_bitcast_fusion), channel_id=1, source_target_pairs={{0,4},{4,0},{8,12},{12,8},{16,20},{20,16},{24,28},{28,24},{1,5},{5... | collective-permute-start | bytes 23048 | tf_op jit(solution)/shard_map/ppermute | solution.py:976
  211.8 4.6 %collective-permute-start.17 = (f32[15,128]{1,0:T(8,128)S(1)}, f32[15,128]{1,0:T(8,128)S(1)}, u32[]{:S(2)}, u32[]{:S(2)}) collective-permute-start(f32[15,128]{1,0:T(8,128)S(1)} %fusion.17), channel_id=1, source_target_pairs={{0,8},{4,12},{8,0},{12,4},{16,24},{20,28},{24,16},{28,20},{1,9},{5... | collective-permute-start | bytes 23048 | tf_op jit(solution)/shard_map/ppermute | solution.py:976
  216.4 4.6 %collective-permute-start.18 = (f32[15,128]{1,0:T(8,128)S(1)}, f32[15,128]{1,0:T(8,128)S(1)}, u32[]{:S(2)}, u32[]{:S(2)}) collective-permute-start(f32[15,128]{1,0:T(8,128)S(1)} %fusion.18), channel_id=1, source_target_pairs={{0,16},{4,20},{8,24},{12,28},{16,0},{20,4},{24,8},{28,12},{1,17},{... | collective-permute-start | bytes 23048 | tf_op jit(solution)/shard_map/ppermute | solution.py:976
  225.4 33.4 %all-to-all-start.3 = ((bf16[8,64,768]{2,1,0:T(8,128)(2,1)}), bf16[8,64,768]{2,1,0:T(8,128)(2,1)S(1)}, u32[]{:S(2)}, u32[]{:S(2)}) async-start(bf16[8,64,768]{2,1,0:T(8,128)(2,1)} %bitcast.36), calls=%async_computation.3 | async-start | bytes 1572864 | tf_op jit(solution)/shard_map/all_to_all | solution.py:971
  232.3 8.1 %collective-permute-start.21 = (bf16[96,1536]{1,0:T(8,128)(2,1)S(1)}, bf16[96,1536]{1,0:T(8,128)(2,1)S(1)}, u32[]{:S(2)}, u32[]{:S(2)}) collective-permute-start(bf16[96,1536]{1,0:T(8,128)(2,1)S(1)} %pad_maximum_fusion.1), channel_id=1, source_target_pairs={{0,2},{1,3},{2,0},{3,1},{4,6},{5,7},{6,4},{7,5},{8,10},{9,11},{10,... | collective-permute-start | bytes 884744 | tf_op jit(solution)/shard_map/ppermute | solution.py:968
  233.7 1.2 collective-permute-start.20
  240.5 4.1 %collective-permute-start.22 = (f32[15,128]{1,0:T(8,128)S(1)}, f32[15,128]{1,0:T(8,128)S(1)}, u32[]{:S(2)}, u32[]{:S(2)}) collective-permute-start(f32[15,128]{1,0:T(8,128)S(1)} %add.77), channel_id=1, source_target_pairs={{0,2},{1,3},{2,0},{3,1},{4,6},{5,7},{6,4},{7,5},{8,10},{9,11},{10,... | collective-permute-start | bytes 23048 | tf_op jit(solution)/shard_map/ppermute | solution.py:968
  252.3 4.1 %collective-permute-start.19 = (bf16[96,192]{1,0:T(8,128)(2,1)S(1)}, bf16[96,192]{1,0:T(8,128)(2,1)S(1)}, u32[]{:S(2)}, u32[]{:S(2)}) collective-permute-start(bf16[96,192]{1,0:T(8,128)(2,1)S(1)} %slice.70), channel_id=1, source_target_pairs={{0,2},{1,3},{2,0},{3,1},{4,6},{5,7},{6,4},{7,5},{8,10},{9,11},{10,... | collective-permute-start | bytes 110600 | tf_op jit(solution)/shard_map/ppermute | solution.py:968
  (34 other events, 181.9 us)
Sparse Core Ops, SparseCore 0:
  10.1 51.9 all-gather.2
  63.7 39.4 all-gather.4
  136.4 70.0 reduce-scatter.2
  208.6 42.8 reduce-scatter.4

commit v4 on v3

--- a/solution.py
+++ b/solution.py
@@ -32,6 +32,18 @@
 def contract(left, left_dim, right, right_dim):
     return lax.dot_general(
         left, right, (((left_dim,), (right_dim,)), ((), ())), preferred_element_type=F32
+    )
+
+
+def chosen(values, order):
+    dims = lax.GatherDimensionNumbers((1,), (0,), (0,))
+    return lax.gather(
+        values,
+        order[:, None],
+        dims,
+        (1, values.shape[1]),
+        unique_indices=True,
+        mode=lax.GatherScatterMode.PROMISE_IN_BOUNDS,
     )
 
 
@@ -998,7 +1010,7 @@
     front, outer_own, proj_own = gather(
         own_front, ((0, ends[0], False), (ends[0], ends[1], False), (ends[1], ends[2], True))
     )
-    low_rows = deal_out(tokens.at[deal].get(mode="promise_in_bounds", unique_indices=True))
+    low_rows = deal_out(chosen(tokens, deal))
     other_rest, low_rows = after(swap(own_rest, 2), low_rows)
     inner_own, inner_other, proj_other = gather(
         jnp.concatenate([own_rest[:, :hidden], other_rest], axis=1),
@@ -1024,7 +1036,7 @@
     slots = (slot0, slot1, slot2, slot3)
     outer_other = swap(outer_own, 2)
 
-    low_grads = deal_out(cotangent.at[deal].get(mode="promise_in_bounds", unique_indices=True))
+    low_grads = deal_out(chosen(cotangent, deal))
 
     mixed_far, wide_far, lse_far, qkv, keys = attend_far(info, base, front, slots)
     mixed_other = swap(mixed_far, 2)

time: 271 us -> 271 us (level)
  no operation moved by 1% of the time
where the time goes in v4:
time: 271 us; the launch traced here: 267 us
  Pallas kernels  112 us (41%)
  waiting for transfers between devices  73 us (27%)
  starting transfers between devices  38.7 us (14%)
  local copies, waits for them, and re-layouts  20.6 us (8%)
  between operations  14.4 us (5%)
  other arithmetic  6.35 us (2%)
    pallas_call x1, Pallas kernels, attend_back(): pl.pallas_call(functools.partial(attend_back_kernel, heads, rows_dev), ou...  36.5 us
    ppermute x20, waiting for transfers between devices, swap(): lax.ppermute(values, 'tensor', [(i, i ^ bit) for i in range(tensor_size)])  28.5 us
    all_to_all x4, starting transfers between devices, deal_out(): return lax.all_to_all(values, 'dp', split_axis=0, concat_axis=0, tiled=True)  24 us
    pallas_call x1, Pallas kernels, ffn(): pl.pallas_call(functools.partial(ffn_kernel, ring), grid=(steps + 2 * (hi...  21.2 us
    all_to_all x4, waiting for transfers between devices, deal_out(): return lax.all_to_all(values, 'dp', split_axis=0, concat_axis=0, tiled=True)  20.7 us
    pallas_call x1, Pallas kernels, attend_far(): pl.pallas_call(functools.partial(attend_far_kernel, heads, rows_dev), out...  13.4 us
    pallas_call x1, Pallas kernels, attend_near(): pl.pallas_call(functools.partial(attend_near_kernel, heads, rows_dev), ou...  11.3 us
    unnamed x73, local copies, waits for them, and re-layouts  10.9 us
  transfers between devices with their start and end apart: 31, of which 17 were waited for; matrix products, arithmetic and copies ran while one was open for 7% of the time, Pallas kernels for 32%

profile of v4, /device:TPU:12, one launch (start us, length us, event | category | flops | bytes accessed | tf_op | source)
XLA Modules:
  0.0 267.5 jit_solution(10485785453365138492)
XLA Ops:
  7.2 2.2 pack_weights.1
  10.1 2.7 %gather_fusion = bf16[512,768]{1,0:T(8,128)(2,1)} fusion(bf16[512,768]{1,0:T(8,128)(2,1)S(1)} %copy-done, s32[1024]{0:T(1024)S(1)} %pad_clamp_fusion), kind=kCustom, calls=%fused_computation | custom fusion | bytes 1574912 | tf_op jit(solution)/shard_map/gather | solution.py:40
  12.9 6.4 %all-to-all-start = ((bf16[8,64,768]{2,1,0:T(8,128)(2,1)}), bf16[8,64,768]{2,1,0:T(8,128)(2,1)S(1)}, u32[]{:S(2)}, u32[]{:S(2)}) async-start(bf16[8,64,768]{2,1,0:T(8,128)(2,1)} %bitcast.1), calls=%async_computation | async-start | bytes 1572864 | tf_op jit(solution)/shard_map/all_to_all | solution.py:983
  19.8 5.6 %collective-permute-done = bf16[96,960]{1,0:T(8,128)(2,1)S(1)} collective-permute-done((bf16[96,960]{1,0:T(8,128)(2,1)S(1)}, bf16[96,960]{1,0:T(8,128)(2,1)S(1)}, u32[]{:S(2)}, u32[]{:S(2)}) %collective-permute-start) | collective-permute-done | bytes 184352 | tf_op jit(solution)/shard_map/ppermute | solution.py:980
  25.4 20.7 %all-to-all-done = bf16[8,64,768]{2,1,0:T(8,128)(2,1)S(1)} async-done(((bf16[8,64,768]{2,1,0:T(8,128)(2,1)}), bf16[8,64,768]{2,1,0:T(8,128)(2,1)S(1)}, u32[]{:S(2)}, u32[]{:S(2)}) %all-to-all-start) | async-done | bytes 786464 | tf_op jit(solution)/shard_map/all_to_all | solution.py:983
  48.0 2.7 %gather_fusion.1 = bf16[512,768]{1,0:T(8,128)(2,1)} fusion(bf16[512,768]{1,0:T(8,128)(2,1)S(1)} %copy-done.19, s32[1024]{0:T(1024)S(1)} %pad_clamp_fusion), kind=kCustom, calls=%fused_computation.1 | custom fusion | bytes 1574912 | tf_op jit(solution)/shard_map/gather | solution.py:40
  50.7 6.1 %all-to-all-start.1 = ((bf16[8,64,768]{2,1,0:T(8,128)(2,1)}), bf16[8,64,768]{2,1,0:T(8,128)(2,1)S(1)}, u32[]{:S(2)}, u32[]{:S(2)}) async-start(bf16[8,64,768]{2,1,0:T(8,128)(2,1)} %bitcast.39), calls=%async_computation.1 | async-start | bytes 1572864 | tf_op jit(solution)/shard_map/all_to_all | solution.py:983
  60.3 1.8 all-gather.3.cloned.1.call-done.found_ref
  62.2 3.6 %unring.2 = (bf16[768,576]{1,0:T(8,128)(2,1)}, bf16[768,768]{1,0:T(8,128)(2,1)}, bf16[192,768]{1,0:T(8,128)(2,1)}) custom-call(bf16[768,1536]{1,0:T(8,128)(2,1)} %all-gather.3.cloned.1.call-done.found_ref), custom_call_target="tpu_custom_call" | custom-call | flops 1048576 | bytes 65536 | tf_op jit(solution)/shard_map/unring/pallas_call | solution.py:142
  66.2 2.0 collective-permute-done.3.slot3_ref
  69.1 13.4 %attend_far.1 = (bf16[192,1024]{1,0:T(8,128)(2,1)}, f32[192,1024]{1,0:T(8,128)}, f32[3,1024]{1,0:T(4,128)}, bf16[576,2048]{1,0:T(8,128)(2,1)}, bf16[3,2048,128]{2,1,0:T(8,128)(2,1)}) custom-call(s32[1,3]{1,0:T(1,128)} %pad_add_fusion.info_ref, f32[15,512]{1,0:T(8,128)} %reshape.102.base_ref, bf16[768,576]{1,0:T(8,128)(2,1)} %get-tuple-element.101.w_ref.w_far, ...), custom_call_target="tpu_custom_call" | custom-call | flops 1048576 | bytes 65536 | tf_op jit(solution)/shard_map/attend_far/pallas_call | solution.py:343
  83.8 11.3 %attend_near.1 = (bf16[192,1024]{1,0:T(8,128)(2,1)}, f32[192,1024]{1,0:T(8,128)}, f32[3,1024]{1,0:T(4,128)}) custom-call(s32[1,3]{1,0:T(1,128)} %pad_add_fusion.info_ref, f32[15,512]{1,0:T(8,128)} %reshape.102.base_ref, bf16[576,2048]{1,0:T(8,128)(2,1)} %get-tuple-element.104.qkv_ref.qkv_far, bf16[3,2048,128]{2,1,0:T(8,128)(2,1)} %get-tuple-element.105.key_ref.key_far), custom_call_target="tpu_custom_call" | custom-call | flops 1048576 | bytes 65536 | tf_op jit(solution)/shard_map/attend_near/pallas_call | solution.py:361
  95.1 8.1 %all-gather.5.cloned.1.call-done.found_ref = bf16[768,1728]{1,0:T(8,128)(2,1)} async-done(((bf16[96,1728]{1,0:T(8,128)(2,1)}), bf16[768,1728]{1,0:T(8,128)(2,1)}) %all-gather.5.cloned.1.call-update) | async-done | bytes 2654224 | tf_op jit(solution)/shard_map/all_gather | solution.py:997
  103.2 3.4 %unring.3 = (bf16[768,768]{1,0:T(8,128)(2,1)}, bf16[768,768]{1,0:T(8,128)(2,1)}, bf16[192,768]{1,0:T(8,128)(2,1)}) custom-call(bf16[768,1728]{1,0:T(8,128)(2,1)} %all-gather.5.cloned.1.call-done.found_ref), custom_call_target="tpu_custom_call" | custom-call | flops 1048576 | bytes 65536 | tf_op jit(solution)/shard_map/unring/pallas_call | solution.py:142
  112.8 2.1 collective-permute-done.7.normed1
  115.0 21.2 %ffn.1 = (bf16[512,768]{1,0:T(8,128)(2,1)}, bf16[512,768]{1,0:T(8,128)(2,1)S(1)}, bf16[512,768]{1,0:T(8,128)(2,1)}, bf16[512,768]{1,0:T(8,128)(2,1)}, bf16[768,3072]{1,0:T(8,128)(2,1)}, /*index=5*/f32[1,768]{1,0:T(1,128)}) custom-call(bf16[512,768]{1,0:T(8,128)(2,1)S(1)} %get-tuple-element.119.normed0, bf16[512,768]{1,0:T(8,128)(2,1)S(1)} %collective-permute-done.7.normed1, ...), custom_call_target="tpu_custom_call" | custom-call | flops 1048576 | bytes 65536 | tf_op jit(solution)/shard_map/ffn/pallas_call | solution.py:799
  136.4 2.2 collective-permute-done.9.far_ref
  149.4 4.9 %all-to-all-start.2 = ((bf16[8,64,768]{2,1,0:T(8,128)(2,1)}), bf16[8,64,768]{2,1,0:T(8,128)(2,1)S(1)}, u32[]{:S(2)}, u32[]{:S(2)}) async-start(bf16[8,64,768]{2,1,0:T(8,128)(2,1)} %bitcast.40), calls=%async_computation.2 | async-start | bytes 1572864 | tf_op jit(solution)/shard_map/all_to_all | solution.py:983
  154.3 3.7 %collective-permute-done.11.grad1_ref = bf16[192,1024]{1,0:T(8,128)(2,1)} collective-permute-done((bf16[192,1024]{1,0:T(8,128)(2,1)}, bf16[192,1024]{1,0:T(8,128)(2,1)}, u32[]{:S(2)}, u32[]{:S(2)}) %collective-permute-start.11) | collective-permute-done | bytes 393248 | tf_op jit(solution)/shard_map/ppermute | solution.py:980
  157.9 36.5 %attend_back.1 = (f32[15,512]{1,0:T(8,128)}, bf16[576,2048]{1,0:T(8,128)(2,1)}, bf16[512,768]{1,0:T(8,128)(2,1)}, bf16[512,768]{1,0:T(8,128)(2,1)}, bf16[512,768]{1,0:T(8,128)(2,1)}, /*index=5*/bf16[512,768]{1,0:T(8,128)(2,1)}) custom-call(s32[1,3]{1,0:T(1,128)} %pad_add_fusion.info_ref, f32[15,512]{1,0:T(8,128)} %reshape.102.base_ref, ...), custom_call_target="tpu_custom_call" | custom-call | flops 25769803776 | bytes 67108864 | tf_op jit(solution)/shard_map/attend_back/pallas_call | solution.py:546
  197.7 2.5 add_convert_fusion
  201.1 6.4 %qkv_grads.1 = (bf16[768,960]{1,0:T(8,128)(2,1)}, f32[1,768]{1,0:T(1,128)}) custom-call(bf16[576,2048]{1,0:T(8,128)(2,1)} %get-tuple-element.147.grad_ref, bf16[512,768]{1,0:T(8,128)(2,1)} %copy-done.20, bf16[512,768]{1,0:T(8,128)(2,1)} %collective-permute-done.2.slot1_ref, bf16[512,768]{1,0:T(8,128)(2,1)} %collective-permute-done.1.slot2_ref, ...), custom_call_target="tpu_custom_call" | custom-call | flops 1048576 | bytes 65536 | tf_op jit(solution)/shard_map/qkv_grads/pallas_call | solution.py:879
  209.6 2.5 collective-permute-done.16
  213.3 2.5 collective-permute-done.17
  215.8 4.3 %collective-permute-start.18 = (f32[15,128]{1,0:T(8,128)S(1)}, f32[15,128]{1,0:T(8,128)S(1)}, u32[]{:S(2)}, u32[]{:S(2)}) collective-permute-start(f32[15,128]{1,0:T(8,128)S(1)} %fusion.18), channel_id=1, source_target_pairs={{0,16},{4,20},{8,24},{12,28},{16,0},{20,4},{24,8},{28,12},{1,17},{... | collective-permute-start | bytes 23048 | tf_op jit(solution)/shard_map/ppermute | solution.py:988
  222.9 2.3 rows_back.1
  226.1 6.6 %all-to-all-start.3 = ((bf16[8,64,768]{2,1,0:T(8,128)(2,1)}), bf16[8,64,768]{2,1,0:T(8,128)(2,1)S(1)}, u32[]{:S(2)}, u32[]{:S(2)}) async-start(bf16[8,64,768]{2,1,0:T(8,128)(2,1)} %bitcast.36), calls=%async_computation.3 | async-start | bytes 1572864 | tf_op jit(solution)/shard_map/all_to_all | solution.py:983
  235.3 5.5 %collective-permute-done.21.taken_ref = bf16[96,1536]{1,0:T(8,128)(2,1)S(1)} collective-permute-done((bf16[96,1536]{1,0:T(8,128)(2,1)S(1)}, bf16[96,1536]{1,0:T(8,128)(2,1)S(1)}, u32[]{:S(2)}, u32[]{:S(2)}) %collective-permute-start.21) | collective-permute-done | bytes 294944 | tf_op jit(solution)/shard_map/ppermute | solution.py:980
  242.7 2.0 finish.1
  244.7 7.2 %reduce-scatter.5.cloned.1.call-done.last_ref = bf16[96,960]{1,0:T(8,128)(2,1)} async-done(((bf16[768,960]{1,0:T(8,128)(2,1)}), bf16[96,960]{1,0:T(8,128)(2,1)}) %reduce-scatter.5.cloned.1.call-update) | async-done | bytes 184336 | tf_op jit(solution)/shard_map/reduce_scatter | solution.py:1001
  254.1 2.7 %collective-permute-done.19.far_ref = bf16[96,192]{1,0:T(8,128)(2,1)S(1)} collective-permute-done((bf16[96,192]{1,0:T(8,128)(2,1)S(1)}, bf16[96,192]{1,0:T(8,128)(2,1)S(1)}, u32[]{:S(2)}, u32[]{:S(2)}) %collective-permute-start.19) | collective-permute-done | bytes 36896 | tf_op jit(solution)/shard_map/ppermute | solution.py:980
  257.4 1.8 finish_last.1
  (178 shorter events, 46.1 us)
Async XLA Ops:
  7.2 55.0 %all-gather.3.cloned.1.call-start = ((), (), s32[]{:S(2)}) async-start(), calls=%async_computation.6 | async-start | bytes 2654208 | tf_op jit(solution)/shard_map/all_gather | solution.py:997
  12.9 33.2 %all-to-all-start = ((bf16[8,64,768]{2,1,0:T(8,128)(2,1)}), bf16[8,64,768]{2,1,0:T(8,128)(2,1)S(1)}, u32[]{:S(2)}, u32[]{:S(2)}) async-start(bf16[8,64,768]{2,1,0:T(8,128)(2,1)} %bitcast.1), calls=%async_computation | async-start | bytes 1572864 | tf_op jit(solution)/shard_map/all_to_all | solution.py:983
  19.2 83.9 %all-gather.5.cloned.1.call-start = ((), (), s32[]{:S(2)}) async-start(), calls=%async_computation.7 | async-start | bytes 3096576 | tf_op jit(solution)/shard_map/all_gather | solution.py:997
  19.2 6.1 %collective-permute-start = (bf16[96,960]{1,0:T(8,128)(2,1)S(1)}, bf16[96,960]{1,0:T(8,128)(2,1)S(1)}, u32[]{:S(2)}, u32[]{:S(2)}) collective-permute-start(bf16[96,960]{1,0:T(8,128)(2,1)S(1)} %copy-done.25), channel_id=1, source_target_pairs={{0,2},{1,3},{2,0},{3,1},{4,6},{5,7},{6,4},{7,5},{8,10},{9,11},{10,... | collective-permute-start | bytes 552968 | tf_op jit(solution)/shard_map/ppermute | solution.py:980
  47.4 18.3 %collective-permute-start.1 = (bf16[512,768]{1,0:T(8,128)(2,1)S(1)}, bf16[512,768]{1,0:T(8,128)(2,1)}, u32[]{:S(2)}, u32[]{:S(2)}) collective-permute-start(bf16[512,768]{1,0:T(8,128)(2,1)S(1)} %fusion.3.slot0_ref), channel_id=1, source_target_pairs={{0,2},{1,3},{2,0},{3,1},{4,6},{5,7},{6,4},{7,5},{8,10},{9,11},{10,... | collective-permute-start | bytes 2359304 | tf_op jit(solution)/shard_map/ppermute | solution.py:980
  50.7 33.0 %all-to-all-start.1 = ((bf16[8,64,768]{2,1,0:T(8,128)(2,1)}), bf16[8,64,768]{2,1,0:T(8,128)(2,1)S(1)}, u32[]{:S(2)}, u32[]{:S(2)}) async-start(bf16[8,64,768]{2,1,0:T(8,128)(2,1)} %bitcast.39), calls=%async_computation.1 | async-start | bytes 1572864 | tf_op jit(solution)/shard_map/all_to_all | solution.py:983
  56.8 150.7 %reduce-scatter.3.cloned.1.call-start = ((), (), s32[]{:S(2)}) async-start(), calls=%async_computation.8 | async-start | bytes 5308416 | tf_op jit(solution)/shard_map/reduce_scatter | solution.py:1001
  60.3 5.9 %collective-permute-start.2 = (bf16[512,768]{1,0:T(8,128)(2,1)S(1)}, bf16[512,768]{1,0:T(8,128)(2,1)}, u32[]{:S(2)}, u32[]{:S(2)}) collective-permute-start(bf16[512,768]{1,0:T(8,128)(2,1)S(1)} %fusion.3.slot0_ref), channel_id=1, source_target_pairs={{0,1},{1,0},{2,3},{3,2},{4,5},{5,4},{6,7},{7,6},{8,9},{9,8},{10,11... | collective-permute-start | bytes 2359304 | tf_op jit(solution)/shard_map/ppermute | solution.py:980
  65.7 2.5 collective-permute-start.3
  65.7 40.9 %collective-permute-start.4 = (bf16[768,768]{1,0:T(8,128)(2,1)}, bf16[768,768]{1,0:T(8,128)(2,1)}, u32[]{:S(2)}, u32[]{:S(2)}) collective-permute-start(bf16[768,768]{1,0:T(8,128)(2,1)} %get-tuple-element.109.outer0), channel_id=1, source_target_pairs={{0,2},{1,3},{2,0},{3,1},{4,6},{5,7},{6,4},{7,5},{8,10},{9,11},{10,... | collective-permute-start | bytes 3538952 | tf_op jit(solution)/shard_map/ppermute | solution.py:980
  82.5 24.1 %collective-permute-start.5 = (bf16[192,1024]{1,0:T(8,128)(2,1)}, bf16[192,1024]{1,0:T(8,128)(2,1)S(1)}, u32[]{:S(2)}, u32[]{:S(2)}) collective-permute-start(bf16[192,1024]{1,0:T(8,128)(2,1)} %get-tuple-element.113), channel_id=1, source_target_pairs={{0,2},{1,3},{2,0},{3,1},{4,6},{5,7},{6,4},{7,5},{8,10},{9,11},{10,... | collective-permute-start | bytes 1179656 | tf_op jit(solution)/shard_map/ppermute | solution.py:980
  108.6 2.4 collective-permute-start.6
  108.7 4.1 %collective-permute-start.8 = (bf16[512,768]{1,0:T(8,128)(2,1)S(1)}, bf16[512,768]{1,0:T(8,128)(2,1)S(1)}, u32[]{:S(2)}, u32[]{:S(2)}) collective-permute-start(bf16[512,768]{1,0:T(8,128)(2,1)S(1)} %bitcast.31), channel_id=1, source_target_pairs={{0,1},{1,0},{2,3},{3,2},{4,5},{5,4},{6,7},{7,6},{8,9},{9,8},{10,11... | collective-permute-start | bytes 2359304 | tf_op jit(solution)/shard_map/ppermute | solution.py:980
  112.7 2.3 collective-permute-start.7
  136.2 2.4 collective-permute-start.9
  141.9 2.4 collective-permute-start.10
  142.2 6.0 %collective-permute-start.12 = (bf16[512,768]{1,0:T(8,128)(2,1)S(1)}, bf16[512,768]{1,0:T(8,128)(2,1)S(1)}, u32[]{:S(2)}, u32[]{:S(2)}) collective-permute-start(bf16[512,768]{1,0:T(8,128)(2,1)S(1)} %copy-done.31), channel_id=1, source_target_pairs={{0,1},{1,0},{2,3},{3,2},{4,5},{5,4},{6,7},{7,6},{8,9},{9,8},{10,11... | collective-permute-start | bytes 2359304 | tf_op jit(solution)/shard_map/ppermute | solution.py:980
  146.4 11.5 %collective-permute-start.11 = (bf16[192,1024]{1,0:T(8,128)(2,1)}, bf16[192,1024]{1,0:T(8,128)(2,1)}, u32[]{:S(2)}, u32[]{:S(2)}) collective-permute-start(bf16[192,1024]{1,0:T(8,128)(2,1)} %get-tuple-element.129), channel_id=1, source_target_pairs={{0,2},{1,3},{2,0},{3,1},{4,6},{5,7},{6,4},{7,5},{8,10},{9,11},{10,... | collective-permute-start | bytes 1179656 | tf_op jit(solution)/shard_map/ppermute | solution.py:980
  149.4 45.1 %all-to-all-start.2 = ((bf16[8,64,768]{2,1,0:T(8,128)(2,1)}), bf16[8,64,768]{2,1,0:T(8,128)(2,1)S(1)}, u32[]{:S(2)}, u32[]{:S(2)}) async-start(bf16[8,64,768]{2,1,0:T(8,128)(2,1)} %bitcast.40), calls=%async_computation.2 | async-start | bytes 1572864 | tf_op jit(solution)/shard_map/all_to_all | solution.py:983
  154.3 97.7 %reduce-scatter.5.cloned.1.call-start = ((), (), s32[]{:S(2)}) async-start(), calls=%async_computation.9 | async-start | bytes 1769472 | tf_op jit(solution)/shard_map/reduce_scatter | solution.py:1001
  157.9 38.8 %copy-start.33 = (s32[257]{0:T(512)S(1)}, s32[257]{0:T(512)}, u32[]{:S(2)}) copy-start(s32[257]{0:T(512)} %param.27) | copy-start | bytes 3088
  194.5 3.2 %collective-permute-start.13 = (bf16[512,768]{1,0:T(8,128)(2,1)}, bf16[512,768]{1,0:T(8,128)(2,1)}, u32[]{:S(2)}, u32[]{:S(2)}) collective-permute-start(bf16[512,768]{1,0:T(8,128)(2,1)} %get-tuple-element.140), channel_id=1, source_target_pairs={{0,1},{1,0},{2,3},{3,2},{4,5},{5,4},{6,7},{7,6},{8,9},{9,8},{10,11... | collective-permute-start | bytes 2359304 | tf_op jit(solution)/shard_map/ppermute | solution.py:980
  200.1 21.6 %collective-permute-start.15 = (bf16[512,768]{1,0:T(8,128)(2,1)}, bf16[512,768]{1,0:T(8,128)(2,1)}, u32[]{:S(2)}, u32[]{:S(2)}) collective-permute-start(bf16[512,768]{1,0:T(8,128)(2,1)} %add_convert_fusion), channel_id=1, source_target_pairs={{0,2},{1,3},{2,0},{3,1},{4,6},{5,7},{6,4},{7,5},{8,10},{9,11},{10,... | collective-permute-start | bytes 2359304 | tf_op jit(solution)/shard_map/ppermute | solution.py:980
  200.8 20.9 %collective-permute-start.14 = (bf16[512,768]{1,0:T(8,128)(2,1)}, bf16[512,768]{1,0:T(8,128)(2,1)}, u32[]{:S(2)}, u32[]{:S(2)}) collective-permute-start(bf16[512,768]{1,0:T(8,128)(2,1)} %get-tuple-element.143), channel_id=1, source_target_pairs={{0,1},{1,0},{2,3},{3,2},{4,5},{5,4},{6,7},{7,6},{8,9},{9,8},{10,11... | collective-permute-start | bytes 2359304 | tf_op jit(solution)/shard_map/ppermute | solution.py:980
  208.4 3.7 %collective-permute-start.16 = (f32[15,128]{1,0:T(8,128)S(1)}, f32[15,128]{1,0:T(8,128)S(1)}, u32[]{:S(2)}, u32[]{:S(2)}) collective-permute-start(f32[15,128]{1,0:T(8,128)S(1)} %maximum_bitcast_fusion), channel_id=1, source_target_pairs={{0,4},{4,0},{8,12},{12,8},{16,20},{20,16},{24,28},{28,24},{1,5},{5... | collective-permute-start | bytes 23048 | tf_op jit(solution)/shard_map/ppermute | solution.py:988
  212.1 3.7 %collective-permute-start.17 = (f32[15,128]{1,0:T(8,128)S(1)}, f32[15,128]{1,0:T(8,128)S(1)}, u32[]{:S(2)}, u32[]{:S(2)}) collective-permute-start(f32[15,128]{1,0:T(8,128)S(1)} %fusion.17), channel_id=1, source_target_pairs={{0,8},{4,12},{8,0},{12,4},{16,24},{20,28},{24,16},{28,20},{1,9},{5... | collective-permute-start | bytes 23048 | tf_op jit(solution)/shard_map/ppermute | solution.py:988
  215.8 5.9 %collective-permute-start.18 = (f32[15,128]{1,0:T(8,128)S(1)}, f32[15,128]{1,0:T(8,128)S(1)}, u32[]{:S(2)}, u32[]{:S(2)}) collective-permute-start(f32[15,128]{1,0:T(8,128)S(1)} %fusion.18), channel_id=1, source_target_pairs={{0,16},{4,20},{8,24},{12,28},{16,0},{20,4},{24,8},{28,12},{1,17},{... | collective-permute-start | bytes 23048 | tf_op jit(solution)/shard_map/ppermute | solution.py:988
  226.1 33.2 %all-to-all-start.3 = ((bf16[8,64,768]{2,1,0:T(8,128)(2,1)}), bf16[8,64,768]{2,1,0:T(8,128)(2,1)S(1)}, u32[]{:S(2)}, u32[]{:S(2)}) async-start(bf16[8,64,768]{2,1,0:T(8,128)(2,1)} %bitcast.36), calls=%async_computation.3 | async-start | bytes 1572864 | tf_op jit(solution)/shard_map/all_to_all | solution.py:983
  232.7 8.1 %collective-permute-start.21 = (bf16[96,1536]{1,0:T(8,128)(2,1)S(1)}, bf16[96,1536]{1,0:T(8,128)(2,1)S(1)}, u32[]{:S(2)}, u32[]{:S(2)}) collective-permute-start(bf16[96,1536]{1,0:T(8,128)(2,1)S(1)} %pad_maximum_fusion.1), channel_id=1, source_target_pairs={{0,2},{1,3},{2,0},{3,1},{4,6},{5,7},{6,4},{7,5},{8,10},{9,11},{10,... | collective-permute-start | bytes 884744 | tf_op jit(solution)/shard_map/ppermute | solution.py:980
  234.2 1.2 collective-permute-start.20
  240.8 3.8 %collective-permute-start.22 = (f32[15,128]{1,0:T(8,128)S(1)}, f32[15,128]{1,0:T(8,128)S(1)}, u32[]{:S(2)}, u32[]{:S(2)}) collective-permute-start(f32[15,128]{1,0:T(8,128)S(1)} %add.72), channel_id=1, source_target_pairs={{0,2},{1,3},{2,0},{3,1},{4,6},{5,7},{6,4},{7,5},{8,10},{9,11},{10,... | collective-permute-start | bytes 23048 | tf_op jit(solution)/shard_map/ppermute | solution.py:980
  252.7 4.1 %collective-permute-start.19 = (bf16[96,192]{1,0:T(8,128)(2,1)S(1)}, bf16[96,192]{1,0:T(8,128)(2,1)S(1)}, u32[]{:S(2)}, u32[]{:S(2)}) collective-permute-start(bf16[96,192]{1,0:T(8,128)(2,1)S(1)} %slice.70), channel_id=1, source_target_pairs={{0,2},{1,3},{2,0},{3,1},{4,6},{5,7},{6,4},{7,5},{8,10},{9,11},{10,... | collective-permute-start | bytes 110600 | tf_op jit(solution)/shard_map/ppermute | solution.py:980
  (34 other events, 177.5 us)
Sparse Core Ops, SparseCore 0:
  10.1 51.9 all-gather.2
  63.7 39.4 all-gather.4
  136.3 70.1 reduce-scatter.2
  208.6 43.2 reduce-scatter.4
